TPU v7x, 32 devices: a whole 2x2x4 slice. The times are simulated.
32 devices in a mesh: ctx: 4 (over x, core), tp: 4 (over z), grp: 2 (over y).
Axes of the slice: x: 2, y: 2, z: 4, core: 2. Of those that a mesh axis runs over, the one named last changes fastest.
Arguments:
- pre_act: bfloat16 [2048, 5120], P(('ctx', 'grp')), may hold values from -6 to 6
- w_out: bfloat16 [5120, 8192], P(None, 'tp'), may hold values from -0.078125 to 0.078125
- b_out: bfloat16 [8192], P('tp'), may hold values from -3 to 3
- row_slot: int32 [2048], P(('ctx', 'grp')), may hold values from 0 to 511, as said below
- ctx_slot: int32 [4096], P(('ctx', 'grp')), may hold values from -1 to 511, as said below
- text_rows: bfloat16 [4096, 8192], P(('ctx', 'grp'), 'tp'), may hold values from -6 to 6
- cotangent: bfloat16 [4096, 8192], P(('ctx', 'grp'), 'tp'), may hold values from -6 to 6
Outputs:
- embeds: bfloat16 [4096, 8192], P(('ctx', 'grp'), 'tp')
- grad_pre: bfloat16 [2048, 5120], P(('ctx', 'grp'))
Inputs may be any that keep to these rules, and one draw needn't show every extreme that they name: `row_slot`: within each aligned block of 256 rows (one encoder device) the values are distinct; value // 64 is the context shard (index along ctx+grp) that receives the row and value % 64 its slot there; in every block some shard receives exactly 64 rows. `ctx_slot`: within each aligned block of 512 positions (one context shard) the values other than -1 are distinct; a value s names the row that encoder device s // 64 (index along ctx+grp) sent in slot s % 64 to this shard; every image token is placed at exactly one position and every used slot names a sent row.
All inputs are finite; a program needn't handle non-finite values.
Results may differ from a plain program's by a relative error of at most 0.018.
Values may be sent and summed in bfloat16 or wider, within the bound.
No kernel may reach another device: no remote copies, remote signals or barrier semaphores. Data moves between devices by JAX's collectives and lax.ppermute only.
A program may use at most 64 MiB of HBM per device.

v0:
```python
import jax
import jax.numpy as jnp
from jax import lax
from jax.sharding import PartitionSpec as P


def gelu_value(values):
    return 0.5 * values * (1.0 + lax.erf(values * 0.7071067811865476))


def gelu_slope(values):
    return (
        0.5 * (1.0 + lax.erf(values * 0.7071067811865476))
        + values * jnp.exp(-0.5 * values * values) * 0.3989422804014327
    )


def shards(pre_act, w_out, b_out, row_slot, ctx_slot, text_rows, cotangent):
    ctx_count = lax.axis_size("ctx")
    grp_count = lax.axis_size("grp")
    groups = ctx_count * grp_count
    row_count = pre_act.shape[0]
    slot_count = 2 * row_count
    capacity = slot_count // groups
    width = w_out.shape[1]
    pre_float = pre_act.astype(jnp.float32)
    hidden = gelu_value(pre_float).astype(jnp.bfloat16)
    merged = (
        jnp.dot(hidden, w_out, preferred_element_type=jnp.float32) + b_out.astype(jnp.float32)
    ).astype(jnp.bfloat16)
    outgoing = jnp.zeros((slot_count, width), jnp.bfloat16).at[row_slot].set(merged)
    placed = ctx_slot >= 0
    returning = (
        jnp.zeros((slot_count, width), jnp.bfloat16)
        .at[jnp.where(placed, ctx_slot, slot_count)]
        .set(cotangent, mode="drop")
    )
    arrived = lax.all_to_all(
        outgoing.reshape(groups, capacity, width),
        ("ctx", "grp"),
        split_axis=0,
        concat_axis=0,
        tiled=True,
    )
    returned = lax.all_to_all(
        returning.reshape(groups, capacity, width),
        ("ctx", "grp"),
        split_axis=0,
        concat_axis=0,
        tiled=True,
    )
    arrived = arrived.reshape(slot_count, width)
    embeds = jnp.where(placed[:, None], arrived[jnp.where(placed, ctx_slot, 0)], text_rows)
    grad_rows = returned.reshape(slot_count, width)[row_slot]
    partial_value = lax.dot_general(
        grad_rows, w_out, (((1,), (1,)), ((), ())), preferred_element_type=jnp.float32
    )
    term = partial_value.astype(jnp.bfloat16)
    summed = lax.psum(term, "tp").astype(jnp.float32)
    grad_pre = (summed * gelu_slope(pre_float)).astype(jnp.bfloat16)
    return (embeds, grad_pre)


def solution(mesh):
    in_specs = (
        P(("ctx", "grp"), None),
        P(None, "tp"),
        P("tp"),
        P(("ctx", "grp")),
        P(("ctx", "grp")),
        P(("ctx", "grp"), "tp"),
        P(("ctx", "grp"), "tp"),
    )
    out_specs = (P(("ctx", "grp"), "tp"), P(("ctx", "grp"), None))
    return jax.shard_map(shards, mesh=mesh, in_specs=in_specs, out_specs=out_specs, check_vma=False)
```

profile of v0, /device:TPU:0, one launch (start us, length us, event | category | flops | bytes accessed | tf_op | source)
XLA Modules:
  0.0 174.8 jit_solution(8031651821931673217)
XLA Ops:
  7.2 0.7 compare_select_fusion
  7.9 6.1 %scatter_custom_fusion.1 = bf16[512,2048]{1,0:T(8,128)(2,1)} fusion(s32[512]{0:T(512)S(1)} %get-tuple-element.2, bf16[512,2048]{1,0:T(8,128)(2,1)} %param.13, bf16[]{:T(256)} %constant.9.clone.1), kind=kCustom, calls=%fused_computation.23 | custom fusion | bytes 2097664 | tf_op jit(solution)/shard_map/scatter | solution.py:36
  14.0 0.0 copy-start.3
  14.0 0.0 copy-start.4
  14.0 5.3 %all-to-all-start.1 = ((bf16[8,64,2048]{2,1,0:T(8,128)(2,1)}), bf16[8,64,2048]{2,1,0:T(8,128)(2,1)S(1)}, u32[]{:S(2)}, u32[]{:S(2)}) async-start(bf16[8,64,2048]{2,1,0:T(8,128)(2,1)} %bitcast.10), calls=%async_computation.1 | async-start | bytes 4194304 | tf_op jit(solution)/shard_map/all_to_all | solution.py:45
  19.3 0.0 all-reduce.2.cloned.1.call-start
  19.3 0.0 copy-done.3
  19.4 0.0 copy-done.4
  19.4 25.7 %all-to-all-done.1 = bf16[8,64,2048]{2,1,0:T(8,128)(2,1)S(1)} async-done(((bf16[8,64,2048]{2,1,0:T(8,128)(2,1)}), bf16[8,64,2048]{2,1,0:T(8,128)(2,1)S(1)}, u32[]{:S(2)}, u32[]{:S(2)}) %all-to-all-start.1) | async-done | bytes 2097184 | tf_op jit(solution)/shard_map/all_to_all | solution.py:45
  45.1 1.4 gather_fusion.1
  46.4 11.7 %convolution_convert_fusion = bf16[256,5120]{1,0:T(8,128)(2,1)} fusion(bf16[256,2048]{1,0:T(8,128)(2,1)S(1)} %gather_fusion.1, bf16[5120,2048]{1,0:T(8,128)(2,1)} %param.8), kind=kOutput, calls=%fused_computation.9 | convolution fusion | flops 5370019840 | bytes 24641536 | tf_op jit(solution)/shard_map/dot_general | solution.py:55
  58.1 0.0 copy-start
  58.1 0.0 all-reduce.2.cloned.1.call-update
  58.1 1.7 copy-done
  59.9 11.1 %fusion.11 = bf16[256,2048]{1,0:T(8,128)(2,1)} fusion(bf16[5120,2048]{1,0:T(8,128)(2,1)} %param.8, bf16[256,5120]{1,0:T(8,128)(2,1)S(1)} %copy-done, f32[2048]{0:T(1024)S(1)} %convert_element_type.23), kind=kOutput, calls=%fused_computation.21 | convolution fusion | flops 5377622016 | bytes 24649728 | tf_op jit(solution)/shard_map/dot_general | solution.py:29
  70.9 4.4 %scatter_custom_fusion = bf16[512,2048]{1,0:T(8,128)(2,1)} fusion(s32[256]{0:T(256)S(1)} %compare_select_fusion.2, bf16[256,2048]{1,0:T(8,128)(2,1)} %fusion.11, bf16[]{:T(256)} %constant.9.clone.1), kind=kCustom, calls=%fused_computation.25 | custom fusion | bytes 2097664 | tf_op jit(solution)/shard_map/scatter | solution.py:31
  75.4 0.0 copy-start.2
  75.4 3.7 %all-to-all-start = ((bf16[8,64,2048]{2,1,0:T(8,128)(2,1)}), bf16[8,64,2048]{2,1,0:T(8,128)(2,1)S(1)}, u32[]{:S(2)}, u32[]{:S(2)}) async-start(bf16[8,64,2048]{2,1,0:T(8,128)(2,1)} %bitcast.9), calls=%async_computation | async-start | bytes 4194304 | tf_op jit(solution)/shard_map/all_to_all | solution.py:38
  79.1 0.0 copy-done.2
  79.1 25.7 %all-to-all-done = bf16[8,64,2048]{2,1,0:T(8,128)(2,1)S(1)} async-done(((bf16[8,64,2048]{2,1,0:T(8,128)(2,1)}), bf16[8,64,2048]{2,1,0:T(8,128)(2,1)S(1)}, u32[]{:S(2)}, u32[]{:S(2)}) %all-to-all-start) | async-done | bytes 2097184 | tf_op jit(solution)/shard_map/all_to_all | solution.py:38
  104.8 3.3 %gather_fusion = bf16[512,2048]{1,0:T(8,128)(2,1)} fusion(bf16[512,2048]{1,0:T(8,128)(2,1)S(1)} %bitcast.7, s32[1024]{0:T(1024)S(1)} %pad_clamp_fusion.1), kind=kCustom, calls=%fused_computation | custom fusion | bytes 4196352 | tf_op jit(solution)/shard_map/gather | solution.py:53
  108.1 0.0 copy-start.1
  108.1 4.0 %broadcast_select_fusion = bf16[512,2048]{1,0:T(8,128)(2,1)} fusion(bf16[512,2048]{1,0:T(8,128)(2,1)} %gather_fusion, bf16[512,2048]{1,0:T(8,128)(2,1)} %param.12, pred[512]{0:T(512)(128)(4,1)S(1)} %broadcast_compare_fusion), kind=kLoop, calls=%fused_computation.22 | loop fusion | flops 1048576 | bytes 6291968 | tf_op jit(solution)/shard_map/jit(_where)/select_n | solution.py:53
  112.1 50.6 %all-reduce.2.cloned.1.call-done = bf16[256,5120]{1,0:T(8,128)(2,1)} async-done(((bf16[256,5120]{1,0:T(8,128)(2,1)}), bf16[256,5120]{1,0:T(8,128)(2,1)}) %all-reduce.2.cloned.1.call-update) | async-done | bytes 2621456 | tf_op jit(solution)/shard_map/psum | solution.py:59
  162.7 0.0 copy-done.1
  162.7 5.2 %fusion.8 = bf16[256,5120]{1,0:T(8,128)(2,1)} fusion(bf16[256,5120]{1,0:T(8,128)(2,1)S(1)} %copy-done.1, bf16[256,5120]{1,0:T(8,128)(2,1)} %all-reduce.2.cloned.1.call-done), kind=kLoop, calls=%fused_computation.18 | loop fusion | flops 15728640 | bytes 7864320 | tf_op jit(solution)/shard_map/convert_element_type | solution.py:60
  (5 shorter events, 0.0 us)
Async XLA Ops:
  14.0 5.4 %copy-start.3 = (bf16[2048]{0:T(1024)(128)(2,1)S(1)}, bf16[2048]{0:T(1024)(128)(2,1)}, u32[]{:S(2)}) copy-start(bf16[2048]{0:T(1024)(128)(2,1)} %param.9) | copy-start | bytes 12292
  14.0 5.4 %copy-start.4 = (s32[256]{0:T(256)S(1)}, s32[256]{0:T(256)}, u32[]{:S(2)}) copy-start(s32[256]{0:T(256)} %param.10) | copy-start | bytes 3076
  14.0 31.1 %all-to-all-start.1 = ((bf16[8,64,2048]{2,1,0:T(8,128)(2,1)}), bf16[8,64,2048]{2,1,0:T(8,128)(2,1)S(1)}, u32[]{:S(2)}, u32[]{:S(2)}) async-start(bf16[8,64,2048]{2,1,0:T(8,128)(2,1)} %bitcast.10), calls=%async_computation.1 | async-start | bytes 4194304 | tf_op jit(solution)/shard_map/all_to_all | solution.py:45
  19.3 143.4 %all-reduce.2.cloned.1.call-start = ((), (), s32[]{:S(2)}) async-start(), calls=%async_computation.2 | async-start | bytes 5242880 | tf_op jit(solution)/shard_map/psum | solution.py:59
  58.1 1.7 copy-start
  75.4 3.8 %copy-start.2 = (s32[512]{0:T(512)S(1)}, s32[512]{0:T(512)}, u32[]{:S(2)}) copy-start(s32[512]{0:T(512)} %param.11) | copy-start | bytes 6148
  75.4 29.5 %all-to-all-start = ((bf16[8,64,2048]{2,1,0:T(8,128)(2,1)}), bf16[8,64,2048]{2,1,0:T(8,128)(2,1)S(1)}, u32[]{:S(2)}, u32[]{:S(2)}) async-start(bf16[8,64,2048]{2,1,0:T(8,128)(2,1)} %bitcast.9), calls=%async_computation | async-start | bytes 4194304 | tf_op jit(solution)/shard_map/all_to_all | solution.py:38
  108.1 54.6 %copy-start.1 = (bf16[256,5120]{1,0:T(8,128)(2,1)S(1)}, bf16[256,5120]{1,0:T(8,128)(2,1)}, u32[]{:S(2)}) copy-start(bf16[256,5120]{1,0:T(8,128)(2,1)} %param.7) | copy-start | bytes 7864324
Sparse Core Ops, SparseCore 0:
  58.3 104.3 all-reduce.1
where the time goes:
time: 175 us
  waiting for transfers between devices  102 us (58%)
  matrix products  22.8 us (13%)
  local copies, waits for them, and re-layouts  16.9 us (10%)
  between operations  14.1 us (8%)
  other arithmetic  9.93 us (6%)
  starting transfers between devices  9.07 us (5%)
    psum x1, waiting for transfers between devices, shards(): summed = lax.psum(term, 'tp').astype(jnp.float32)  50.6 us
    all_to_all x1, waiting for transfers between devices, shards(): lax.all_to_all(returning.reshape(groups, capacity, width), ('ctx', 'grp')...  25.7 us
    all_to_all x1, waiting for transfers between devices, shards(): lax.all_to_all(outgoing.reshape(groups, capacity, width), ('ctx', 'grp'),...  25.7 us
    dot_general x1, matrix products, shards(): lax.dot_general(grad_rows, w_out, (((1,), (1,)), ((), ())), preferred_ele...  11.7 us
    dot_general x1, matrix products, shards(): jnp.dot(hidden, w_out, preferred_element_type=jnp.float32)  11.1 us
    scatter x1, local copies, waits for them, and re-layouts, shards(): returning = jnp.zeros((slot_count, width), jnp.bfloat16).at[jnp.where(pla...  6.13 us
    all_to_all x1, starting transfers between devices, shards(): lax.all_to_all(returning.reshape(groups, capacity, width), ('ctx', 'grp')...  5.3 us
    convert_element_type x1, other arithmetic, shards(): grad_pre = (summed * gelu_slope(pre_float)).astype(jnp.bfloat16)  5.24 us
  transfers between devices with their start and end apart: 3, of which 3 were waited for; matrix products, arithmetic and copies ran while one was open for 13% of the time, Pallas kernels for 0%

commit v1 on v0

v1 whole, which is shorter than its diff:
```python
import functools
import math

import jax
import jax.numpy as jnp
from jax import lax
from jax.experimental import pallas as pl
from jax.experimental.pallas import tpu as pltpu
from jax.sharding import PartitionSpec as P

BF = jnp.bfloat16
F32 = jnp.float32
I32 = jnp.int32
GROUP_AXES = ("ctx", "grp")
VMEM = pl.BlockSpec(memory_space=pltpu.VMEM)
SMEM = pl.BlockSpec(memory_space=pltpu.SMEM)
ANY = pl.BlockSpec(memory_space=pl.ANY)


def gelu_value(values):
    return 0.5 * values * (1.0 + lax.erf(values * 0.7071067811865476))


def gelu_slope(values):
    return (
        0.5 * (1.0 + lax.erf(values * 0.7071067811865476))
        + values * jnp.exp(-0.5 * values * values) * 0.3989422804014327
    )


def plain(pre_act, w_out, b_out, row_slot, ctx_slot, text_rows, cotangent):
    groups = lax.axis_size("ctx") * lax.axis_size("grp")
    slot_count = 2 * pre_act.shape[0]
    capacity = slot_count // groups
    width = w_out.shape[1]
    pre_float = pre_act.astype(F32)
    hidden = gelu_value(pre_float).astype(BF)
    merged = (jnp.dot(hidden, w_out, preferred_element_type=F32) + b_out.astype(F32)).astype(BF)
    outgoing = jnp.zeros((slot_count, width), BF).at[row_slot].set(merged)
    placed = ctx_slot >= 0
    returning = (
        jnp.zeros((slot_count, width), BF)
        .at[jnp.where(placed, ctx_slot, slot_count)]
        .set(cotangent, mode="drop")
    )

    def exchange(sent):
        blocks = sent.reshape(groups, capacity, width)
        return lax.all_to_all(
            blocks, GROUP_AXES, split_axis=0, concat_axis=0, tiled=True
        ).reshape(slot_count, width)

    arrived = exchange(outgoing)
    embeds = jnp.where(placed[:, None], arrived[jnp.where(placed, ctx_slot, 0)], text_rows)
    grad_rows = exchange(returning)[row_slot]
    partial_value = lax.dot_general(
        grad_rows, w_out, (((1,), (1,)), ((), ())), preferred_element_type=F32
    )
    summed = lax.psum(partial_value.astype(BF), "tp").astype(F32)
    grad_pre = (summed * gelu_slope(pre_float)).astype(BF)
    return embeds, grad_pre


def iota(shape, axis):
    return lax.broadcasted_iota(I32, shape, axis)


def as_column(row):
    n = row.shape[1]
    return jnp.sum(jnp.where(iota((n, n), 0) == iota((n, n), 1), row, 0), axis=1, keepdims=True)


def rank_in_block(row, shift):
    column = as_column(row)
    smaller = ((column >> shift) == (row >> shift)) & (column < row) & (column >= 0)
    return jnp.sum(smaller.astype(I32), axis=0, keepdims=True)


def arrival(row, shift, early):
    n = row.shape[1]
    rank = rank_in_block(row, shift)
    is_early = (rank < early).astype(I32)
    before = jnp.sum(
        jnp.where(iota((n, n), 0) < iota((n, n), 1), as_column(is_early), 0), axis=0, keepdims=True
    )
    index = iota((1, n), 1)
    place = jnp.where(is_early > 0, before, jnp.sum(is_early) + index - before)
    return rank, is_early, place


def call(kernel, name, out_shape, in_specs, out_specs, args, deps=(), limit=8, pins=None, **more):
    n = len(args)
    pins = pins or {}
    args = [
        pltpu.with_memory_space_constraint(arg, pins[i]) if i in pins else arg
        for i, arg in enumerate(args)
    ]
    deps = [
        pltpu.with_memory_space_constraint(dep, pltpu.HBM) if dep.size > 1 << 20 else dep
        for dep in deps
    ]

    def body(*refs):
        kernel(*refs[:n], *refs[n + len(deps) :])

    return pl.pallas_call(
        body,
        out_shape=out_shape,
        in_specs=list(in_specs) + [ANY] * len(deps),
        out_specs=out_specs,
        cost_estimate=pl.CostEstimate(flops=1000, bytes_accessed=1000, transcendentals=0),
        compiler_params=pltpu.CompilerParams(vmem_limit_bytes=limit << 20),
        name=name,
        **more,
    )(*args, *deps)


def full(shape):
    return pl.BlockSpec(shape, lambda *_: (0,) * len(shape))


def columns(rows, block):
    return pl.BlockSpec((rows, block), lambda i: (0, i))


def as_hot(mask):
    return jnp.where(mask, 1.0, 0.0).astype(BF)


def pack_context(me, slots, cotangent, low, high, shift, groups, load=None, deps=()):
    count = high - low
    tokens, width = cotangent.shape
    block = 512
    spans = [slice(start, start + block) for start in range(0, width, block)]

    def kernel(me_ref, slot_ref, rows_ref, *refs):
        here_ref, sems = refs[-2:]
        slots_copy = pltpu.make_async_copy(slot_ref, here_ref, sems.at[0])
        slots_copy.start()
        if load is None:
            outs, held_ref = refs[:groups], refs[groups]
            copy = pltpu.make_async_copy(rows_ref, held_ref, sems.at[1])
        else:
            outs, held_ref = refs[1 : 1 + groups], rows_ref
            copy = pltpu.make_async_copy(refs[0].at[load[1]], refs[1 + groups], sems.at[1])
        copy.start()
        slots_copy.wait()
        row = here_ref[...]
        rank = rank_in_block(row, shift)
        used = (row >= 0) & (rank >= low) & (rank < high)
        wire = jnp.where(used, ((row >> shift) ^ me_ref[0]) * count + rank - low, -1)
        hot = as_hot(iota((groups * count, tokens), 0) == wire)
        if load is None:
            copy.wait()
        for span in spans:
            packed = jnp.dot(hot, held_ref[:, span], preferred_element_type=F32).astype(BF)
            for k, out in enumerate(outs):
                out[:, span] = packed[k * count : (k + 1) * count]
        if load is not None:
            copy.wait()

    if load is None:
        more = ()
        held = pltpu.VMEM((tokens, width), BF)
    else:
        more = (load[0],)
        held = pltpu.VMEM((load[1].stop - load[1].start, load[0].shape[1]), BF)
    pins = {1: pltpu.HBM, 2: pltpu.HBM}
    if load is not None:
        pins = {1: pltpu.HBM, 2: pltpu.VMEM, 3: pltpu.HBM}
    *outs, held = call(
        kernel,
        "pack_context",
        [jax.ShapeDtypeStruct((count, width), BF)] * groups + [held],
        [SMEM, ANY, ANY if load is None else VMEM] + [ANY] * len(more),
        [VMEM] * (groups + 1),
        (me, slots, cotangent, *more),
        deps,
        pins=pins,
        scratch_shapes=[pltpu.VMEM((1, tokens), I32), pltpu.SemaphoreType.DMA((2,))],
    )
    return outs, held


def route(me, row_slots, ctx_slots, early, shift, groups, deps=()):
    n = row_slots.shape[1]
    tokens = ctx_slots.shape[1]
    capacity = 1 << shift
    late = capacity - early
    half = n * early // capacity
    wires = groups * capacity

    def kernel(me_ref, row_ref, ctx_ref, early_ref, all_ref, back_ref, merged_ref, place_ref):
        row = row_ref[...]
        rank, is_early, place = arrival(row, shift, early)
        piece = (row >> shift) ^ me_ref[0]
        wire = jnp.where(
            is_early > 0, piece * early + rank, groups * early + piece * late + rank - early
        )
        order = iota((n, n), 0) == place
        source = jnp.sum(jnp.where(order, wire, 0), axis=1, keepdims=True)
        early_ref[...] = as_hot(iota((half, groups * early), 1) == source[:half])
        all_ref[...] = as_hot(iota((n, wires), 1) == source)
        back_ref[...] = as_hot(iota((n, n), 1) == as_column(place))
        slot = (piece << shift) + (row & (capacity - 1))
        merged_ref[...] = as_hot(iota((wires, n), 0) == slot)
        ctx = ctx_ref[...]
        slot = (((ctx >> shift) ^ me_ref[0]) << shift) + (ctx & (capacity - 1))
        slot = as_column(jnp.where(ctx >= 0, slot, -1))
        place_ref[...] = as_hot(iota((tokens, wires), 1) == slot)

    shapes = [(half, groups * early), (n, wires), (n, n), (wires, n), (tokens, wires)]
    return call(
        kernel,
        "route",
        [jax.ShapeDtypeStruct(shape, BF) for shape in shapes],
        [SMEM, VMEM, VMEM],
        [VMEM] * len(shapes),
        (me, row_slots, ctx_slots),
        deps,
    )


def dot_columns(hot, rows_ref, out_ref, block=512):
    for start in range(0, out_ref.shape[1], block):
        span = slice(start, start + block)
        out_ref[:, span] = jnp.dot(
            hot, rows_ref[:, span], preferred_element_type=F32
        ).astype(BF)


def take_rows(hot, pieces, deps=()):
    width = pieces[0].shape[1]

    def kernel(hot_ref, *refs):
        ins, out_ref, wire_ref = refs[:-2], refs[-2], refs[-1]
        start = 0
        for piece in ins:
            wire_ref[start : start + piece.shape[0]] = piece[...]
            start += piece.shape[0]
        dot_columns(hot_ref[...], wire_ref, out_ref)

    return call(
        kernel,
        "take_rows",
        jax.ShapeDtypeStruct((hot.shape[0], width), BF),
        [VMEM] * (1 + len(pieces)),
        VMEM,
        (hot, *pieces),
        deps,
        scratch_shapes=[pltpu.VMEM((hot.shape[1], width), BF)],
    )


def back_product(rows, w_rows, span, first, last, height, deps=()):
    count = span.stop - span.start
    width = last - first

    def kernel(rows_ref, w_ref, out_ref):
        product = lax.dot_general(
            rows_ref[span],
            w_ref[first:last],
            (((1,), (1,)), ((), ())),
            preferred_element_type=F32,
        ).astype(BF)
        for i in range(count // height):
            out_ref[:, i * width : (i + 1) * width] = product[i * height : (i + 1) * height]

    return call(
        kernel,
        "back_product",
        jax.ShapeDtypeStruct((height, width * count // height), BF),
        [VMEM, VMEM],
        VMEM,
        (rows, w_rows),
        deps,
        pins={1: pltpu.VMEM},
    )


def forward_product(pre_act, w_rows, before, first, load=None, deps=()):
    rows = pre_act.shape[0]
    depth, width = w_rows.shape
    block = 512

    def kernel(pre_ref, w_ref, before_ref, *refs):
        if load is not None:
            copy = pltpu.make_async_copy(refs[0].at[load[1]], refs[3], refs[-1])
            copy.start()
            refs = refs[1:]
        out_ref, slope_ref = refs[:2]
        total = refs[-2]
        for start in range(0, depth, block):
            values = pre_ref[:, first + start : first + start + block].astype(F32)
            share = 0.5 * (1.0 + lax.erf(values * 0.7071067811865476))
            slope = share + values * jnp.exp(-0.5 * values * values) * 0.3989422804014327
            span = slice(start, start + block)
            slope_ref[:, span] = slope.astype(slope_ref.dtype)
            term = jnp.dot(
                (values * share).astype(BF), w_ref[span], preferred_element_type=F32
            )
            so_far = before_ref[...].astype(F32) if start == 0 else total[...]
            if start + block < depth:
                total[...] = so_far + term
            else:
                out_ref[...] = (so_far + term).astype(out_ref.dtype)
        if load is not None:
            copy.wait()

    more, outs, pins = (), [], {1: pltpu.VMEM}
    if load is not None:
        more, pins = (load[0],), {1: pltpu.VMEM, 3: pltpu.HBM}
        outs = [pltpu.VMEM((load[1].stop - load[1].start, load[0].shape[1]), BF)]
    return call(
        kernel,
        "forward_product",
        [
            jax.ShapeDtypeStruct((rows, width), BF if load is None else F32),
            jax.ShapeDtypeStruct((rows, depth), BF),
            *outs,
        ],
        [VMEM, VMEM, VMEM] + [ANY] * len(more),
        [VMEM] * (2 + len(outs)),
        (pre_act, w_rows, before, *more),
        deps,
        pins=pins,
        scratch_shapes=[pltpu.VMEM((rows, width), F32), pltpu.SemaphoreType.DMA],
    )


def pack_merged(hot, merged, index, capacity, deps=()):
    def kernel(hot_ref, rows_ref, out_ref):
        dot_columns(hot_ref[index * capacity : (index + 1) * capacity], rows_ref, out_ref)

    return call(
        kernel,
        "pack_merged",
        jax.ShapeDtypeStruct((capacity, merged.shape[1]), BF),
        [VMEM, VMEM],
        VMEM,
        (hot, merged),
        deps,
    )


def place_rows(slots, hot, pieces, text, deps=()):
    tokens, width = text.shape
    block = 512
    total = hot.shape[1]
    spans = [slice(start, start + block) for start in range(0, width, block)]

    def kernel(slot_ref, hot_ref, text_ref, *refs):
        ins, out_ref, wire_ref, done_ref, sems = refs[:-4], *refs[-4:]
        used = as_column((slot_ref[...] >= 0).astype(I32))
        start = 0
        for piece in ins:
            wire_ref[start : start + piece.shape[0]] = piece[...]
            start += piece.shape[0]
        copies = []
        for i, span in enumerate(spans):
            rows = jnp.dot(hot_ref[...], wire_ref[:, span], preferred_element_type=F32)
            done_ref[:, span] = jnp.where(
                used > 0, rows, text_ref[:, span].astype(F32)
            ).astype(BF)
            copies.append(
                pltpu.make_async_copy(done_ref.at[:, span], out_ref.at[:, span], sems.at[i])
            )
            copies[-1].start()
        for copy in copies:
            copy.wait()

    return call(
        kernel,
        "place_rows",
        pltpu.HBM((tokens, width), BF),
        [VMEM] * (3 + len(pieces)),
        ANY,
        (slots, hot, text, *pieces),
        deps,
        limit=12,
        scratch_shapes=[
            pltpu.VMEM((total, width), BF),
            pltpu.VMEM((tokens, width), BF),
            pltpu.SemaphoreType.DMA((len(spans),)),
        ],
    )


def add_term(own, other, deps=()):
    def kernel(a_ref, b_ref, out_ref):
        out_ref[...] = (a_ref[...].astype(F32) + b_ref[...].astype(F32)).astype(BF)

    shape = jax.ShapeDtypeStruct(own.shape, BF)
    return call(
        kernel, "add_term", shape, [VMEM, VMEM], VMEM, (own, other), deps, limit=4
    )


def add_and_choose(me, own, other, term, deps=()):
    def kernel(me_ref, a_ref, b_ref, term_ref, sum_ref, next_ref):
        total = (a_ref[...].astype(F32) + b_ref[...].astype(F32)).astype(BF)
        sum_ref[...] = total
        next_ref[...] = jnp.where(
            me_ref[1] > 0, total.astype(F32), term_ref[...].astype(F32)
        ).astype(BF)

    shape = jax.ShapeDtypeStruct(own.shape, BF)
    return call(
        kernel,
        "add_and_choose",
        (shape, shape),
        [SMEM, VMEM, VMEM, VMEM],
        (VMEM, VMEM),
        (me, own, other, term),
        deps,
        limit=4,
    )


def finish(me, hot, sums, slope, depth, so_far, first, width, deps=()):
    n = hot.shape[0]
    flat = [array for pair in sums for array in pair]
    slope, start_at = slope

    def kernel(me_ref, hot_ref, slope_ref, *refs):
        ins = refs[: len(flat)]
        out_ref, rows_ref, done_ref, sem = refs[-4:]
        start = 0
        for held, came in zip(ins[::2], ins[1::2]):
            block = jnp.where(
                me_ref[1] > 0, held[...].astype(F32), came[...].astype(F32)
            ).astype(BF)
            height = held.shape[0]
            for i in range(held.shape[1] // width):
                rows_ref[start : start + height] = block[:, i * width : (i + 1) * width]
                start += height
        total = jnp.dot(hot_ref[...], rows_ref[...], preferred_element_type=F32)
        slopes = slope_ref[:, first - start_at : first - start_at + width]
        done_ref[...] = (total * slopes.astype(F32)).astype(BF)
        copy = pltpu.make_async_copy(done_ref, out_ref.at[:, first : first + width], sem)
        copy.start()
        copy.wait()

    args = (me, hot, slope, *flat)
    in_specs = [SMEM] + [VMEM] * (2 + len(flat))
    aliases, pins = {}, {}
    if so_far is not None:
        aliases = {len(args): 0}
        pins = {len(args): pltpu.HBM}
        args += (so_far,)
        in_specs.append(ANY)
    return call(
        kernel,
        "finish",
        pltpu.HBM((n, depth), BF),
        in_specs,
        ANY,
        args,
        deps,
        pins=pins,
        scratch_shapes=[
            pltpu.VMEM((n, width), BF),
            pltpu.VMEM((n, width), BF),
            pltpu.SemaphoreType.DMA,
        ],
        input_output_aliases=aliases,
    )


def pipelined(pre_act, w_out, b_out, row_slot, ctx_slot, text_rows, cotangent):
    ctx_size, grp_size, tp_size = (lax.axis_size(name) for name in ("ctx", "grp", "tp"))
    groups = ctx_size * grp_size
    rows, depth = pre_act.shape
    width = w_out.shape[1]
    tokens = ctx_slot.shape[0]
    capacity = 2 * rows // groups
    shift = capacity.bit_length() - 1
    tp_index = lax.axis_index("tp")
    me = jnp.stack(
        [
            lax.axis_index("ctx") * grp_size + lax.axis_index("grp"),
            ((tp_index == 1) | (tp_index == 2)).astype(I32),
        ]
    )
    row_slots = row_slot.reshape(1, rows)
    ctx_slots = ctx_slot.reshape(1, tokens)

    def exchange(k, piece):
        return lax.ppermute(piece, GROUP_AXES, [(i, i ^ k) for i in range(groups)])

    def exchange_all(pieces):
        return [pieces[0]] + [exchange(k, pieces[k]) for k in range(1, groups)]

    early = capacity // 2
    early_rows = rows // 2
    first_part, second_part, every = (
        slice(0, early_rows), slice(early_rows, rows), slice(0, rows)
    )
    wide, narrow = depth // 5, depth // 10
    cut = 3 * wide
    blocks = [(first_part, c, c + wide) for c in range(0, cut, wide)]
    blocks += [(second_part, c, c + wide) for c in range(0, cut, wide)]
    blocks += [(every, c, c + narrow) for c in range(cut, depth, narrow)]
    chunks = len(blocks)

    bias = b_out.reshape(1, width)
    first_out, held = pack_context(me, ctx_slots, cotangent, 0, early, shift, groups)
    first_in = exchange_all(first_out)
    second_out, w_low = pack_context(
        me,
        ctx_slots,
        held,
        early,
        capacity,
        shift,
        groups,
        (w_out, slice(0, cut)),
        (first_out[1], bias),
    )
    second_in = exchange_all(second_out)
    hot_early, hot_all, hot_back, hot_merged, hot_place = route(
        me, row_slots, ctx_slots, early, shift, groups, (second_out[1],)
    )

    def product(j, deps=()):
        span, first, last = blocks[j]
        w_rows, start = (w_low, 0) if last <= cut else (w_high, cut)
        return back_product(grads, w_rows, span, first - start, last - start, early_rows, deps)

    grads = take_rows(hot_early, first_in)
    terms = {0: product(0)}
    terms[1] = product(1, (terms[0],))

    outer_pairs = [(0, 1), (1, 0), (2, 3), (3, 2)]
    inner_pairs = [
        (c * tp_size + t, c * tp_size + 3 - t if t in (1, 2) else (c ^ 1) * tp_size + t)
        for c in range(ctx_size)
        for t in range(tp_size)
    ]
    from_pair, from_far, halves, totals, send = {}, {}, {}, {}, {}
    outgoing, arrived = {}, {}

    def to_pair(j, value):
        from_pair[j] = lax.ppermute(value, "tp", outer_pairs)

    def sums_of(*indices):
        return [(totals[k], from_pair[k + 3]) for k in indices]

    def slope_at(column):
        return (slopes[0], 0) if column < cut else (slopes[1], cut)

    def finish_block(k, so_far, *deps):
        _, column, stop = blocks[k]
        indices = (k, k + 3) if k < 3 else (k,)
        return finish(
            me,
            hot_back,
            sums_of(*indices),
            slope_at(column),
            depth,
            so_far,
            column,
            stop - column,
            deps,
        )

    to_pair(0, terms[0])
    to_pair(1, terms[1])
    slopes = {}
    merged = None
    grad_pre = None
    sent_at = {}
    for k in range(1, groups):
        sent_at.setdefault(4 + (k - 1) * 5 // max(groups - 1, 1), []).append(groups - k)
    for j in range(chunks):
        after = []
        ahead = j + 2
        if ahead < chunks:
            previous = (send[j + 1],) if j >= 2 else (terms[ahead - 1],)
            if ahead == 3:
                grads = take_rows(hot_all, first_in + second_in, previous)
            terms[ahead] = product(ahead, previous)
            after.append(terms[ahead])
        if j == 0:
            partial, slopes[0], w_high = forward_product(
                pre_act,
                w_low,
                bias,
                0,
                (w_out, slice(cut, depth)),
                (terms[2],),
            )
            after.append(slopes[0])
        if j == 3:
            merged, slopes[1] = forward_product(
                pre_act, w_high, partial, cut, deps=(terms[ahead],)
            )
            after.append(merged)
        for k in sent_at.get(j, ()):
            outgoing[k] = pack_merged(hot_merged, merged, k, capacity, (terms[ahead],) if ahead in terms else ())
            arrived[k] = exchange(k, outgoing[k])
            after.append(outgoing[k])
        for k in sent_at.get(j - 2, ()):
            after.append(arrived[k])
        if 7 <= j:
            grad_pre = finish_block(j - 7, grad_pre)
            after.append(grad_pre)
        halves[j] = add_term(terms[j], from_pair[j], tuple(after))
        from_far[j] = lax.ppermute(halves[j], ("ctx", "tp"), inner_pairs)
        if j == 0:
            value, _ = lax.optimization_barrier((terms[2], halves[0]))
            to_pair(2, value)
        elif ahead < chunks:
            totals[j - 1], send[ahead] = add_and_choose(
                me, halves[j - 1], from_far[j - 1], terms[ahead], (halves[j],)
            )
            to_pair(ahead, send[ahead])
        else:
            totals[j - 1] = add_term(halves[j - 1], from_far[j - 1], (halves[j],))
            to_pair(ahead, totals[j - 1])
    arrived[0] = pack_merged(hot_merged, merged, 0, capacity, (totals[chunks - 2],))
    embeds = place_rows(
        ctx_slots,
        hot_place,
        [arrived[k] for k in range(groups)],
        text_rows,
        (totals[chunks - 2],),
    )
    totals[chunks - 1] = add_term(halves[chunks - 1], from_far[chunks - 1], (embeds,))
    to_pair(chunks + 2, totals[chunks - 1])
    for k in range(6, chunks):
        grad_pre = finish_block(k, grad_pre)
    return embeds, grad_pre


def shards(pre_act, w_out, b_out, row_slot, ctx_slot, text_rows, cotangent):
    groups = lax.axis_size("ctx") * lax.axis_size("grp")
    rows, depth = pre_act.shape
    width = w_out.shape[1]
    capacity = 2 * rows // groups
    power = lambda value: value & (value - 1) == 0
    fits = (
        lax.axis_size("tp") == 4
        and lax.axis_size("ctx") % 2 == 0
        and 2 <= groups <= 8
        and power(groups)
        and power(capacity)
        and capacity % 32 == 0
        and rows % 256 == 0
        and ctx_slot.shape[0] % 128 == 0
        and depth % 640 == 0
        and width % 512 == 0
    )
    plan = pipelined if fits else plain
    return plan(pre_act, w_out, b_out, row_slot, ctx_slot, text_rows, cotangent)


def solution(mesh):
    in_specs = (
        P(("ctx", "grp"), None),
        P(None, "tp"),
        P("tp"),
        P(("ctx", "grp")),
        P(("ctx", "grp")),
        P(("ctx", "grp"), "tp"),
        P(("ctx", "grp"), "tp"),
    )
    out_specs = (P(("ctx", "grp"), "tp"), P(("ctx", "grp"), None))
    return jax.shard_map(shards, mesh=mesh, in_specs=in_specs, out_specs=out_specs, check_vma=False)
```

time: 175 us -> 132 us (0.75)
  waiting for transfers between devices: 102 us -> 20.1 us
  Pallas kernels: 0 us -> 50.2 us
  starting transfers between devices: 9.07 us -> 57.3 us
  matrix products: 22.8 us -> 0 us
  local copies, waits for them, and re-layouts: 16.9 us -> 2.3 us
  between operations: 14.1 us -> 1.5 us
  other arithmetic: 9.93 us -> 0.08 us
    ppermute x0 -> x44, starting transfers between devices: none -> 57.3 us  [the longest x13 35.6 us: to_pair(): from_pair[j] = lax.ppermute(value, 'tp', outer_pairs)]
    all_to_all x2 -> x0, waiting for transfers between devices: 51.4 us -> none  [the longest x1 25.7 us: shards(): lax.all_to_all(returning.reshape(groups, capacity, width), ('ctx', 'grp')...]
    psum x1 -> x0, waiting for transfers between devices: 50.6 us -> none  [shards(): summed = lax.psum(term, 'tp').astype(jnp.float32)]
    pallas_call x0 -> x53, Pallas kernels: none -> 50.2 us  [call(): pl.pallas_call(body, out_shape=out_shape, in_specs=list(in_specs) + [ANY]...]
    dot_general x2 -> x0, matrix products: 22.8 us -> none  [the longest x1 11.7 us: shards(): lax.dot_general(grad_rows, w_out, (((1,), (1,)), ((), ())), preferred_ele...]
    ppermute x0 -> x44, waiting for transfers between devices: none -> 20.1 us  [the longest x13 13 us: to_pair(): from_pair[j] = lax.ppermute(value, 'tp', outer_pairs)]
    scatter x2 -> x0, local copies, waits for them, and re-layouts: 10.5 us -> none  [the longest x1 6.13 us: shards(): returning = jnp.zeros((slot_count, width), jnp.bfloat16).at[jnp.where(pla...]
    all_to_all x2 -> x0, starting transfers between devices: 9.04 us -> none  [the longest x1 5.3 us: shards(): lax.all_to_all(returning.reshape(groups, capacity, width), ('ctx', 'grp')...]
  transfers between devices with their start and end apart: 3 -> 44, of which waited for: 3 -> 12; matrix products, arithmetic and copies ran while one was open for 13% -> 1% of each run, Pallas kernels for 0% -> 33%
where the time goes in v1:
time: 132 us; the launch traced here: 131 us
  starting transfers between devices  57.3 us (43%)
  Pallas kernels  50.2 us (38%)
  waiting for transfers between devices  20.1 us (15%)
  local copies, waits for them, and re-layouts  2.3 us (2%)
  between operations  1.5 us (1%)
    pallas_call x53, Pallas kernels, call(): pl.pallas_call(body, out_shape=out_shape, in_specs=list(in_specs) + [ANY]...  50.2 us
    ppermute x13, starting transfers between devices, to_pair(): from_pair[j] = lax.ppermute(value, 'tp', outer_pairs)  35.6 us
    ppermute x21, starting transfers between devices, exchange(): return lax.ppermute(piece, GROUP_AXES, [(i, i ^ k) for i in range(groups)])  19.9 us
    ppermute x13, waiting for transfers between devices, to_pair(): from_pair[j] = lax.ppermute(value, 'tp', outer_pairs)  13 us
    ppermute x21, waiting for transfers between devices, exchange(): return lax.ppermute(piece, GROUP_AXES, [(i, i ^ k) for i in range(groups)])  7.03 us
  transfers between devices with their start and end apart: 44, of which 12 were waited for; matrix products, arithmetic and copies ran while one was open for 1% of the time, Pallas kernels for 33%

profile of v1, /device:TPU:0, one launch (start us, length us, event | category | flops | bytes accessed | tf_op | source)
XLA Modules:
  0.0 131.4 jit_solution(17753730108017302745)
XLA Ops:
  0.7 2.9 %pack_context.2 = (bf16[32,2048]{1,0:T(8,128)(2,1)S(1)}, bf16[32,2048]{1,0:T(8,128)(2,1)S(1)}, bf16[32,2048]{1,0:T(8,128)(2,1)S(1)}, bf16[32,2048]{1,0:T(8,128)(...) custom-call(s32[2]{0:T(128)S(1)} %pad_add_fusion.refs_0_, ...), custom_call_target="tpu_custom_call" | custom-call | flops 1000 | bytes 1000 | tf_op jit(solution)/shard_map/pack_context/pallas_call | solution.py:106
  4.1 2.6 %collective-permute-start.2 = (bf16[32,2048]{1,0:T(8,128)(2,1)S(1)}, bf16[32,2048]{1,0:T(8,128)(2,1)S(1)}, u32[]{:S(2)}, u32[]{:S(2)}) collective-permute-start(bf16[32,2048]{1,0:T(8,128)(2,1)S(1)} %get-tuple-element.54), channel_id=1, source_target_pairs={{0,9},{1,8},{8,1},{9,0},{16,25},{17,24},{24,17},{25,16},{2,11},{3,... | collective-permute-start | bytes 393224 | tf_op jit(solution)/shard_map/ppermute | solution.py:489
  6.8 1.5 %collective-permute-start.3 = (bf16[32,2048]{1,0:T(8,128)(2,1)S(1)}, bf16[32,2048]{1,0:T(8,128)(2,1)S(1)}, u32[]{:S(2)}, u32[]{:S(2)}) collective-permute-start(bf16[32,2048]{1,0:T(8,128)(2,1)S(1)} %get-tuple-element.55), channel_id=1, source_target_pairs={{0,16},{1,17},{8,24},{9,25},{16,0},{17,1},{24,8},{25,9},{2,18},{3,... | collective-permute-start | bytes 393224 | tf_op jit(solution)/shard_map/ppermute | solution.py:489
  8.3 1.1 collective-permute-start.5
  9.3 2.1 %collective-permute-start.6 = (bf16[32,2048]{1,0:T(8,128)(2,1)S(1)}, bf16[32,2048]{1,0:T(8,128)(2,1)S(1)}, u32[]{:S(2)}, u32[]{:S(2)}) collective-permute-start(bf16[32,2048]{1,0:T(8,128)(2,1)S(1)} %get-tuple-element.58), channel_id=1, source_target_pairs={{0,25},{1,24},{8,17},{9,16},{16,9},{17,8},{24,1},{25,0},{2,27},{3,... | collective-permute-start | bytes 393224 | tf_op jit(solution)/shard_map/ppermute | solution.py:489
  11.9 0.7 reshape.15.refs_5_.refs_2_
  12.6 5.2 %pack_context.3 = (bf16[32,2048]{1,0:T(8,128)(2,1)S(1)}, bf16[32,2048]{1,0:T(8,128)(2,1)S(1)}, bf16[32,2048]{1,0:T(8,128)(2,1)S(1)}, bf16[32,2048]{1,0:T(8,128)(...) custom-call(s32[2]{0:T(128)S(1)} %pad_add_fusion.refs_0_, ...), custom_call_target="tpu_custom_call" | custom-call | flops 1000 | bytes 1000 | tf_op jit(solution)/shard_map/pack_context/pallas_call | solution.py:106
  17.8 1.3 %route.1 = (bf16[128,256]{1,0:T(8,128)(2,1)S(1)}, bf16[256,512]{1,0:T(8,128)(2,1)S(1)}, bf16[256,256]{1,0:T(8,128)(2,1)S(1)}, bf16[512,256]{1,0:T(8,128)(2,1)S(1)}, bf16[512,512]{1,0:T(8,128)(2,1)S(1)}) custom-call(s32[2]{0:T(128)S(1)} %pad_add_fusion.refs_0_, s32[1,256]{1,0:T(1,128)S(1)} %bitcast.8, s32[1,512]{1,0:T(1,128)S(1)} %bitcast.6, ...), custom_call_target="tpu_custom_call" | custom-call | flops 1000 | bytes 1000 | tf_op jit(solution)/shard_map/route/pallas_call | solution.py:106
  20.0 1.5 %back_product.10.refs_2_.refs_0_ = bf16[128,1024]{1,0:T(8,128)(2,1)S(1)} custom-call(bf16[128,2048]{1,0:T(8,128)(2,1)S(1)} %take_rows.2.refs_0_, bf16[3072,2048]{1,0:T(8,128)(2,1)S(1)} %get-tuple-element.50.refs_1_), custom_call_target="tpu_custom_call" | custom-call | flops 1000 | bytes 1000 | tf_op jit(solution)/shard_map/back_product/pallas_call | solution.py:106
  21.5 2.0 %collective-permute-start.16 = (bf16[128,1024]{1,0:T(8,128)(2,1)S(1)}, bf16[128,1024]{1,0:T(8,128)(2,1)S(1)}, u32[]{:S(2)}, u32[]{:S(2)}) collective-permute-start(bf16[128,1024]{1,0:T(8,128)(2,1)S(1)} %back_product.10.refs_2_.refs_0_), channel_id=1, source_target_pairs={{0,2},{2,0},{4,6},{6,4},{1,3},{3,1},{5,7},{7,5},{8,10},{10,8},{12,... | collective-permute-start | bytes 786440 | tf_op jit(solution)/shard_map/ppermute | solution.py:544
  23.6 1.2 collective-permute-start.9
  24.8 1.5 %collective-permute-start.10 = (bf16[32,2048]{1,0:T(8,128)(2,1)S(1)}, bf16[32,2048]{1,0:T(8,128)(2,1)S(1)}, u32[]{:S(2)}, u32[]{:S(2)}) collective-permute-start(bf16[32,2048]{1,0:T(8,128)(2,1)S(1)} %get-tuple-element.65), channel_id=1, source_target_pairs={{0,16},{1,17},{8,24},{9,25},{16,0},{17,1},{24,8},{25,9},{2,18},{3,... | collective-permute-start | bytes 393224 | tf_op jit(solution)/shard_map/ppermute | solution.py:489
  26.3 0.8 collective-permute-start.11
  27.1 1.5 %back_product.11.refs_2_.refs_0_ = bf16[128,1024]{1,0:T(8,128)(2,1)S(1)} custom-call(bf16[128,2048]{1,0:T(8,128)(2,1)S(1)} %take_rows.2.refs_0_, bf16[3072,2048]{1,0:T(8,128)(2,1)S(1)} %get-tuple-element.50.refs_1_, bf16[128,1024]{1,0:T(8,128)(2,1)S(1)} %back_product.10.refs_2_.refs_0_), custom_call_target="tpu_custom_call" | custom-call | flops 1000 | bytes 1000 | tf_op jit(solution)/shard_map/back_product/pallas_call | solution.py:106
  28.6 1.8 %collective-permute-done.16.refs_1_ = bf16[128,1024]{1,0:T(8,128)(2,1)S(1)} collective-permute-done((bf16[128,1024]{1,0:T(8,128)(2,1)S(1)}, bf16[128,1024]{1,0:T(8,128)(2,1)S(1)}, u32[]{:S(2)}, u32[]{:S(2)}) %collective-permute-start.16) | collective-permute-done | bytes 262176 | tf_op jit(solution)/shard_map/ppermute | solution.py:544
  30.4 1.7 %collective-permute-start.14 = (bf16[128,1024]{1,0:T(8,128)(2,1)S(1)}, bf16[128,1024]{1,0:T(8,128)(2,1)S(1)}, u32[]{:S(2)}, u32[]{:S(2)}) collective-permute-start(bf16[128,1024]{1,0:T(8,128)(2,1)S(1)} %back_product.11.refs_2_.refs_0_), channel_id=1, source_target_pairs={{0,2},{2,0},{4,6},{6,4},{1,3},{3,1},{5,7},{7,5},{8,10},{10,8},{12,... | collective-permute-start | bytes 786440 | tf_op jit(solution)/shard_map/ppermute | solution.py:544
  32.1 1.5 %back_product.12.refs_4_.refs_17_.refs_2_.refs_0_ = bf16[128,1024]{1,0:T(8,128)(2,1)S(1)} custom-call(bf16[128,2048]{1,0:T(8,128)(2,1)S(1)} %take_rows.2.refs_0_, bf16[3072,2048]{1,0:T(8,128)(2,1)S(1)} %get-tuple-element.50.refs_1_, bf16[128,1024]{1,0:T(8,128)(2,1)S(1)} %back_product.11.refs_2_.refs_0_), custom_call_target="tpu_custom_call" | custom-call | flops 1000 | bytes 1000 | tf_op jit(solution)/shard_map/back_product/pallas_call | solution.py:106
  33.6 4.0 %forward_product.2 = (f32[256,2048]{1,0:T(8,128)S(1)}, bf16[256,3072]{1,0:T(8,128)(2,1)S(1)}, bf16[2048,2048]{1,0:T(8,128)(2,1)S(1)}) custom-call(bf16[256,5120]{1,0:T(8,128)(2,1)S(1)} %copy-done, bf16[3072,2048]{1,0:T(8,128)(2,1)S(1)} %get-tuple-element.50.refs_1_, bf16[1,2048]{1,0:T(2,128)(2,1)S(1)} %reshape.15.refs_5_.refs_2_, ...), custom_call_target="tpu_custom_call" | custom-call | flops 1000 | bytes 1000 | tf_op jit(solution)/shard_map/forward_product/pallas_call | solution.py:106
  37.8 1.6 %collective-permute-start.12 = (bf16[32,2048]{1,0:T(8,128)(2,1)S(1)}, bf16[32,2048]{1,0:T(8,128)(2,1)S(1)}, u32[]{:S(2)}, u32[]{:S(2)}) collective-permute-start(bf16[32,2048]{1,0:T(8,128)(2,1)S(1)} %get-tuple-element.67), channel_id=1, source_target_pairs={{0,24},{1,25},{8,16},{9,17},{16,8},{17,9},{24,0},{25,1},{2,26},{3,... | collective-permute-start | bytes 393224 | tf_op jit(solution)/shard_map/ppermute | solution.py:489
  39.4 1.2 collective-permute-start.13
  41.0 2.1 %collective-permute-done.12.refs_15_ = bf16[32,2048]{1,0:T(8,128)(2,1)S(1)} collective-permute-done((bf16[32,2048]{1,0:T(8,128)(2,1)S(1)}, bf16[32,2048]{1,0:T(8,128)(2,1)S(1)}, u32[]{:S(2)}, u32[]{:S(2)}) %collective-permute-start.12) | collective-permute-done | bytes 131104 | tf_op jit(solution)/shard_map/ppermute | solution.py:489
  43.2 3.5 %collective-permute-start.18 = (bf16[128,1024]{1,0:T(8,128)(2,1)S(1)}, bf16[128,1024]{1,0:T(8,128)(2,1)S(1)}, u32[]{:S(2)}, u32[]{:S(2)}) collective-permute-start(bf16[128,1024]{1,0:T(8,128)(2,1)S(1)} %back_product.12.refs_4_.refs_17_.refs_2_.refs_0_), channel_id=1, source_target_pairs={{0,2},{2,0},{4,6},{6,4},{1,3},{3,1},{5,7},{7,5},{8,10},{10,8},{12,... | collective-permute-start | bytes 786440 | tf_op jit(solution)/shard_map/ppermute | solution.py:544
  46.9 2.3 %collective-permute-done.7.refs_10_ = bf16[32,2048]{1,0:T(8,128)(2,1)S(1)} collective-permute-done((bf16[32,2048]{1,0:T(8,128)(2,1)S(1)}, bf16[32,2048]{1,0:T(8,128)(2,1)S(1)}, u32[]{:S(2)}, u32[]{:S(2)}) %collective-permute-start.7) | collective-permute-done | bytes 131104 | tf_op jit(solution)/shard_map/ppermute | solution.py:489
  49.2 0.7 take_rows.3.refs_0_
  49.9 1.5 %back_product.13.refs_2_.refs_3_.refs_0_ = bf16[128,1024]{1,0:T(8,128)(2,1)S(1)} custom-call(bf16[256,2048]{1,0:T(8,128)(2,1)S(1)} %take_rows.3.refs_0_, bf16[3072,2048]{1,0:T(8,128)(2,1)S(1)} %get-tuple-element.50.refs_1_, bf16[128,1024]{1,0:T(8,128)(2,1)S(1)} %back_product.12.refs_4_.refs_17_.refs_2_.refs_0_), custom_call_target="tpu_custom_call" | custom-call | flops 1000 | bytes 1000 | tf_op jit(solution)/shard_map/back_product/pallas_call | solution.py:106
  51.6 0.7 add_and_choose.7
  52.3 2.7 %collective-permute-start.21 = (bf16[128,1024]{1,0:T(8,128)(2,1)S(1)}, bf16[128,1024]{1,0:T(8,128)(2,1)S(1)}, u32[]{:S(2)}, u32[]{:S(2)}) collective-permute-start(bf16[128,1024]{1,0:T(8,128)(2,1)S(1)} %get-tuple-element.70.refs_2_), channel_id=1, source_target_pairs={{0,2},{2,0},{4,6},{6,4},{1,3},{3,1},{5,7},{7,5},{8,10},{10,8},{12,... | collective-permute-start | bytes 786440 | tf_op jit(solution)/shard_map/ppermute | solution.py:544
  55.0 1.7 %back_product.14.refs_2_.refs_3_.refs_0_ = bf16[128,1024]{1,0:T(8,128)(2,1)S(1)} custom-call(bf16[256,2048]{1,0:T(8,128)(2,1)S(1)} %take_rows.3.refs_0_, bf16[3072,2048]{1,0:T(8,128)(2,1)S(1)} %get-tuple-element.50.refs_1_, bf16[128,1024]{1,0:T(8,128)(2,1)S(1)} %get-tuple-element.70.refs_2_), custom_call_target="tpu_custom_call" | custom-call | flops 1000 | bytes 1000 | tf_op jit(solution)/shard_map/back_product/pallas_call | solution.py:106
  56.8 0.6 add_and_choose.8
  57.5 6.6 %collective-permute-start.19 = (bf16[128,1024]{1,0:T(8,128)(2,1)S(1)}, bf16[128,1024]{1,0:T(8,128)(2,1)S(1)}, u32[]{:S(2)}, u32[]{:S(2)}) collective-permute-start(bf16[128,1024]{1,0:T(8,128)(2,1)S(1)} %get-tuple-element.72.refs_2_), channel_id=1, source_target_pairs={{0,2},{2,0},{4,6},{6,4},{1,3},{3,1},{5,7},{7,5},{8,10},{10,8},{12,... | collective-permute-start | bytes 786440 | tf_op jit(solution)/shard_map/ppermute | solution.py:544
  64.1 1.5 %back_product.15.refs_3_.refs_2_.refs_0_ = bf16[128,1024]{1,0:T(8,128)(2,1)S(1)} custom-call(bf16[256,2048]{1,0:T(8,128)(2,1)S(1)} %take_rows.3.refs_0_, bf16[3072,2048]{1,0:T(8,128)(2,1)S(1)} %get-tuple-element.50.refs_1_, bf16[128,1024]{1,0:T(8,128)(2,1)S(1)} %get-tuple-element.72.refs_2_), custom_call_target="tpu_custom_call" | custom-call | flops 1000 | bytes 1000 | tf_op jit(solution)/shard_map/back_product/pallas_call | solution.py:106
  65.6 2.7 %forward_product.3 = (bf16[256,2048]{1,0:T(8,128)(2,1)S(1)}, bf16[256,2048]{1,0:T(8,128)(2,1)S(1)}) custom-call(bf16[256,5120]{1,0:T(8,128)(2,1)S(1)} %copy-done, bf16[2048,2048]{1,0:T(8,128)(2,1)S(1)} %get-tuple-element.59.refs_1_, f32[256,2048]{1,0:T(8,128)S(1)} %get-tuple-element.60.refs_2_, bf16[128,1024]{1,0:T(8,128)(2,1)S(1)} %back_product.15.refs_3_.refs_2_.refs_0_), custom_call_target="tpu_custom_call" | custom-call | flops 1000 | bytes 1000 | tf_op jit(solution)/shard_map/forward_product/pallas_call | solution.py:106
  68.5 0.7 add_and_choose.9
  69.2 0.7 back_product.16.refs_2_.refs_3_.refs_0_
  71.2 1.8 %collective-permute-start.28 = (bf16[64,2048]{1,0:T(8,128)(2,1)S(1)}, bf16[64,2048]{1,0:T(8,128)(2,1)S(1)}, u32[]{:S(2)}, u32[]{:S(2)}) collective-permute-start(bf16[64,2048]{1,0:T(8,128)(2,1)S(1)} %pack_merged.9.refs_4_), channel_id=1, source_target_pairs={{0,24},{1,25},{8,16},{9,17},{16,8},{17,9},{24,0},{25,1},{2,26},{3,... | collective-permute-start | bytes 786440 | tf_op jit(solution)/shard_map/ppermute | solution.py:489
  73.7 1.9 %collective-permute-start.26 = (bf16[128,1024]{1,0:T(8,128)(2,1)S(1)}, bf16[128,1024]{1,0:T(8,128)(2,1)S(1)}, u32[]{:S(2)}, u32[]{:S(2)}) collective-permute-start(bf16[128,1024]{1,0:T(8,128)(2,1)S(1)} %get-tuple-element.75.refs_2_), channel_id=1, source_target_pairs={{0,2},{2,0},{4,6},{6,4},{1,3},{3,1},{5,7},{7,5},{8,10},{10,8},{12,... | collective-permute-start | bytes 786440 | tf_op jit(solution)/shard_map/ppermute | solution.py:544
  75.6 0.7 back_product.17.refs_2_.refs_3_.refs_0_
  76.6 2.4 %collective-permute-done.24.refs_1_.refs_4_ = bf16[128,1024]{1,0:T(8,128)(2,1)S(1)} collective-permute-done((bf16[128,1024]{1,0:T(8,128)(2,1)S(1)}, bf16[128,1024]{1,0:T(8,128)(2,1)S(1)}, u32[]{:S(2)}, u32[]{:S(2)}) %collective-permute-start.24) | collective-permute-done | bytes 262176 | tf_op jit(solution)/shard_map/ppermute | solution.py:544
  79.2 0.6 add_and_choose.11
  79.9 2.0 %collective-permute-start.32 = (bf16[128,1024]{1,0:T(8,128)(2,1)S(1)}, bf16[128,1024]{1,0:T(8,128)(2,1)S(1)}, u32[]{:S(2)}, u32[]{:S(2)}) collective-permute-start(bf16[128,1024]{1,0:T(8,128)(2,1)S(1)} %get-tuple-element.76.refs_2_), channel_id=1, source_target_pairs={{0,2},{2,0},{4,6},{6,4},{1,3},{3,1},{5,7},{7,5},{8,10},{10,8},{12,... | collective-permute-start | bytes 786440 | tf_op jit(solution)/shard_map/ppermute | solution.py:544
  81.9 0.7 back_product.18.refs_2_.refs_3_.refs_0_
  83.3 1.9 %collective-permute-done.28.refs_6_.refs_9_ = bf16[64,2048]{1,0:T(8,128)(2,1)S(1)} collective-permute-done((bf16[64,2048]{1,0:T(8,128)(2,1)S(1)}, bf16[64,2048]{1,0:T(8,128)(2,1)S(1)}, u32[]{:S(2)}, u32[]{:S(2)}) %collective-permute-start.28) | collective-permute-done | bytes 262176 | tf_op jit(solution)/shard_map/ppermute | solution.py:489
  85.3 0.7 collective-permute-start.34
  86.0 0.7 add_and_choose.12
  86.6 0.7 back_product.19.refs_2_.refs_3_.refs_0_
  87.4 1.2 collective-permute-start.31
  88.9 1.0 collective-permute-done.32.refs_6_.refs_1_
  89.9 2.1 %collective-permute-start.29 = (bf16[128,1024]{1,0:T(8,128)(2,1)S(1)}, bf16[128,1024]{1,0:T(8,128)(2,1)S(1)}, u32[]{:S(2)}, u32[]{:S(2)}) collective-permute-start(bf16[128,1024]{1,0:T(8,128)(2,1)S(1)} %get-tuple-element.77.refs_2_), channel_id=1, source_target_pairs={{0,2},{2,0},{4,6},{6,4},{1,3},{3,1},{5,7},{7,5},{8,10},{10,8},{12,... | collective-permute-start | bytes 786440 | tf_op jit(solution)/shard_map/ppermute | solution.py:544
  92.0 1.7 %finish.7.refs_7_.refs_5_ = bf16[256,5120]{1,0:T(8,128)(2,1)} custom-call(s32[2]{0:T(128)S(1)} %pad_add_fusion.refs_0_, bf16[256,256]{1,0:T(8,128)(2,1)S(1)} %get-tuple-element.78.refs_1_, bf16[256,3072]{1,0:T(8,128)(2,1)S(1)} %get-tuple-element.69.refs_3_.refs_2_, bf16[128,1024]{1,0:T(8,128)(2,1)S(1)} %get-tuple-element.81.refs_3_, ...), custom_call_target="tpu_custom_call" | custom-call | flops 1000 | bytes 1000 | tf_op jit(solution)/shard_map/finish/pallas_call | solution.py:106
  94.7 1.9 %collective-permute-start.36 = (bf16[128,1024]{1,0:T(8,128)(2,1)S(1)}, bf16[128,1024]{1,0:T(8,128)(2,1)S(1)}, u32[]{:S(2)}, u32[]{:S(2)}) collective-permute-start(bf16[128,1024]{1,0:T(8,128)(2,1)S(1)} %get-tuple-element.83), channel_id=1, source_target_pairs={{0,2},{2,0},{4,6},{6,4},{1,3},{3,1},{5,7},{7,5},{8,10},{10,8},{12,... | collective-permute-start | bytes 786440 | tf_op jit(solution)/shard_map/ppermute | solution.py:544
  96.9 1.7 %finish.8.refs_5_.refs_7_ = bf16[256,5120]{1,0:T(8,128)(2,1)} custom-call(s32[2]{0:T(128)S(1)} %pad_add_fusion.refs_0_, bf16[256,256]{1,0:T(8,128)(2,1)S(1)} %get-tuple-element.78.refs_1_, bf16[256,3072]{1,0:T(8,128)(2,1)S(1)} %get-tuple-element.69.refs_3_.refs_2_, bf16[128,1024]{1,0:T(8,128)(2,1)S(1)} %get-tuple-element.79.refs_3_, ...), custom_call_target="tpu_custom_call", output_to_operand_aliasing={{}: (7, {})} | custom-call | flops 1000 | bytes 1000 | tf_op jit(solution)/shard_map/finish/pallas_call | solution.py:106
  99.3 1.4 %collective-permute-start.38 = (bf16[64,2048]{1,0:T(8,128)(2,1)S(1)}, bf16[64,2048]{1,0:T(8,128)(2,1)S(1)}, u32[]{:S(2)}, u32[]{:S(2)}) collective-permute-start(bf16[64,2048]{1,0:T(8,128)(2,1)S(1)} %pack_merged.13.refs_2_), channel_id=1, source_target_pairs={{0,1},{1,0},{8,9},{9,8},{16,17},{17,16},{24,25},{25,24},{2,3},{3,2... | collective-permute-start | bytes 786440 | tf_op jit(solution)/shard_map/ppermute | solution.py:489
  100.7 1.7 %finish.9.refs_3_.refs_5_ = bf16[256,5120]{1,0:T(8,128)(2,1)} custom-call(s32[2]{0:T(128)S(1)} %pad_add_fusion.refs_0_, bf16[256,256]{1,0:T(8,128)(2,1)S(1)} %get-tuple-element.78.refs_1_, bf16[256,3072]{1,0:T(8,128)(2,1)S(1)} %get-tuple-element.69.refs_3_.refs_2_, bf16[128,1024]{1,0:T(8,128)(2,1)S(1)} %get-tuple-element.84.refs_3_, ...), custom_call_target="tpu_custom_call", output_to_operand_aliasing={{}: (7, {})} | custom-call | flops 1000 | bytes 1000 | tf_op jit(solution)/shard_map/finish/pallas_call | solution.py:106
  102.4 2.1 %collective-permute-done.36.refs_1_.refs_4_ = bf16[128,1024]{1,0:T(8,128)(2,1)S(1)} collective-permute-done((bf16[128,1024]{1,0:T(8,128)(2,1)S(1)}, bf16[128,1024]{1,0:T(8,128)(2,1)S(1)}, u32[]{:S(2)}, u32[]{:S(2)}) %collective-permute-start.36) | collective-permute-done | bytes 262176 | tf_op jit(solution)/shard_map/ppermute | solution.py:544
  104.9 8.9 %collective-permute-start.43 = (bf16[128,1024]{1,0:T(8,128)(2,1)S(1)}, bf16[128,1024]{1,0:T(8,128)(2,1)S(1)}, u32[]{:S(2)}, u32[]{:S(2)}) collective-permute-start(bf16[128,1024]{1,0:T(8,128)(2,1)S(1)} %add_term.25.refs_3_), channel_id=1, source_target_pairs={{0,2},{2,0},{4,6},{6,4},{1,3},{3,1},{5,7},{7,5},{8,10},{10,8},{12,... | collective-permute-start | bytes 786440 | tf_op jit(solution)/shard_map/ppermute | solution.py:544
  114.2 2.1 %place_rows.1.refs_2_ = bf16[512,2048]{1,0:T(8,128)(2,1)} custom-call(s32[1,512]{1,0:T(1,128)S(1)} %bitcast.7, bf16[512,512]{1,0:T(8,128)(2,1)S(1)} %get-tuple-element.48.refs_1_, bf16[512,2048]{1,0:T(8,128)(2,1)S(1)} %copy-done.2, bf16[64,2048]{1,0:T(8,128)(2,1)S(1)} %pack_merged.15.refs_3_, bf16[64,2048]{1,0:T(8,128)(2,1)S(1)} %collective-permute-done.38.refs_4_, ...), custom_call_target="tpu_custom_call" | custom-call | flops 1000 | bytes 1000 | tf_op jit(solution)/shard_map/place_rows/pallas_call | solution.py:106
  116.3 1.6 %copy-done.1 = bf16[512,2048]{1,0:T(8,128)(2,1)S(1)} copy-done((bf16[512,2048]{1,0:T(8,128)(2,1)S(1)}, bf16[512,2048]{1,0:T(8,128)(2,1)}, u32[]{:S(2)}) %copy-start.1) | copy-done | bytes 2097176
  118.0 2.1 %collective-permute-start.40 = (bf16[128,1024]{1,0:T(8,128)(2,1)S(1)}, bf16[128,1024]{1,0:T(8,128)(2,1)S(1)}, u32[]{:S(2)}, u32[]{:S(2)}) collective-permute-start(bf16[128,1024]{1,0:T(8,128)(2,1)S(1)} %add_term.24.refs_3_), channel_id=1, source_target_pairs={{0,2},{2,0},{4,6},{6,4},{1,3},{3,1},{5,7},{7,5},{8,10},{10,8},{12,... | collective-permute-start | bytes 786440 | tf_op jit(solution)/shard_map/ppermute | solution.py:544
  120.1 1.5 %finish.10.refs_5_ = bf16[256,5120]{1,0:T(8,128)(2,1)} custom-call(s32[2]{0:T(128)S(1)} %pad_add_fusion.refs_0_, bf16[256,256]{1,0:T(8,128)(2,1)S(1)} %get-tuple-element.78.refs_1_, bf16[256,2048]{1,0:T(8,128)(2,1)S(1)} %get-tuple-element.86.refs_2_, bf16[128,1024]{1,0:T(8,128)(2,1)S(1)} %get-tuple-element.87.refs_3_, ...), custom_call_target="tpu_custom_call", output_to_operand_aliasing={{}: (5, {})} | custom-call | flops 1000 | bytes 1000 | tf_op jit(solution)/shard_map/finish/pallas_call | solution.py:106
  121.6 1.5 %finish.11.refs_5_ = bf16[256,5120]{1,0:T(8,128)(2,1)} custom-call(s32[2]{0:T(128)S(1)} %pad_add_fusion.refs_0_, bf16[256,256]{1,0:T(8,128)(2,1)S(1)} %get-tuple-element.78.refs_1_, bf16[256,2048]{1,0:T(8,128)(2,1)S(1)} %get-tuple-element.86.refs_2_, bf16[128,1024]{1,0:T(8,128)(2,1)S(1)} %add_term.25.refs_3_, ...), custom_call_target="tpu_custom_call", output_to_operand_aliasing={{}: (5, {})} | custom-call | flops 1000 | bytes 1000 | tf_op jit(solution)/shard_map/finish/pallas_call | solution.py:106
  123.1 3.5 %collective-permute-done.41.refs_4_ = bf16[128,1024]{1,0:T(8,128)(2,1)S(1)} collective-permute-done((bf16[128,1024]{1,0:T(8,128)(2,1)S(1)}, bf16[128,1024]{1,0:T(8,128)(2,1)S(1)}, u32[]{:S(2)}, u32[]{:S(2)}) %collective-permute-start.41) | collective-permute-done | bytes 262176 | tf_op jit(solution)/shard_map/ppermute | solution.py:544
  126.6 1.5 %finish.12.refs_5_ = bf16[256,5120]{1,0:T(8,128)(2,1)} custom-call(s32[2]{0:T(128)S(1)} %pad_add_fusion.refs_0_, bf16[256,256]{1,0:T(8,128)(2,1)S(1)} %get-tuple-element.78.refs_1_, bf16[256,2048]{1,0:T(8,128)(2,1)S(1)} %get-tuple-element.86.refs_2_, bf16[128,1024]{1,0:T(8,128)(2,1)S(1)} %add_term.23.refs_2_.refs_11_.refs_3_, ...), custom_call_target="tpu_custom_call", output_to_operand_aliasing={{}: (5, {})} | custom-call | flops 1000 | bytes 1000 | tf_op jit(solution)/shard_map/finish/pallas_call | solution.py:106
  128.1 1.7 %collective-permute-done.40.refs_4_ = bf16[128,1024]{1,0:T(8,128)(2,1)S(1)} collective-permute-done((bf16[128,1024]{1,0:T(8,128)(2,1)S(1)}, bf16[128,1024]{1,0:T(8,128)(2,1)S(1)}, u32[]{:S(2)}, u32[]{:S(2)}) %collective-permute-start.40) | collective-permute-done | bytes 262176 | tf_op jit(solution)/shard_map/ppermute | solution.py:544
  129.8 1.5 %finish.13 = bf16[256,5120]{1,0:T(8,128)(2,1)} custom-call(s32[2]{0:T(128)S(1)} %pad_add_fusion.refs_0_, bf16[256,256]{1,0:T(8,128)(2,1)S(1)} %get-tuple-element.78.refs_1_, bf16[256,2048]{1,0:T(8,128)(2,1)S(1)} %get-tuple-element.86.refs_2_, bf16[128,1024]{1,0:T(8,128)(2,1)S(1)} %add_term.24.refs_3_, ...), custom_call_target="tpu_custom_call", output_to_operand_aliasing={{}: (5, {})} | custom-call | flops 1000 | bytes 1000 | tf_op jit(solution)/shard_map/finish/pallas_call | solution.py:106
  (89 shorter events, 9.5 us)
Async XLA Ops:
  3.6 5.7 %collective-permute-start.1 = (bf16[32,2048]{1,0:T(8,128)(2,1)S(1)}, bf16[32,2048]{1,0:T(8,128)(2,1)S(1)}, u32[]{:S(2)}, u32[]{:S(2)}) collective-permute-start(bf16[32,2048]{1,0:T(8,128)(2,1)S(1)} %get-tuple-element.53), channel_id=1, source_target_pairs={{0,8},{1,9},{8,0},{9,1},{16,24},{17,25},{24,16},{25,17},{2,10},{3,... | collective-permute-start | bytes 393224 | tf_op jit(solution)/shard_map/ppermute | solution.py:489
  4.1 7.3 %collective-permute-start.2 = (bf16[32,2048]{1,0:T(8,128)(2,1)S(1)}, bf16[32,2048]{1,0:T(8,128)(2,1)S(1)}, u32[]{:S(2)}, u32[]{:S(2)}) collective-permute-start(bf16[32,2048]{1,0:T(8,128)(2,1)S(1)} %get-tuple-element.54), channel_id=1, source_target_pairs={{0,9},{1,8},{8,1},{9,0},{16,25},{17,24},{24,17},{25,16},{2,11},{3,... | collective-permute-start | bytes 393224 | tf_op jit(solution)/shard_map/ppermute | solution.py:489
  6.8 12.4 %collective-permute-start.3 = (bf16[32,2048]{1,0:T(8,128)(2,1)S(1)}, bf16[32,2048]{1,0:T(8,128)(2,1)S(1)}, u32[]{:S(2)}, u32[]{:S(2)}) collective-permute-start(bf16[32,2048]{1,0:T(8,128)(2,1)S(1)} %get-tuple-element.55), channel_id=1, source_target_pairs={{0,16},{1,17},{8,24},{9,25},{16,0},{17,1},{24,8},{25,9},{2,18},{3,... | collective-permute-start | bytes 393224 | tf_op jit(solution)/shard_map/ppermute | solution.py:489
  8.3 10.9 %collective-permute-start.4 = (bf16[32,2048]{1,0:T(8,128)(2,1)S(1)}, bf16[32,2048]{1,0:T(8,128)(2,1)S(1)}, u32[]{:S(2)}, u32[]{:S(2)}) collective-permute-start(bf16[32,2048]{1,0:T(8,128)(2,1)S(1)} %get-tuple-element.56), channel_id=1, source_target_pairs={{0,17},{1,16},{8,25},{9,24},{16,1},{17,0},{24,9},{25,8},{2,19},{3,... | collective-permute-start | bytes 393224 | tf_op jit(solution)/shard_map/ppermute | solution.py:489
  8.3 10.9 %collective-permute-start.5 = (bf16[32,2048]{1,0:T(8,128)(2,1)S(1)}, bf16[32,2048]{1,0:T(8,128)(2,1)S(1)}, u32[]{:S(2)}, u32[]{:S(2)}) collective-permute-start(bf16[32,2048]{1,0:T(8,128)(2,1)S(1)} %get-tuple-element.57), channel_id=1, source_target_pairs={{0,24},{1,25},{8,16},{9,17},{16,8},{17,9},{24,0},{25,1},{2,26},{3,... | collective-permute-start | bytes 393224 | tf_op jit(solution)/shard_map/ppermute | solution.py:489
  9.3 10.3 %collective-permute-start.6 = (bf16[32,2048]{1,0:T(8,128)(2,1)S(1)}, bf16[32,2048]{1,0:T(8,128)(2,1)S(1)}, u32[]{:S(2)}, u32[]{:S(2)}) collective-permute-start(bf16[32,2048]{1,0:T(8,128)(2,1)S(1)} %get-tuple-element.58), channel_id=1, source_target_pairs={{0,25},{1,24},{8,17},{9,16},{16,9},{17,8},{24,1},{25,0},{2,27},{3,... | collective-permute-start | bytes 393224 | tf_op jit(solution)/shard_map/ppermute | solution.py:489
  11.4 8.2 %collective-permute-start = (bf16[32,2048]{1,0:T(8,128)(2,1)S(1)}, bf16[32,2048]{1,0:T(8,128)(2,1)S(1)}, u32[]{:S(2)}, u32[]{:S(2)}) collective-permute-start(bf16[32,2048]{1,0:T(8,128)(2,1)S(1)} %get-tuple-element.46.refs_4_), channel_id=1, source_target_pairs={{0,1},{1,0},{8,9},{9,8},{16,17},{17,16},{24,25},{25,24},{2,3},{3,2... | collective-permute-start | bytes 393224 | tf_op jit(solution)/shard_map/ppermute | solution.py:489
  12.6 5.2 %copy-start.3 = (s32[512]{0:T(512)S(1)}, s32[512]{0:T(512)}, u32[]{:S(2)}) copy-start(s32[512]{0:T(512)} %param.11) | copy-start | bytes 6148
  12.6 5.2 %copy-start.4 = (s32[256]{0:T(256)S(1)}, s32[256]{0:T(256)}, u32[]{:S(2)}) copy-start(s32[256]{0:T(256)} %param.10) | copy-start | bytes 3076
  21.5 8.9 %collective-permute-start.16 = (bf16[128,1024]{1,0:T(8,128)(2,1)S(1)}, bf16[128,1024]{1,0:T(8,128)(2,1)S(1)}, u32[]{:S(2)}, u32[]{:S(2)}) collective-permute-start(bf16[128,1024]{1,0:T(8,128)(2,1)S(1)} %back_product.10.refs_2_.refs_0_), channel_id=1, source_target_pairs={{0,2},{2,0},{4,6},{6,4},{1,3},{3,1},{5,7},{7,5},{8,10},{10,8},{12,... | collective-permute-start | bytes 786440 | tf_op jit(solution)/shard_map/ppermute | solution.py:544
  23.5 14.2 %collective-permute-start.8 = (bf16[32,2048]{1,0:T(8,128)(2,1)S(1)}, bf16[32,2048]{1,0:T(8,128)(2,1)S(1)}, u32[]{:S(2)}, u32[]{:S(2)}) collective-permute-start(bf16[32,2048]{1,0:T(8,128)(2,1)S(1)} %get-tuple-element.63), channel_id=1, source_target_pairs={{0,8},{1,9},{8,0},{9,1},{16,24},{17,25},{24,16},{25,17},{2,10},{3,... | collective-permute-start | bytes 393224 | tf_op jit(solution)/shard_map/ppermute | solution.py:489
  23.6 14.1 %collective-permute-start.9 = (bf16[32,2048]{1,0:T(8,128)(2,1)S(1)}, bf16[32,2048]{1,0:T(8,128)(2,1)S(1)}, u32[]{:S(2)}, u32[]{:S(2)}) collective-permute-start(bf16[32,2048]{1,0:T(8,128)(2,1)S(1)} %get-tuple-element.64), channel_id=1, source_target_pairs={{0,9},{1,8},{8,1},{9,0},{16,25},{17,24},{24,17},{25,16},{2,11},{3,... | collective-permute-start | bytes 393224 | tf_op jit(solution)/shard_map/ppermute | solution.py:489
  24.8 14.6 %collective-permute-start.10 = (bf16[32,2048]{1,0:T(8,128)(2,1)S(1)}, bf16[32,2048]{1,0:T(8,128)(2,1)S(1)}, u32[]{:S(2)}, u32[]{:S(2)}) collective-permute-start(bf16[32,2048]{1,0:T(8,128)(2,1)S(1)} %get-tuple-element.65), channel_id=1, source_target_pairs={{0,16},{1,17},{8,24},{9,25},{16,0},{17,1},{24,8},{25,9},{2,18},{3,... | collective-permute-start | bytes 393224 | tf_op jit(solution)/shard_map/ppermute | solution.py:489
  26.3 14.2 %collective-permute-start.11 = (bf16[32,2048]{1,0:T(8,128)(2,1)S(1)}, bf16[32,2048]{1,0:T(8,128)(2,1)S(1)}, u32[]{:S(2)}, u32[]{:S(2)}) collective-permute-start(bf16[32,2048]{1,0:T(8,128)(2,1)S(1)} %get-tuple-element.66), channel_id=1, source_target_pairs={{0,17},{1,16},{8,25},{9,24},{16,1},{17,0},{24,9},{25,8},{2,19},{3,... | collective-permute-start | bytes 393224 | tf_op jit(solution)/shard_map/ppermute | solution.py:489
  28.6 5.1 %copy-start = (bf16[256,5120]{1,0:T(8,128)(2,1)S(1)}, bf16[256,5120]{1,0:T(8,128)(2,1)}, u32[]{:S(2)}) copy-start(bf16[256,5120]{1,0:T(8,128)(2,1)} %refs_0_.3) | copy-start | bytes 7864324
  30.4 21.1 %collective-permute-start.14 = (bf16[128,1024]{1,0:T(8,128)(2,1)S(1)}, bf16[128,1024]{1,0:T(8,128)(2,1)S(1)}, u32[]{:S(2)}, u32[]{:S(2)}) collective-permute-start(bf16[128,1024]{1,0:T(8,128)(2,1)S(1)} %back_product.11.refs_2_.refs_0_), channel_id=1, source_target_pairs={{0,2},{2,0},{4,6},{6,4},{1,3},{3,1},{5,7},{7,5},{8,10},{10,8},{12,... | collective-permute-start | bytes 786440 | tf_op jit(solution)/shard_map/ppermute | solution.py:544
  37.7 13.9 %collective-permute-start.17 = (bf16[128,1024]{1,0:T(8,128)(2,1)S(1)}, bf16[128,1024]{1,0:T(8,128)(2,1)S(1)}, u32[]{:S(2)}, u32[]{:S(2)}) collective-permute-start(bf16[128,1024]{1,0:T(8,128)(2,1)S(1)} %add_term.14.refs_1_), channel_id=1, source_target_pairs={{0,8},{2,4},{4,2},{6,14},{8,0},{10,12},{12,10},{14,6},{16,24},{18,... | collective-permute-start | bytes 786440 | tf_op jit(solution)/shard_map/ppermute | solution.py:609
  37.8 5.4 %collective-permute-start.12 = (bf16[32,2048]{1,0:T(8,128)(2,1)S(1)}, bf16[32,2048]{1,0:T(8,128)(2,1)S(1)}, u32[]{:S(2)}, u32[]{:S(2)}) collective-permute-start(bf16[32,2048]{1,0:T(8,128)(2,1)S(1)} %get-tuple-element.67), channel_id=1, source_target_pairs={{0,24},{1,25},{8,16},{9,17},{16,8},{17,9},{24,0},{25,1},{2,26},{3,... | collective-permute-start | bytes 393224 | tf_op jit(solution)/shard_map/ppermute | solution.py:489
  39.4 7.6 %collective-permute-start.13 = (bf16[32,2048]{1,0:T(8,128)(2,1)S(1)}, bf16[32,2048]{1,0:T(8,128)(2,1)S(1)}, u32[]{:S(2)}, u32[]{:S(2)}) collective-permute-start(bf16[32,2048]{1,0:T(8,128)(2,1)S(1)} %get-tuple-element.68), channel_id=1, source_target_pairs={{0,25},{1,24},{8,17},{9,16},{16,9},{17,8},{24,1},{25,0},{2,27},{3,... | collective-permute-start | bytes 393224 | tf_op jit(solution)/shard_map/ppermute | solution.py:489
  40.5 8.7 %collective-permute-start.7 = (bf16[32,2048]{1,0:T(8,128)(2,1)S(1)}, bf16[32,2048]{1,0:T(8,128)(2,1)S(1)}, u32[]{:S(2)}, u32[]{:S(2)}) collective-permute-start(bf16[32,2048]{1,0:T(8,128)(2,1)S(1)} %get-tuple-element.47.refs_3_), channel_id=1, source_target_pairs={{0,1},{1,0},{8,9},{9,8},{16,17},{17,16},{24,25},{25,24},{2,3},{3,2... | collective-permute-start | bytes 393224 | tf_op jit(solution)/shard_map/ppermute | solution.py:489
  43.2 13.4 %collective-permute-start.18 = (bf16[128,1024]{1,0:T(8,128)(2,1)S(1)}, bf16[128,1024]{1,0:T(8,128)(2,1)S(1)}, u32[]{:S(2)}, u32[]{:S(2)}) collective-permute-start(bf16[128,1024]{1,0:T(8,128)(2,1)S(1)} %back_product.12.refs_4_.refs_17_.refs_2_.refs_0_), channel_id=1, source_target_pairs={{0,2},{2,0},{4,6},{6,4},{1,3},{3,1},{5,7},{7,5},{8,10},{10,8},{12,... | collective-permute-start | bytes 786440 | tf_op jit(solution)/shard_map/ppermute | solution.py:544
  51.5 5.3 %collective-permute-start.15 = (bf16[128,1024]{1,0:T(8,128)(2,1)S(1)}, bf16[128,1024]{1,0:T(8,128)(2,1)S(1)}, u32[]{:S(2)}, u32[]{:S(2)}) collective-permute-start(bf16[128,1024]{1,0:T(8,128)(2,1)S(1)} %add_term.13.refs_4_.refs_1_), channel_id=1, source_target_pairs={{0,8},{2,4},{4,2},{6,14},{8,0},{10,12},{12,10},{14,6},{16,24},{18,... | collective-permute-start | bytes 786440 | tf_op jit(solution)/shard_map/ppermute | solution.py:609
  52.3 16.1 %collective-permute-start.21 = (bf16[128,1024]{1,0:T(8,128)(2,1)S(1)}, bf16[128,1024]{1,0:T(8,128)(2,1)S(1)}, u32[]{:S(2)}, u32[]{:S(2)}) collective-permute-start(bf16[128,1024]{1,0:T(8,128)(2,1)S(1)} %get-tuple-element.70.refs_2_), channel_id=1, source_target_pairs={{0,2},{2,0},{4,6},{6,4},{1,3},{3,1},{5,7},{7,5},{8,10},{10,8},{12,... | collective-permute-start | bytes 786440 | tf_op jit(solution)/shard_map/ppermute | solution.py:544
  56.7 11.8 %collective-permute-start.20 = (bf16[128,1024]{1,0:T(8,128)(2,1)S(1)}, bf16[128,1024]{1,0:T(8,128)(2,1)S(1)}, u32[]{:S(2)}, u32[]{:S(2)}) collective-permute-start(bf16[128,1024]{1,0:T(8,128)(2,1)S(1)} %add_term.15.refs_4_.refs_1_), channel_id=1, source_target_pairs={{0,8},{2,4},{4,2},{6,14},{8,0},{10,12},{12,10},{14,6},{16,24},{18,... | collective-permute-start | bytes 786440 | tf_op jit(solution)/shard_map/ppermute | solution.py:609
  57.5 13.1 %collective-permute-start.19 = (bf16[128,1024]{1,0:T(8,128)(2,1)S(1)}, bf16[128,1024]{1,0:T(8,128)(2,1)S(1)}, u32[]{:S(2)}, u32[]{:S(2)}) collective-permute-start(bf16[128,1024]{1,0:T(8,128)(2,1)S(1)} %get-tuple-element.72.refs_2_), channel_id=1, source_target_pairs={{0,2},{2,0},{4,6},{6,4},{1,3},{3,1},{5,7},{7,5},{8,10},{10,8},{12,... | collective-permute-start | bytes 786440 | tf_op jit(solution)/shard_map/ppermute | solution.py:544
  68.4 4.6 %collective-permute-start.23 = (bf16[128,1024]{1,0:T(8,128)(2,1)S(1)}, bf16[128,1024]{1,0:T(8,128)(2,1)S(1)}, u32[]{:S(2)}, u32[]{:S(2)}) collective-permute-start(bf16[128,1024]{1,0:T(8,128)(2,1)S(1)} %add_term.16.refs_4_.refs_1_), channel_id=1, source_target_pairs={{0,8},{2,4},{4,2},{6,14},{8,0},{10,12},{12,10},{14,6},{16,24},{18,... | collective-permute-start | bytes 786440 | tf_op jit(solution)/shard_map/ppermute | solution.py:609
  69.9 9.2 %collective-permute-start.24 = (bf16[128,1024]{1,0:T(8,128)(2,1)S(1)}, bf16[128,1024]{1,0:T(8,128)(2,1)S(1)}, u32[]{:S(2)}, u32[]{:S(2)}) collective-permute-start(bf16[128,1024]{1,0:T(8,128)(2,1)S(1)} %get-tuple-element.74.refs_2_), channel_id=1, source_target_pairs={{0,2},{2,0},{4,6},{6,4},{1,3},{3,1},{5,7},{7,5},{8,10},{10,8},{12,... | collective-permute-start | bytes 786440 | tf_op jit(solution)/shard_map/ppermute | solution.py:544
  70.7 8.5 %collective-permute-start.22 = (bf16[128,1024]{1,0:T(8,128)(2,1)S(1)}, bf16[128,1024]{1,0:T(8,128)(2,1)S(1)}, u32[]{:S(2)}, u32[]{:S(2)}) collective-permute-start(bf16[128,1024]{1,0:T(8,128)(2,1)S(1)} %add_term.17.refs_4_.refs_1_), channel_id=1, source_target_pairs={{0,8},{2,4},{4,2},{6,14},{8,0},{10,12},{12,10},{14,6},{16,24},{18,... | collective-permute-start | bytes 786440 | tf_op jit(solution)/shard_map/ppermute | solution.py:609
  71.2 12.0 %collective-permute-start.27 = (bf16[64,2048]{1,0:T(8,128)(2,1)S(1)}, bf16[64,2048]{1,0:T(8,128)(2,1)S(1)}, u32[]{:S(2)}, u32[]{:S(2)}) collective-permute-start(bf16[64,2048]{1,0:T(8,128)(2,1)S(1)} %pack_merged.8.refs_3_), channel_id=1, source_target_pairs={{0,25},{1,24},{8,17},{9,16},{16,9},{17,8},{24,1},{25,0},{2,27},{3,... | collective-permute-start | bytes 786440 | tf_op jit(solution)/shard_map/ppermute | solution.py:489
  71.2 14.0 %collective-permute-start.28 = (bf16[64,2048]{1,0:T(8,128)(2,1)S(1)}, bf16[64,2048]{1,0:T(8,128)(2,1)S(1)}, u32[]{:S(2)}, u32[]{:S(2)}) collective-permute-start(bf16[64,2048]{1,0:T(8,128)(2,1)S(1)} %pack_merged.9.refs_4_), channel_id=1, source_target_pairs={{0,24},{1,25},{8,16},{9,17},{16,8},{17,9},{24,0},{25,1},{2,26},{3,... | collective-permute-start | bytes 786440 | tf_op jit(solution)/shard_map/ppermute | solution.py:489
  73.7 11.5 %collective-permute-start.26 = (bf16[128,1024]{1,0:T(8,128)(2,1)S(1)}, bf16[128,1024]{1,0:T(8,128)(2,1)S(1)}, u32[]{:S(2)}, u32[]{:S(2)}) collective-permute-start(bf16[128,1024]{1,0:T(8,128)(2,1)S(1)} %get-tuple-element.75.refs_2_), channel_id=1, source_target_pairs={{0,2},{2,0},{4,6},{6,4},{1,3},{3,1},{5,7},{7,5},{8,10},{10,8},{12,... | collective-permute-start | bytes 786440 | tf_op jit(solution)/shard_map/ppermute | solution.py:544
  79.1 6.8 %collective-permute-start.25 = (bf16[128,1024]{1,0:T(8,128)(2,1)S(1)}, bf16[128,1024]{1,0:T(8,128)(2,1)S(1)}, u32[]{:S(2)}, u32[]{:S(2)}) collective-permute-start(bf16[128,1024]{1,0:T(8,128)(2,1)S(1)} %add_term.18.refs_4_.refs_1_), channel_id=1, source_target_pairs={{0,8},{2,4},{4,2},{6,14},{8,0},{10,12},{12,10},{14,6},{16,24},{18,... | collective-permute-start | bytes 786440 | tf_op jit(solution)/shard_map/ppermute | solution.py:609
  79.9 10.0 %collective-permute-start.32 = (bf16[128,1024]{1,0:T(8,128)(2,1)S(1)}, bf16[128,1024]{1,0:T(8,128)(2,1)S(1)}, u32[]{:S(2)}, u32[]{:S(2)}) collective-permute-start(bf16[128,1024]{1,0:T(8,128)(2,1)S(1)} %get-tuple-element.76.refs_2_), channel_id=1, source_target_pairs={{0,2},{2,0},{4,6},{6,4},{1,3},{3,1},{5,7},{7,5},{8,10},{10,8},{12,... | collective-permute-start | bytes 786440 | tf_op jit(solution)/shard_map/ppermute | solution.py:544
  83.3 10.4 %collective-permute-start.35 = (bf16[64,2048]{1,0:T(8,128)(2,1)S(1)}, bf16[64,2048]{1,0:T(8,128)(2,1)S(1)}, u32[]{:S(2)}, u32[]{:S(2)}) collective-permute-start(bf16[64,2048]{1,0:T(8,128)(2,1)S(1)} %pack_merged.10.refs_3_), channel_id=1, source_target_pairs={{0,17},{1,16},{8,25},{9,24},{16,1},{17,0},{24,9},{25,8},{2,19},{3,... | collective-permute-start | bytes 786440 | tf_op jit(solution)/shard_map/ppermute | solution.py:489
  85.3 8.7 %collective-permute-start.34 = (bf16[128,1024]{1,0:T(8,128)(2,1)S(1)}, bf16[128,1024]{1,0:T(8,128)(2,1)S(1)}, u32[]{:S(2)}, u32[]{:S(2)}) collective-permute-start(bf16[128,1024]{1,0:T(8,128)(2,1)S(1)} %add_term.19.refs_4_.refs_1_), channel_id=1, source_target_pairs={{0,8},{2,4},{4,2},{6,14},{8,0},{10,12},{12,10},{14,6},{16,24},{18,... | collective-permute-start | bytes 786440 | tf_op jit(solution)/shard_map/ppermute | solution.py:609
  86.0 12.6 %collective-permute-start.30 = (bf16[64,2048]{1,0:T(8,128)(2,1)S(1)}, bf16[64,2048]{1,0:T(8,128)(2,1)S(1)}, u32[]{:S(2)}, u32[]{:S(2)}) collective-permute-start(bf16[64,2048]{1,0:T(8,128)(2,1)S(1)} %pack_merged.11.refs_3_), channel_id=1, source_target_pairs={{0,16},{1,17},{8,24},{9,25},{16,0},{17,1},{24,8},{25,9},{2,18},{3,... | collective-permute-start | bytes 786440 | tf_op jit(solution)/shard_map/ppermute | solution.py:489
  87.4 11.3 %collective-permute-start.31 = (bf16[64,2048]{1,0:T(8,128)(2,1)S(1)}, bf16[64,2048]{1,0:T(8,128)(2,1)S(1)}, u32[]{:S(2)}, u32[]{:S(2)}) collective-permute-start(bf16[64,2048]{1,0:T(8,128)(2,1)S(1)} %pack_merged.12.refs_4_), channel_id=1, source_target_pairs={{0,9},{1,8},{8,1},{9,0},{16,25},{17,24},{24,17},{25,16},{2,11},{3,... | collective-permute-start | bytes 786440 | tf_op jit(solution)/shard_map/ppermute | solution.py:489
  89.9 9.2 %collective-permute-start.29 = (bf16[128,1024]{1,0:T(8,128)(2,1)S(1)}, bf16[128,1024]{1,0:T(8,128)(2,1)S(1)}, u32[]{:S(2)}, u32[]{:S(2)}) collective-permute-start(bf16[128,1024]{1,0:T(8,128)(2,1)S(1)} %get-tuple-element.77.refs_2_), channel_id=1, source_target_pairs={{0,2},{2,0},{4,6},{6,4},{1,3},{3,1},{5,7},{7,5},{8,10},{10,8},{12,... | collective-permute-start | bytes 786440 | tf_op jit(solution)/shard_map/ppermute | solution.py:544
  93.7 8.7 %collective-permute-start.37 = (bf16[64,2048]{1,0:T(8,128)(2,1)S(1)}, bf16[64,2048]{1,0:T(8,128)(2,1)S(1)}, u32[]{:S(2)}, u32[]{:S(2)}) collective-permute-start(bf16[64,2048]{1,0:T(8,128)(2,1)S(1)} %pack_merged.14.refs_3_), channel_id=1, source_target_pairs={{0,8},{1,9},{8,0},{9,1},{16,24},{17,25},{24,16},{25,17},{2,10},{3,... | collective-permute-start | bytes 786440 | tf_op jit(solution)/shard_map/ppermute | solution.py:489
  94.7 9.9 %collective-permute-start.36 = (bf16[128,1024]{1,0:T(8,128)(2,1)S(1)}, bf16[128,1024]{1,0:T(8,128)(2,1)S(1)}, u32[]{:S(2)}, u32[]{:S(2)}) collective-permute-start(bf16[128,1024]{1,0:T(8,128)(2,1)S(1)} %get-tuple-element.83), channel_id=1, source_target_pairs={{0,2},{2,0},{4,6},{6,4},{1,3},{3,1},{5,7},{7,5},{8,10},{10,8},{12,... | collective-permute-start | bytes 786440 | tf_op jit(solution)/shard_map/ppermute | solution.py:544
  98.6 6.1 %collective-permute-start.42 = (bf16[128,1024]{1,0:T(8,128)(2,1)S(1)}, bf16[128,1024]{1,0:T(8,128)(2,1)S(1)}, u32[]{:S(2)}, u32[]{:S(2)}) collective-permute-start(bf16[128,1024]{1,0:T(8,128)(2,1)S(1)} %add_term.21.refs_4_.refs_0_), channel_id=1, source_target_pairs={{0,8},{2,4},{4,2},{6,14},{8,0},{10,12},{12,10},{14,6},{16,24},{18,... | collective-permute-start | bytes 786440 | tf_op jit(solution)/shard_map/ppermute | solution.py:609
  99.2 5.6 %collective-permute-start.33 = (bf16[128,1024]{1,0:T(8,128)(2,1)S(1)}, bf16[128,1024]{1,0:T(8,128)(2,1)S(1)}, u32[]{:S(2)}, u32[]{:S(2)}) collective-permute-start(bf16[128,1024]{1,0:T(8,128)(2,1)S(1)} %add_term.20.refs_0_.refs_2_), channel_id=1, source_target_pairs={{0,8},{2,4},{4,2},{6,14},{8,0},{10,12},{12,10},{14,6},{16,24},{18,... | collective-permute-start | bytes 786440 | tf_op jit(solution)/shard_map/ppermute | solution.py:609
  99.3 14.8 %collective-permute-start.38 = (bf16[64,2048]{1,0:T(8,128)(2,1)S(1)}, bf16[64,2048]{1,0:T(8,128)(2,1)S(1)}, u32[]{:S(2)}, u32[]{:S(2)}) collective-permute-start(bf16[64,2048]{1,0:T(8,128)(2,1)S(1)} %pack_merged.13.refs_2_), channel_id=1, source_target_pairs={{0,1},{1,0},{8,9},{9,8},{16,17},{17,16},{24,25},{25,24},{2,3},{3,2... | collective-permute-start | bytes 786440 | tf_op jit(solution)/shard_map/ppermute | solution.py:489
  104.6 9.5 %copy-start.2 = (bf16[512,2048]{1,0:T(8,128)(2,1)S(1)}, bf16[512,2048]{1,0:T(8,128)(2,1)}, u32[]{:S(2)}) copy-start(bf16[512,2048]{1,0:T(8,128)(2,1)} %refs_2_.3) | copy-start | bytes 6291460
  104.6 11.7 %collective-permute-start.39 = (bf16[128,1024]{1,0:T(8,128)(2,1)S(1)}, bf16[128,1024]{1,0:T(8,128)(2,1)S(1)}, u32[]{:S(2)}, u32[]{:S(2)}) collective-permute-start(bf16[128,1024]{1,0:T(8,128)(2,1)S(1)} %add_term.22.refs_2_.refs_0_), channel_id=1, source_target_pairs={{0,8},{2,4},{4,2},{6,14},{8,0},{10,12},{12,10},{14,6},{16,24},{18,... | collective-permute-start | bytes 786440 | tf_op jit(solution)/shard_map/ppermute | solution.py:609
  104.9 16.7 %collective-permute-start.43 = (bf16[128,1024]{1,0:T(8,128)(2,1)S(1)}, bf16[128,1024]{1,0:T(8,128)(2,1)S(1)}, u32[]{:S(2)}, u32[]{:S(2)}) collective-permute-start(bf16[128,1024]{1,0:T(8,128)(2,1)S(1)} %add_term.25.refs_3_), channel_id=1, source_target_pairs={{0,2},{2,0},{4,6},{6,4},{1,3},{3,1},{5,7},{7,5},{8,10},{10,8},{12,... | collective-permute-start | bytes 786440 | tf_op jit(solution)/shard_map/ppermute | solution.py:544
  114.1 12.5 %collective-permute-start.41 = (bf16[128,1024]{1,0:T(8,128)(2,1)S(1)}, bf16[128,1024]{1,0:T(8,128)(2,1)S(1)}, u32[]{:S(2)}, u32[]{:S(2)}) collective-permute-start(bf16[128,1024]{1,0:T(8,128)(2,1)S(1)} %add_term.23.refs_2_.refs_11_.refs_3_), channel_id=1, source_target_pairs={{0,2},{2,0},{4,6},{6,4},{1,3},{3,1},{5,7},{7,5},{8,10},{10,8},{12,... | collective-permute-start | bytes 786440 | tf_op jit(solution)/shard_map/ppermute | solution.py:544
  116.3 1.6 %copy-start.1 = (bf16[512,2048]{1,0:T(8,128)(2,1)S(1)}, bf16[512,2048]{1,0:T(8,128)(2,1)}, u32[]{:S(2)}) copy-start(bf16[512,2048]{1,0:T(8,128)(2,1)} %place_rows.1.refs_2_) | copy-start | bytes 6291460
  118.0 11.8 %collective-permute-start.40 = (bf16[128,1024]{1,0:T(8,128)(2,1)S(1)}, bf16[128,1024]{1,0:T(8,128)(2,1)S(1)}, u32[]{:S(2)}, u32[]{:S(2)}) collective-permute-start(bf16[128,1024]{1,0:T(8,128)(2,1)S(1)} %add_term.24.refs_3_), channel_id=1, source_target_pairs={{0,2},{2,0},{4,6},{6,4},{1,3},{3,1},{5,7},{7,5},{8,10},{10,8},{12,... | collective-permute-start | bytes 786440 | tf_op jit(solution)/shard_map/ppermute | solution.py:544

commit v2 on v1

v2 whole, which is shorter than its diff:
```python
import functools
import math

import jax
import jax.numpy as jnp
from jax import lax
from jax.experimental import pallas as pl
from jax.experimental.pallas import tpu as pltpu
from jax.sharding import PartitionSpec as P

BF = jnp.bfloat16
F32 = jnp.float32
I32 = jnp.int32
GROUP_AXES = ("ctx", "grp")
VMEM = pl.BlockSpec(memory_space=pltpu.VMEM)
SMEM = pl.BlockSpec(memory_space=pltpu.SMEM)
ANY = pl.BlockSpec(memory_space=pl.ANY)
NODE = 800_000_000
TAKE = 3_200_000_000
PLACE = 6_400_000_000


def gelu_value(values):
    return 0.5 * values * (1.0 + lax.erf(values * 0.7071067811865476))


def gelu_slope(values):
    return (
        0.5 * (1.0 + lax.erf(values * 0.7071067811865476))
        + values * jnp.exp(-0.5 * values * values) * 0.3989422804014327
    )


def plain(pre_act, w_out, b_out, row_slot, ctx_slot, text_rows, cotangent):
    groups = lax.axis_size("ctx") * lax.axis_size("grp")
    slot_count = 2 * pre_act.shape[0]
    capacity = slot_count // groups
    width = w_out.shape[1]
    pre_float = pre_act.astype(F32)
    hidden = gelu_value(pre_float).astype(BF)
    merged = (jnp.dot(hidden, w_out, preferred_element_type=F32) + b_out.astype(F32)).astype(BF)
    outgoing = jnp.zeros((slot_count, width), BF).at[row_slot].set(merged)
    placed = ctx_slot >= 0
    returning = (
        jnp.zeros((slot_count, width), BF)
        .at[jnp.where(placed, ctx_slot, slot_count)]
        .set(cotangent, mode="drop")
    )

    def exchange(sent):
        blocks = sent.reshape(groups, capacity, width)
        return lax.all_to_all(
            blocks, GROUP_AXES, split_axis=0, concat_axis=0, tiled=True
        ).reshape(slot_count, width)

    arrived = exchange(outgoing)
    embeds = jnp.where(placed[:, None], arrived[jnp.where(placed, ctx_slot, 0)], text_rows)
    grad_rows = exchange(returning)[row_slot]
    partial_value = lax.dot_general(
        grad_rows, w_out, (((1,), (1,)), ((), ())), preferred_element_type=F32
    )
    summed = lax.psum(partial_value.astype(BF), "tp").astype(F32)
    grad_pre = (summed * gelu_slope(pre_float)).astype(BF)
    return embeds, grad_pre


def iota(shape, axis):
    return lax.broadcasted_iota(I32, shape, axis)


def as_column(row):
    n = row.shape[1]
    return jnp.sum(jnp.where(iota((n, n), 0) == iota((n, n), 1), row, 0), axis=1, keepdims=True)


def rank_in_block(row, shift):
    column = as_column(row)
    smaller = ((column >> shift) == (row >> shift)) & (column < row) & (column >= 0)
    return jnp.sum(smaller.astype(I32), axis=0, keepdims=True)


def arrival(row, shift, early):
    n = row.shape[1]
    rank = rank_in_block(row, shift)
    is_early = (rank < early).astype(I32)
    before = jnp.sum(
        jnp.where(iota((n, n), 0) < iota((n, n), 1), as_column(is_early), 0), axis=0, keepdims=True
    )
    index = iota((1, n), 1)
    place = jnp.where(is_early > 0, before, jnp.sum(is_early) + index - before)
    return rank, is_early, place


def call(kernel, name, out_shape, in_specs, out_specs, args, deps=(), limit=8, pins=None, flops=1000, **more):
    n = len(args)
    pins = pins or {}
    args = [
        pltpu.with_memory_space_constraint(arg, pins[i]) if i in pins else arg
        for i, arg in enumerate(args)
    ]
    deps = [
        pltpu.with_memory_space_constraint(dep, pltpu.HBM) if dep.size >= 1 << 20 else dep
        for dep in deps
    ]

    def body(*refs):
        kernel(*refs[:n], *refs[n + len(deps) :])

    return pl.pallas_call(
        body,
        out_shape=out_shape,
        in_specs=list(in_specs) + [ANY] * len(deps),
        out_specs=out_specs,
        cost_estimate=pl.CostEstimate(flops=flops, bytes_accessed=flops // 300, transcendentals=0),
        compiler_params=pltpu.CompilerParams(vmem_limit_bytes=limit << 20),
        name=name,
        **more,
    )(*args, *deps)


def full(shape):
    return pl.BlockSpec(shape, lambda *_: (0,) * len(shape))


def columns(rows, block):
    return pl.BlockSpec((rows, block), lambda i: (0, i))


def as_hot(mask):
    return jnp.where(mask, 1.0, 0.0).astype(BF)


def place_of(offset, pair):
    return ((offset & ~(2 * pair - 1)) >> 1) | (offset & (pair - 1))


def goes_to(offset, pair):
    return place_of(offset, pair) * 2 + jnp.where((offset & pair) > 0, 1, 0)


def came_from(offset, pair, groups):
    return place_of(offset, pair) + jnp.where((offset & pair) > 0, groups // 2, 0)


def pack_context(me, inner, slots, cotangent, low, high, shift, groups, pair):
    tokens, width = cotangent.shape
    count = high - low
    spans = [slice(start, start + 512) for start in range(0, width, 512)]
    parts = groups // 2
    height = 2 * count

    def kernel(me_ref, inner_ref, slot_ref, rows_ref, *refs):
        outs, held_ref, here_ref, sems = refs[:parts], *refs[parts:]
        slots_copy = pltpu.make_async_copy(slot_ref, here_ref, sems.at[0])
        copy = pltpu.make_async_copy(rows_ref, held_ref, sems.at[1])
        slots_copy.start()
        copy.start()
        slots_copy.wait()
        row = here_ref[...]
        rank = rank_in_block(row, shift)
        used = (row >= 0) & (rank >= low) & (rank < high)
        wire = goes_to((row >> shift) ^ me_ref[0], pair) * count + rank - low
        hot = as_hot(iota((groups * count, tokens), 0) == jnp.where(used, wire, -1))
        copy.wait()
        for span in spans:
            packed = jnp.dot(hot, held_ref[:, span], preferred_element_type=F32).astype(BF)
            for k, out in enumerate(outs):
                out[:, span] = packed[k * height : (k + 1) * height]

    *outs, held = call(
        kernel,
        "pack_context",
        [pltpu.VMEM((height, width), BF)] * parts + [pltpu.VMEM((tokens, width), BF)],
        [SMEM, SMEM, ANY, ANY],
        [VMEM] * (parts + 1),
        (me, inner, slots, cotangent),
        pins={2: pltpu.HBM, 3: pltpu.HBM},
        scratch_shapes=[pltpu.VMEM((1, tokens), I32), pltpu.SemaphoreType.DMA((2,))],
    )
    return outs, held


def split_rows(hot, rows, deps=()):
    height = hot.shape[0] // 2

    def kernel(hot_ref, rows_ref, stay_ref, swap_ref):
        dot_columns(hot_ref[:height], rows_ref, stay_ref)
        dot_columns(hot_ref[height:], rows_ref, swap_ref)

    return call(
        kernel,
        "split_rows",
        [pltpu.VMEM((height, rows.shape[1]), BF)] * 2,
        [VMEM, VMEM],
        [VMEM] * 2,
        (hot, rows),
        deps,
    )


def join(stay, got, index, height, deps=()):
    span = slice(index * height, (index + 1) * height)

    def kernel(stay_ref, got_ref, out_ref):
        out_ref[:height] = stay_ref[span]
        out_ref[height:] = got_ref[span]

    return call(
        kernel,
        "join",
        pltpu.VMEM((2 * height, stay.shape[1]), BF),
        [VMEM, VMEM],
        VMEM,
        (stay, got),
        deps,
    )


def relay(pieces, deps=()):
    height, width = pieces[0].shape
    half = height // 2

    def kernel(*refs):
        for i, piece in enumerate(refs[:-1]):
            refs[-1][i * half : (i + 1) * half] = piece[half:]

    return call(
        kernel,
        "relay",
        pltpu.VMEM((len(pieces) * half, width), BF),
        [VMEM] * len(pieces),
        VMEM,
        pieces,
        deps,
    )


def gelu_product(pre_ref, w_ref, slope_ref, total_ref, first, waits):
    block = 512
    for i, wait in enumerate(waits):
        span = slice(i * block, (i + 1) * block)
        values = pre_ref[:, span].astype(F32)
        share = 0.5 * (1.0 + lax.erf(values * 0.7071067811865476))
        slope = share + values * jnp.exp(-0.5 * values * values) * 0.3989422804014327
        slope_ref[:, span] = slope.astype(BF)
        wait()
        term = jnp.dot(
            (values * share).astype(BF),
            w_ref[first + i * block : first + (i + 1) * block],
            preferred_element_type=F32,
        )
        if first + i == 0:
            total_ref[...] = term
        else:
            total_ref[...] += term


def prepare(me, row_slots, ctx_slots, early, shift, groups, pair, pre_act, w_out, cut, deps=()):
    n, depth = pre_act.shape
    width = w_out.shape[1]
    tokens = ctx_slots.shape[1]
    late = (1 << shift) - early
    half = n * early >> shift
    spans = [slice(start, start + 512) for start in range(0, depth, 512)]

    def kernel(me_ref, row_hbm, ctx_hbm, pre_hbm, w_hbm, *refs):
        early_ref, late_ref, w_ref, product_ref, slope_hbm = refs[:5]
        row_ref, ctx_ref, pre_ref, slope_ref, sems = refs[5:]
        small = [
            pltpu.make_async_copy(row_hbm, row_ref, sems.at[len(spans)]),
            pltpu.make_async_copy(ctx_hbm, ctx_ref, sems.at[len(spans) + 1]),
        ]
        values_copy = pltpu.make_async_copy(
            pre_hbm.at[:, 0:cut], pre_ref, sems.at[len(spans) + 2]
        )
        slope_copy = pltpu.make_async_copy(slope_ref, slope_hbm, sems.at[len(spans) + 3])
        copies = [
            pltpu.make_async_copy(w_hbm.at[span], w_ref.at[span], sems.at[i])
            for i, span in enumerate(spans)
        ]
        for copy in [*small, values_copy, *copies]:
            copy.start()
        for copy in small:
            copy.wait()
        row = row_ref[...]
        offset = (row >> shift) ^ me_ref[0]
        rank, is_early, place = arrival(row, shift, early)
        wire = came_from(offset, pair, groups) * early + rank
        order = iota((half, n), 0) == place
        source = jnp.sum(jnp.where(order, wire, 0), axis=1, keepdims=True)
        early_ref[...] = as_hot(iota((half, groups * early), 1) == source)
        ctx = ctx_ref[...]
        offset = (ctx >> shift) ^ me_ref[0]
        rank = rank_in_block(ctx, shift)
        target = came_from(offset, pair, groups) * late + rank - early
        target = jnp.where((ctx >= 0) & (rank >= early), target, -1)
        late_ref[...] = as_hot(iota((groups * late, tokens), 0) == target)
        values_copy.wait()
        used = cut // 512
        waits = [copy.wait for copy in copies[:used]]
        gelu_product(pre_ref, w_ref, slope_ref, product_ref, 0, waits)
        slope_copy.start()
        for copy in copies[used:]:
            copy.wait()
        slope_copy.wait()

    shapes = [(half, groups * early), (groups * late, tokens), (depth, width)]
    return call(
        kernel,
        "prepare",
        [pltpu.VMEM(shape, BF) for shape in shapes]
        + [pltpu.VMEM((n, width), F32), pltpu.HBM((n, cut), BF)],
        [SMEM] + [ANY] * 4,
        [VMEM] * 4 + [ANY],
        (me, row_slots, ctx_slots, pre_act, w_out),
        deps,
        limit=10,
        pins={i: pltpu.HBM for i in range(1, 5)},
        flops=4 * n * depth * width,
        scratch_shapes=[
            pltpu.VMEM((1, n), I32),
            pltpu.VMEM((1, tokens), I32),
            pltpu.VMEM((n, cut), BF),
            pltpu.VMEM((n, cut), BF),
            pltpu.SemaphoreType.DMA((len(spans) + 4,)),
        ],
    )


def prepare_more(
    me, row_slots, ctx_slots, early, shift, groups, pair, pre_act, w_here, product, cut, deps=()
):
    n, depth = pre_act.shape
    width = w_here.shape[1]
    tokens = ctx_slots.shape[1]
    capacity = 1 << shift
    late = capacity - early
    wires = groups * capacity

    def kernel(me_ref, row_hbm, ctx_hbm, pre_hbm, w_ref, part_ref, *refs):
        all_ref, back_ref, merged_ref, place_ref, product_ref, slope_hbm = refs[:6]
        row_ref, ctx_ref, pre_ref, slope_ref, sems = refs[6:]
        small = [
            pltpu.make_async_copy(row_hbm, row_ref, sems.at[0]),
            pltpu.make_async_copy(ctx_hbm, ctx_ref, sems.at[1]),
        ]
        values_copy = pltpu.make_async_copy(pre_hbm.at[:, cut:depth], pre_ref, sems.at[2])
        slope_copy = pltpu.make_async_copy(slope_ref, slope_hbm, sems.at[3])
        for copy in [*small, values_copy]:
            copy.start()
        for copy in small:
            copy.wait()
        row = row_ref[...]
        offset = (row >> shift) ^ me_ref[0]
        rank, is_early, place = arrival(row, shift, early)
        wire = jnp.where(
            is_early > 0,
            came_from(offset, pair, groups) * early + rank,
            groups * early + goes_to(offset, pair) * late + rank - early,
        )
        order = iota((n, n), 0) == place
        source = jnp.sum(jnp.where(order, wire, 0), axis=1, keepdims=True)
        all_ref[...] = as_hot(iota((n, wires), 1) == source)
        back_ref[...] = as_hot(iota((n, n), 1) == as_column(place))
        target = (came_from(offset, pair, groups) << shift) + (row & (capacity - 1))
        merged_ref[...] = as_hot(iota((wires, n), 0) == target)
        ctx = ctx_ref[...]
        offset = (ctx >> shift) ^ me_ref[0]
        source = (goes_to(offset, pair) << shift) + (ctx & (capacity - 1))
        source = as_column(jnp.where(ctx >= 0, source, -1))
        place_ref[...] = as_hot(iota((tokens, wires), 1) == source)
        values_copy.wait()
        product_ref[...] = part_ref[...]
        waits = [lambda: None] * ((depth - cut) // 512)
        gelu_product(pre_ref, w_ref, slope_ref, product_ref, cut, waits)
        slope_copy.start()
        slope_copy.wait()

    shapes = [(n, wires), (n, n), (wires, n), (tokens, wires)]
    return call(
        kernel,
        "prepare_more",
        [pltpu.VMEM(shape, BF) for shape in shapes]
        + [pltpu.VMEM((n, width), F32), pltpu.HBM((n, depth - cut), BF)],
        [SMEM] + [ANY] * 3 + [VMEM] * 2,
        [VMEM] * 5 + [ANY],
        (me, row_slots, ctx_slots, pre_act, w_here, product),
        deps,
        pins={1: pltpu.HBM, 2: pltpu.HBM, 3: pltpu.HBM, 4: pltpu.VMEM},
        scratch_shapes=[
            pltpu.VMEM((1, n), I32),
            pltpu.VMEM((1, tokens), I32),
            pltpu.VMEM((n, depth - cut), BF),
            pltpu.VMEM((n, depth - cut), BF),
            pltpu.SemaphoreType.DMA((4,)),
        ],
    )


def dot_columns(hot, rows_ref, out_ref, block=512):
    for start in range(0, out_ref.shape[1], block):
        span = slice(start, start + block)
        out_ref[:, span] = jnp.dot(
            hot, rows_ref[:, span], preferred_element_type=F32
        ).astype(BF)


def gather(wire_ref, refs, spans):
    start = 0
    for ref, span in zip(refs, spans):
        height = span.stop - span.start
        wire_ref[start : start + height] = ref[span]
        start += height


def take_rows(hot, pieces, deps=()):
    arrays, spans = zip(*pieces)
    width = arrays[0].shape[1]

    def kernel(hot_ref, *refs):
        ins, out_ref, wire_ref = refs[:-2], refs[-2], refs[-1]
        gather(wire_ref, ins, spans)
        dot_columns(hot_ref[...], wire_ref, out_ref)

    return call(
        kernel,
        "take_rows",
        pltpu.VMEM((hot.shape[0], width), BF),
        [VMEM] * (1 + len(arrays)),
        VMEM,
        (hot, *arrays),
        deps,
        flops=TAKE,
        scratch_shapes=[pltpu.VMEM((hot.shape[1], width), BF)],
    )


def back_product(rows, w_rows, span, first, last, deps=()):
    def kernel(rows_ref, w_ref, out_ref):
        out_ref[...] = lax.dot_general(
            rows_ref[span],
            w_ref[first:last],
            (((1,), (1,)), ((), ())),
            preferred_element_type=F32,
        ).astype(BF)

    return call(
        kernel,
        "back_product",
        pltpu.VMEM((span.stop - span.start, last - first), BF),
        [VMEM, VMEM],
        VMEM,
        (rows, w_rows),
        deps,
        pins={1: pltpu.VMEM},
    )


def round_merged(product, bias, deps=()):
    def kernel(product_ref, bias_ref, out_ref):
        out_ref[...] = (product_ref[...] + bias_ref[...].astype(F32)).astype(BF)

    return call(
        kernel,
        "round_merged",
        pltpu.VMEM(product.shape, BF),
        [VMEM, VMEM],
        VMEM,
        (product, bias),
        deps,
    )


def place_rows(slots, hot, pieces, text, deps=()):
    tokens, width = text.shape
    block = 512
    total = hot.shape[1]
    arrays, parts = zip(*pieces)
    spans = [slice(start, start + block) for start in range(0, width, block)]

    def kernel(slot_ref, hot_ref, text_ref, *refs):
        ins, out_ref, wire_ref, done_ref, sems = refs[:-4], *refs[-4:]
        used = as_column((slot_ref[...] >= 0).astype(I32))
        gather(wire_ref, ins, parts)
        copies = []
        for i, span in enumerate(spans):
            rows = jnp.dot(hot_ref[...], wire_ref[:, span], preferred_element_type=F32)
            done_ref[:, span] = jnp.where(
                used > 0, rows, text_ref[:, span].astype(F32)
            ).astype(BF)
            copies.append(
                pltpu.make_async_copy(done_ref.at[:, span], out_ref.at[:, span], sems.at[i])
            )
            copies[-1].start()
        for copy in copies:
            copy.wait()

    return call(
        kernel,
        "place_rows",
        pltpu.HBM((tokens, width), BF),
        [VMEM] * (3 + len(arrays)),
        ANY,
        (slots, hot, text, *arrays),
        deps,
        limit=12,
        flops=PLACE,
        scratch_shapes=[
            pltpu.VMEM((total, width), BF),
            pltpu.VMEM((tokens, width), BF),
            pltpu.SemaphoreType.DMA((len(spans),)),
        ],
    )


def add_term(own, other, deps=(), weight=1):
    def kernel(a_ref, b_ref, out_ref):
        out_ref[...] = (a_ref[...].astype(F32) + b_ref[...].astype(F32)).astype(BF)

    shape = pltpu.VMEM(own.shape, BF)
    return call(
        kernel, "add_term", shape, [VMEM, VMEM], VMEM, (own, other), deps, limit=4, flops=weight * NODE
    )


def add_and_choose(inner, own, other, term, deps=()):
    def kernel(inner_ref, a_ref, b_ref, term_ref, sum_ref, next_ref):
        total = (a_ref[...].astype(F32) + b_ref[...].astype(F32)).astype(BF)
        sum_ref[...] = total
        next_ref[...] = jnp.where(
            inner_ref[0] > 0, total.astype(F32), term_ref[...].astype(F32)
        ).astype(BF)

    shape = pltpu.VMEM(own.shape, BF)
    return call(
        kernel,
        "add_and_choose",
        (shape, shape),
        [SMEM, VMEM, VMEM, VMEM],
        (VMEM, VMEM),
        (inner, own, other, term),
        deps,
        limit=4,
        flops=NODE,
    )


def finish(inner, hot, sums, slope, start_at, depth, so_far, first, width, deps=()):
    n = hot.shape[0]
    flat = [array for pair in sums for array in pair]

    def kernel(inner_ref, hot_ref, slope_ref, *refs):
        ins = refs[: len(flat)]
        out_ref, rows_ref, done_ref, sem = refs[-4:]
        start = 0
        for held, came in zip(ins[::2], ins[1::2]):
            block = jnp.where(
                inner_ref[0] > 0, held[...].astype(F32), came[...].astype(F32)
            ).astype(BF)
            height = held.shape[0]
            for i in range(held.shape[1] // width):
                rows_ref[start : start + height] = block[:, i * width : (i + 1) * width]
                start += height
        total = jnp.dot(hot_ref[...], rows_ref[...], preferred_element_type=F32)
        slopes = slope_ref[:, first - start_at : first - start_at + width]
        done_ref[...] = (total * slopes.astype(F32)).astype(BF)
        copy = pltpu.make_async_copy(done_ref, out_ref.at[:, first : first + width], sem)
        copy.start()
        copy.wait()

    args = (inner, hot, slope, *flat)
    in_specs = [SMEM] + [VMEM] * (2 + len(flat))
    aliases, pins = {}, {}
    if so_far is not None:
        aliases = {len(args): 0}
        pins = {len(args): pltpu.HBM}
        args += (so_far,)
        in_specs.append(ANY)
    return call(
        kernel,
        "finish",
        pltpu.HBM((n, depth), BF),
        in_specs,
        ANY,
        args,
        deps,
        pins=pins,
        scratch_shapes=[
            pltpu.VMEM((n, width), BF),
            pltpu.VMEM((n, width), BF),
            pltpu.SemaphoreType.DMA,
        ],
        input_output_aliases=aliases,
    )


def pipelined(pre_act, w_out, b_out, row_slot, ctx_slot, text_rows, cotangent):
    ctx_size, grp_size, tp_size = (lax.axis_size(name) for name in ("ctx", "grp", "tp"))
    groups = ctx_size * grp_size
    rows, depth = pre_act.shape
    width = w_out.shape[1]
    tokens = ctx_slot.shape[0]
    capacity = 2 * rows // groups
    shift = capacity.bit_length() - 1
    me = (lax.axis_index("ctx") * grp_size + lax.axis_index("grp")).reshape(1)
    tp_index = lax.axis_index("tp")
    inner = ((tp_index == 1) | (tp_index == 2)).astype(I32).reshape(1)
    row_slots = row_slot.reshape(1, rows)
    ctx_slots = ctx_slot.reshape(1, tokens)

    pair = grp_size

    def exchange(k, piece):
        return lax.ppermute(piece, GROUP_AXES, [(i, i ^ k) for i in range(groups)])

    def whole(array):
        return array, slice(0, array.shape[0])

    def exchange_pair(i, sent):
        return exchange((i // pair) * 2 * pair + i % pair, sent)

    def exchange_pairs(sent):
        return [sent[0]] + [exchange_pair(i, sent[i]) for i in range(1, len(sent))]

    def relayed(came, deps=()):
        half = came[0].shape[0] // 2
        last = exchange(pair, relay(came, deps))
        return [(array, slice(0, half)) for array in came] + [whole(last)]

    early = capacity // 2
    late = capacity - early
    early_rows = rows // 2
    per_part = 5
    size = depth // per_part
    chunks = 2 * per_part
    half = groups // 2

    bias = b_out.reshape(1, width)
    first_out, held = pack_context(
        me, inner, ctx_slots, cotangent, 0, early, shift, groups, pair
    )
    first_in = exchange_pairs(first_out)
    cut = 3 * size
    hot_early, hot_late, w_here, forward, slope_low = prepare(
        me, row_slots, ctx_slots, early, shift, groups, pair, pre_act, w_out, cut, (first_out[1],)
    )

    def exchange_in_turn(hot, sent, height, deps):
        stay, swap = split_rows(hot, sent, deps)
        got = exchange(pair, swap)
        came = [(stay, slice(0, height)), (got, slice(0, height))]
        offsets = [(i // pair) * 2 * pair + i % pair for i in range(1, half)]
        blocks = {}
        for straight in (True, False):
            after = tuple(blocks.values())
            for i, offset in enumerate(offsets, 1):
                if (offset & (offset - 1) == 0) == straight:
                    blocks[i] = exchange(offset, join(stay, got, i, height, after))
        return came + [whole(blocks[i]) for i in range(1, half)]

    def product(j, deps=()):
        span = slice(0, early_rows) if j < per_part else slice(early_rows, rows)
        first = j % per_part * size
        return back_product(grads, w_here, span, first, first + size, deps)

    first_in = relayed(first_in, (forward,))
    grads = take_rows(hot_early, first_in)
    terms = {0: product(0)}
    terms[1] = product(1, (terms[0],))
    second_in = exchange_in_turn(hot_late, held, late, (terms[1],))
    outer_pairs = [(0, 1), (1, 0), (2, 3), (3, 2)]
    inner_pairs = [
        (c * tp_size + t, c * tp_size + 3 - t if t in (1, 2) else (c ^ 1) * tp_size + t)
        for c in range(ctx_size)
        for t in range(tp_size)
    ]
    from_pair, from_far, halves, totals, send = {}, {}, {}, {}, {}

    def to_pair(j, value):
        from_pair[j] = lax.ppermute(value, "tp", outer_pairs)

    def finish_block(k, so_far, *deps):
        sums = [(totals[i], from_pair[i + 3]) for i in (k, k + per_part)]
        slope, start_at = (slope_low, 0) if k * size < cut else (slope_high, cut)
        return finish(
            inner, hot_back, sums, slope, start_at, depth, so_far, k * size, size, deps
        )

    to_pair(0, terms[0])
    to_pair(1, terms[1])
    grad_pre = None
    for j in range(chunks):
        after = []
        ahead = j + 2
        if j == 1:
            hot_all, hot_back, hot_merged, hot_place, forward, slope_high = prepare_more(
                me,
                row_slots,
                ctx_slots,
                early,
                shift,
                groups,
                pair,
                pre_act,
                w_here,
                forward,
                cut,
                (halves[j - 1] if j else terms[2],),
            )
            after.append(hot_all)
        if ahead < chunks:
            previous = (send[j + 1],) if j >= 3 else (terms[j + 1],)
            if ahead == per_part:
                grads = take_rows(hot_all, first_in + second_in, previous)
            terms[ahead] = product(ahead, previous)
            if ahead != per_part:
                after.append(terms[ahead])
        if j == 4:
            merged = round_merged(forward, bias, (halves[j - 1],))
            arrived = exchange_in_turn(hot_merged, merged, capacity, (halves[j - 1],))
        if j == chunks - 1:
            grad_pre = finish_block(0, None, halves[j - 1])
            after.append(grad_pre)
        halves[j] = add_term(terms[j], from_pair[j], tuple(after))
        from_far[j] = lax.ppermute(halves[j], ("ctx", "tp"), inner_pairs)
        if j == 0:
            value, _ = lax.optimization_barrier((terms[2], halves[0]))
            to_pair(2, value)
        elif ahead < chunks:
            for k in {1: (), 2: (1, 2)}.get(j, (j,)):
                totals[k - 1], send[k + 2] = add_and_choose(
                    inner, halves[k - 1], from_far[k - 1], terms[k + 2], (halves[j],)
                )
                to_pair(k + 2, send[k + 2])
        else:
            totals[j - 1] = add_term(halves[j - 1], from_far[j - 1], (halves[j],))
            to_pair(ahead, totals[j - 1])
    grad_pre = finish_block(1, grad_pre, totals[chunks - 2])
    totals[chunks - 1] = add_term(halves[chunks - 1], from_far[chunks - 1], (grad_pre,))
    to_pair(chunks + 2, totals[chunks - 1])
    embeds = place_rows(ctx_slots, hot_place, arrived, text_rows, (totals[chunks - 1],))
    for k in range(2, per_part):
        grad_pre = finish_block(k, grad_pre, *([embeds] if k == 3 else []))
    return embeds, grad_pre


def shards(pre_act, w_out, b_out, row_slot, ctx_slot, text_rows, cotangent):
    groups = lax.axis_size("ctx") * lax.axis_size("grp")
    rows, depth = pre_act.shape
    width = w_out.shape[1]
    capacity = 2 * rows // groups
    power = lambda value: value & (value - 1) == 0
    fits = (
        lax.axis_size("tp") == 4
        and lax.axis_size("ctx") % 2 == 0
        and 4 <= groups <= 8
        and power(groups)
        and power(capacity)
        and capacity % 32 == 0
        and rows % 256 == 0
        and ctx_slot.shape[0] % 128 == 0
        and depth % 5120 == 0
        and width % 512 == 0
    )
    plan = pipelined if fits else plain
    return plan(pre_act, w_out, b_out, row_slot, ctx_slot, text_rows, cotangent)


def solution(mesh):
    in_specs = (
        P(("ctx", "grp"), None),
        P(None, "tp"),
        P("tp"),
        P(("ctx", "grp")),
        P(("ctx", "grp")),
        P(("ctx", "grp"), "tp"),
        P(("ctx", "grp"), "tp"),
    )
    out_specs = (P(("ctx", "grp"), "tp"), P(("ctx", "grp"), None))
    return jax.shard_map(shards, mesh=mesh, in_specs=in_specs, out_specs=out_specs, check_vma=False)
```

time: 132 us -> 115 us (0.87)
  Pallas kernels: 50.2 us -> 42.5 us
  starting transfers between devices: 57.3 us -> 49.8 us
    pallas_call x53 -> x51, Pallas kernels: 50.2 us -> 42.5 us  [call(): pl.pallas_call(body, out_shape=out_shape, in_specs=list(in_specs) + [ANY]...]
    ppermute x21 -> x12, starting transfers between devices: 19.9 us -> 13 us  [exchange(): return lax.ppermute(piece, GROUP_AXES, [(i, i ^ k) for i in range(groups)])]
    ppermute x21 -> x12, waiting for transfers between devices: 7.03 us -> 10.6 us  [exchange(): return lax.ppermute(piece, GROUP_AXES, [(i, i ^ k) for i in range(groups)])]
    ppermute x13, waiting for transfers between devices: 13 us -> 9.49 us  [to_pair(): from_pair[j] = lax.ppermute(value, 'tp', outer_pairs)]
  transfers between devices with their start and end apart: 44 -> 35, of which waited for: 12 -> 10; matrix products, arithmetic and copies ran while one was open for 1% -> 0% of each run, Pallas kernels for 33% -> 32%
where the time goes in v2:
time: 115 us
  starting transfers between devices  49.8 us (43%)
  Pallas kernels  42.5 us (37%)
  waiting for transfers between devices  20.1 us (17%)
  between operations  1.4 us (1%)
  local copies, waits for them, and re-layouts  1.17 us (1%)
    pallas_call x51, Pallas kernels, call(): pl.pallas_call(body, out_shape=out_shape, in_specs=list(in_specs) + [ANY]...  42.5 us
    ppermute x13, starting transfers between devices, to_pair(): from_pair[j] = lax.ppermute(value, 'tp', outer_pairs)  35.8 us
    ppermute x12, starting transfers between devices, exchange(): return lax.ppermute(piece, GROUP_AXES, [(i, i ^ k) for i in range(groups)])  13 us
    ppermute x12, waiting for transfers between devices, exchange(): return lax.ppermute(piece, GROUP_AXES, [(i, i ^ k) for i in range(groups)])  10.6 us
    ppermute x13, waiting for transfers between devices, to_pair(): from_pair[j] = lax.ppermute(value, 'tp', outer_pairs)  9.49 us
  transfers between devices with their start and end apart: 35, of which 10 were waited for; matrix products, arithmetic and copies ran while one was open for 0% of the time, Pallas kernels for 32%

profile of v2, /device:TPU:0, one launch (start us, length us, event | category | flops | bytes accessed | tf_op | source)
XLA Modules:
  0.0 114.9 jit_solution(10169882973544837831)
XLA Ops:
  0.6 2.3 %pack_context.1 = (bf16[64,2048]{1,0:T(8,128)(2,1)S(1)}, bf16[64,2048]{1,0:T(8,128)(2,1)S(1)}, bf16[64,2048]{1,0:T(8,128)(2,1)S(1)}, bf16[64,2048]{1,0:T(8,128)(2,1)S(1)}, bf16[512,2048]{1,0:T(8,128)(2,1)S(1)}) custom-call(s32[1]{0:T(128)} %bitcast.1.refs_0_, s32[1]{0:T(128)} %bitcast.3.refs_1_.refs_0_, s32[1,512]{1,0:T(1,128)} %bitcast.4, ...), custom_call_target="tpu_custom_call" | custom-call | flops 1000 | bytes 3 | tf_op jit(solution)/shard_map/pack_context/pallas_call | solution.py:109
  3.0 3.0 %collective-permute-start = (bf16[64,2048]{1,0:T(8,128)(2,1)S(1)}, bf16[64,2048]{1,0:T(8,128)(2,1)S(1)}, u32[]{:S(2)}, u32[]{:S(2)}) collective-permute-start(bf16[64,2048]{1,0:T(8,128)(2,1)S(1)} %get-tuple-element.37.refs_5_), channel_id=1, source_target_pairs={{0,1},{1,0},{8,9},{9,8},{16,17},{17,16},{24,25},{25,24},{2,3},{3,2... | collective-permute-start | bytes 786440 | tf_op jit(solution)/shard_map/ppermute | solution.py:614
  6.0 1.5 %collective-permute-start.1 = (bf16[64,2048]{1,0:T(8,128)(2,1)S(1)}, bf16[64,2048]{1,0:T(8,128)(2,1)S(1)}, u32[]{:S(2)}, u32[]{:S(2)}) collective-permute-start(bf16[64,2048]{1,0:T(8,128)(2,1)S(1)} %get-tuple-element.42), channel_id=1, source_target_pairs={{0,16},{1,17},{8,24},{9,25},{16,0},{17,1},{24,8},{25,9},{2,18},{3,... | collective-permute-start | bytes 786440 | tf_op jit(solution)/shard_map/ppermute | solution.py:614
  7.6 8.1 %prepare.1 = (bf16[128,256]{1,0:T(8,128)(2,1)S(1)}, bf16[256,512]{1,0:T(8,128)(2,1)S(1)}, bf16[5120,2048]{1,0:T(8,128)(2,1)S(1)}, f32[256,2048]{1,0:T(8,128)S(1)}, bf16[256,3072]{1,0:T(8,128)(2,1)}) custom-call(s32[1]{0:T(128)} %bitcast.1.refs_0_, s32[1,256]{1,0:T(1,128)} %bitcast.8, s32[1,512]{1,0:T(1,128)} %bitcast.5, bf16[256,5120]{1,0:T(8,128)(2,1)} %refs_3_.5, ...), custom_call_target="tpu_custom_call" | custom-call | flops 10737418240 | bytes 35791392 | tf_op jit(solution)/shard_map/prepare/pallas_call | solution.py:109
  15.7 3.5 %collective-permute-done.2.refs_3_.refs_4_ = bf16[64,2048]{1,0:T(8,128)(2,1)S(1)} collective-permute-done((bf16[64,2048]{1,0:T(8,128)(2,1)S(1)}, bf16[64,2048]{1,0:T(8,128)(2,1)S(1)}, u32[]{:S(2)}, u32[]{:S(2)}) %collective-permute-start.2) | collective-permute-done | bytes 262176 | tf_op jit(solution)/shard_map/ppermute | solution.py:614
  19.3 1.9 %collective-permute-done.3.refs_5_ = bf16[128,2048]{1,0:T(8,128)(2,1)S(1)} collective-permute-done((bf16[128,2048]{1,0:T(8,128)(2,1)S(1)}, bf16[128,2048]{1,0:T(8,128)(2,1)S(1)}, u32[]{:S(2)}, u32[]{:S(2)}) %collective-permute-start.3) | collective-permute-done | bytes 524320 | tf_op jit(solution)/shard_map/ppermute | solution.py:614
  21.2 0.3 take_rows.2.refs_0_
  21.5 1.5 %back_product.10.refs_2_.refs_0_ = bf16[128,1024]{1,0:T(8,128)(2,1)S(1)} custom-call(bf16[128,2048]{1,0:T(8,128)(2,1)S(1)} %take_rows.2.refs_0_, bf16[5120,2048]{1,0:T(8,128)(2,1)S(1)} %get-tuple-element.38.refs_1_.refs_4_), custom_call_target="tpu_custom_call" | custom-call | flops 1000 | bytes 3 | tf_op jit(solution)/shard_map/back_product/pallas_call | solution.py:109
  23.0 1.8 %collective-permute-start.4 = (bf16[128,1024]{1,0:T(8,128)(2,1)S(1)}, bf16[128,1024]{1,0:T(8,128)(2,1)S(1)}, u32[]{:S(2)}, u32[]{:S(2)}) collective-permute-start(bf16[128,1024]{1,0:T(8,128)(2,1)S(1)} %back_product.10.refs_2_.refs_0_), channel_id=1, source_target_pairs={{0,2},{2,0},{4,6},{6,4},{1,3},{3,1},{5,7},{7,5},{8,10},{10,8},{12,... | collective-permute-start | bytes 786440 | tf_op jit(solution)/shard_map/ppermute | solution.py:680
  24.8 1.5 %back_product.11.refs_2_.refs_0_ = bf16[128,1024]{1,0:T(8,128)(2,1)S(1)} custom-call(bf16[128,2048]{1,0:T(8,128)(2,1)S(1)} %take_rows.2.refs_0_, bf16[5120,2048]{1,0:T(8,128)(2,1)S(1)} %get-tuple-element.38.refs_1_.refs_4_, bf16[128,1024]{1,0:T(8,128)(2,1)S(1)} %back_product.10.refs_2_.refs_0_), custom_call_target="tpu_custom_call" | custom-call | flops 1000 | bytes 3 | tf_op jit(solution)/shard_map/back_product/pallas_call | solution.py:109
  26.3 0.8 split_rows.3
  27.2 1.5 %back_product.12.refs_2_.refs_0_ = bf16[128,1024]{1,0:T(8,128)(2,1)S(1)} custom-call(bf16[128,2048]{1,0:T(8,128)(2,1)S(1)} %take_rows.2.refs_0_, bf16[5120,2048]{1,0:T(8,128)(2,1)S(1)} %get-tuple-element.38.refs_1_.refs_4_, bf16[128,1024]{1,0:T(8,128)(2,1)S(1)} %back_product.11.refs_2_.refs_0_), custom_call_target="tpu_custom_call" | custom-call | flops 1000 | bytes 3 | tf_op jit(solution)/shard_map/back_product/pallas_call | solution.py:109
  28.7 2.7 %collective-permute-done.4.refs_1_ = bf16[128,1024]{1,0:T(8,128)(2,1)S(1)} collective-permute-done((bf16[128,1024]{1,0:T(8,128)(2,1)S(1)}, bf16[128,1024]{1,0:T(8,128)(2,1)S(1)}, u32[]{:S(2)}, u32[]{:S(2)}) %collective-permute-start.4) | collective-permute-done | bytes 262176 | tf_op jit(solution)/shard_map/ppermute | solution.py:680
  31.5 1.8 %collective-permute-start.6 = (bf16[128,1024]{1,0:T(8,128)(2,1)S(1)}, bf16[128,1024]{1,0:T(8,128)(2,1)S(1)}, u32[]{:S(2)}, u32[]{:S(2)}) collective-permute-start(bf16[128,1024]{1,0:T(8,128)(2,1)S(1)} %back_product.12.refs_2_.refs_0_), channel_id=1, source_target_pairs={{0,2},{2,0},{4,6},{6,4},{1,3},{3,1},{5,7},{7,5},{8,10},{10,8},{12,... | collective-permute-start | bytes 786440 | tf_op jit(solution)/shard_map/ppermute | solution.py:680
  33.3 1.5 %back_product.13.refs_2_.refs_3_.refs_0_ = bf16[128,1024]{1,0:T(8,128)(2,1)S(1)} custom-call(bf16[128,2048]{1,0:T(8,128)(2,1)S(1)} %take_rows.2.refs_0_, bf16[5120,2048]{1,0:T(8,128)(2,1)S(1)} %get-tuple-element.38.refs_1_.refs_4_, bf16[128,1024]{1,0:T(8,128)(2,1)S(1)} %back_product.12.refs_2_.refs_0_), custom_call_target="tpu_custom_call" | custom-call | flops 1000 | bytes 3 | tf_op jit(solution)/shard_map/back_product/pallas_call | solution.py:109
  34.8 3.2 %collective-permute-start.16 = (bf16[128,1024]{1,0:T(8,128)(2,1)S(1)}, bf16[128,1024]{1,0:T(8,128)(2,1)S(1)}, u32[]{:S(2)}, u32[]{:S(2)}) collective-permute-start(bf16[128,1024]{1,0:T(8,128)(2,1)S(1)} %back_product.11.refs_2_.refs_0_), channel_id=1, source_target_pairs={{0,2},{2,0},{4,6},{6,4},{1,3},{3,1},{5,7},{7,5},{8,10},{10,8},{12,... | collective-permute-start | bytes 786440 | tf_op jit(solution)/shard_map/ppermute | solution.py:680
  38.0 1.7 %back_product.14.refs_2_.refs_3_.refs_0_ = bf16[128,1024]{1,0:T(8,128)(2,1)S(1)} custom-call(bf16[128,2048]{1,0:T(8,128)(2,1)S(1)} %take_rows.2.refs_0_, bf16[5120,2048]{1,0:T(8,128)(2,1)S(1)} %get-tuple-element.38.refs_1_.refs_4_, bf16[128,1024]{1,0:T(8,128)(2,1)S(1)} %back_product.13.refs_2_.refs_3_.refs_0_), custom_call_target="tpu_custom_call" | custom-call | flops 1000 | bytes 3 | tf_op jit(solution)/shard_map/back_product/pallas_call | solution.py:109
  39.8 1.6 %collective-permute-start.14 = (bf16[64,2048]{1,0:T(8,128)(2,1)S(1)}, bf16[64,2048]{1,0:T(8,128)(2,1)S(1)}, u32[]{:S(2)}, u32[]{:S(2)}) collective-permute-start(bf16[64,2048]{1,0:T(8,128)(2,1)S(1)} %join.10), channel_id=1, source_target_pairs={{0,16},{1,17},{8,24},{9,25},{16,0},{17,1},{24,8},{25,9},{2,18},{3,... | collective-permute-start | bytes 786440 | tf_op jit(solution)/shard_map/ppermute | solution.py:614
  41.3 1.6 %collective-permute-start.13 = (bf16[64,2048]{1,0:T(8,128)(2,1)S(1)}, bf16[64,2048]{1,0:T(8,128)(2,1)S(1)}, u32[]{:S(2)}, u32[]{:S(2)}) collective-permute-start(bf16[64,2048]{1,0:T(8,128)(2,1)S(1)} %join.9), channel_id=1, source_target_pairs={{0,1},{1,0},{8,9},{9,8},{16,17},{17,16},{24,25},{25,24},{2,3},{3,2... | collective-permute-start | bytes 786440 | tf_op jit(solution)/shard_map/ppermute | solution.py:614
  43.0 0.1 add_and_choose.7
  43.2 4.7 %prepare_more.1 = (bf16[256,512]{1,0:T(8,128)(2,1)S(1)}, bf16[256,256]{1,0:T(8,128)(2,1)S(1)}, bf16[512,256]{1,0:T(8,128)(2,1)S(1)}, bf16[512,512]{1,0:T(8,128)(...) custom-call(s32[1]{0:T(128)} %bitcast.1.refs_0_, s32[1,256]{1,0:T(1,128)} %bitcast.9, s32[1,512]{1,0:T(1,128)} %bitcast.6, ...), custom_call_target="tpu_custom_call" | custom-call | flops 1000 | bytes 3 | tf_op jit(solution)/shard_map/prepare_more/pallas_call | solution.py:109
  48.1 0.5 copy-done.4
  48.6 1.8 %collective-permute-start.15 = (bf16[64,2048]{1,0:T(8,128)(2,1)S(1)}, bf16[64,2048]{1,0:T(8,128)(2,1)S(1)}, u32[]{:S(2)}, u32[]{:S(2)}) collective-permute-start(bf16[64,2048]{1,0:T(8,128)(2,1)S(1)} %join.11), channel_id=1, source_target_pairs={{0,17},{1,16},{8,25},{9,24},{16,1},{17,0},{24,9},{25,8},{2,19},{3,... | collective-permute-start | bytes 786440 | tf_op jit(solution)/shard_map/ppermute | solution.py:614
  50.5 0.1 round_merged.1.refs_1_
  50.6 0.7 split_rows.2
  51.4 0.5 collective-permute-start.18
  51.9 0.1 add_and_choose.8
  52.0 4.6 %collective-permute-start.21 = (bf16[128,1024]{1,0:T(8,128)(2,1)S(1)}, bf16[128,1024]{1,0:T(8,128)(2,1)S(1)}, u32[]{:S(2)}, u32[]{:S(2)}) collective-permute-start(bf16[128,1024]{1,0:T(8,128)(2,1)S(1)} %get-tuple-element.56.refs_11_.refs_2_), channel_id=1, source_target_pairs={{0,2},{2,0},{4,6},{6,4},{1,3},{3,1},{5,7},{7,5},{8,10},{10,8},{12,... | collective-permute-start | bytes 786440 | tf_op jit(solution)/shard_map/ppermute | solution.py:680
  56.6 1.2 %collective-permute-done.15.refs_10_ = bf16[64,2048]{1,0:T(8,128)(2,1)S(1)} collective-permute-done((bf16[64,2048]{1,0:T(8,128)(2,1)S(1)}, bf16[64,2048]{1,0:T(8,128)(2,1)S(1)}, u32[]{:S(2)}, u32[]{:S(2)}) %collective-permute-start.15) | collective-permute-done | bytes 262176 | tf_op jit(solution)/shard_map/ppermute | solution.py:614
  57.8 0.7 take_rows.3.refs_0_
  58.5 1.5 %back_product.15.refs_3_.refs_0_ = bf16[128,1024]{1,0:T(8,128)(2,1)S(1)} custom-call(bf16[256,2048]{1,0:T(8,128)(2,1)S(1)} %take_rows.3.refs_0_, bf16[5120,2048]{1,0:T(8,128)(2,1)S(1)} %get-tuple-element.38.refs_1_.refs_4_, bf16[128,1024]{1,0:T(8,128)(2,1)S(1)} %get-tuple-element.56.refs_11_.refs_2_), custom_call_target="tpu_custom_call" | custom-call | flops 1000 | bytes 3 | tf_op jit(solution)/shard_map/back_product/pallas_call | solution.py:109
  60.0 0.1 add_and_choose.9
  60.1 3.6 %collective-permute-start.19 = (bf16[128,1024]{1,0:T(8,128)(2,1)S(1)}, bf16[128,1024]{1,0:T(8,128)(2,1)S(1)}, u32[]{:S(2)}, u32[]{:S(2)}) collective-permute-start(bf16[128,1024]{1,0:T(8,128)(2,1)S(1)} %get-tuple-element.57.refs_2_), channel_id=1, source_target_pairs={{0,2},{2,0},{4,6},{6,4},{1,3},{3,1},{5,7},{7,5},{8,10},{10,8},{12,... | collective-permute-start | bytes 786440 | tf_op jit(solution)/shard_map/ppermute | solution.py:680
  63.7 1.5 %back_product.16.refs_2_.refs_3_.refs_0_ = bf16[128,1024]{1,0:T(8,128)(2,1)S(1)} custom-call(bf16[256,2048]{1,0:T(8,128)(2,1)S(1)} %take_rows.3.refs_0_, bf16[5120,2048]{1,0:T(8,128)(2,1)S(1)} %get-tuple-element.38.refs_1_.refs_4_, bf16[128,1024]{1,0:T(8,128)(2,1)S(1)} %get-tuple-element.57.refs_2_), custom_call_target="tpu_custom_call" | custom-call | flops 1000 | bytes 3 | tf_op jit(solution)/shard_map/back_product/pallas_call | solution.py:109
  65.4 0.1 add_and_choose.10
  65.5 3.8 %collective-permute-start.24 = (bf16[128,1024]{1,0:T(8,128)(2,1)S(1)}, bf16[128,1024]{1,0:T(8,128)(2,1)S(1)}, u32[]{:S(2)}, u32[]{:S(2)}) collective-permute-start(bf16[128,1024]{1,0:T(8,128)(2,1)S(1)} %get-tuple-element.58.refs_2_), channel_id=1, source_target_pairs={{0,2},{2,0},{4,6},{6,4},{1,3},{3,1},{5,7},{7,5},{8,10},{10,8},{12,... | collective-permute-start | bytes 786440 | tf_op jit(solution)/shard_map/ppermute | solution.py:680
  69.3 1.5 %back_product.17.refs_2_.refs_3_.refs_0_ = bf16[128,1024]{1,0:T(8,128)(2,1)S(1)} custom-call(bf16[256,2048]{1,0:T(8,128)(2,1)S(1)} %take_rows.3.refs_0_, bf16[5120,2048]{1,0:T(8,128)(2,1)S(1)} %get-tuple-element.38.refs_1_.refs_4_, bf16[128,1024]{1,0:T(8,128)(2,1)S(1)} %get-tuple-element.58.refs_2_), custom_call_target="tpu_custom_call" | custom-call | flops 1000 | bytes 3 | tf_op jit(solution)/shard_map/back_product/pallas_call | solution.py:109
  71.0 0.1 add_and_choose.11
  71.1 1.5 %back_product.18.refs_2_.refs_3_.refs_0_ = bf16[128,1024]{1,0:T(8,128)(2,1)S(1)} custom-call(bf16[256,2048]{1,0:T(8,128)(2,1)S(1)} %take_rows.3.refs_0_, bf16[5120,2048]{1,0:T(8,128)(2,1)S(1)} %get-tuple-element.38.refs_1_.refs_4_, bf16[128,1024]{1,0:T(8,128)(2,1)S(1)} %get-tuple-element.59.refs_2_), custom_call_target="tpu_custom_call" | custom-call | flops 1000 | bytes 3 | tf_op jit(solution)/shard_map/back_product/pallas_call | solution.py:109
  72.6 3.8 %collective-permute-start.26 = (bf16[128,1024]{1,0:T(8,128)(2,1)S(1)}, bf16[128,1024]{1,0:T(8,128)(2,1)S(1)}, u32[]{:S(2)}, u32[]{:S(2)}) collective-permute-start(bf16[128,1024]{1,0:T(8,128)(2,1)S(1)} %get-tuple-element.59.refs_2_), channel_id=1, source_target_pairs={{0,2},{2,0},{4,6},{6,4},{1,3},{3,1},{5,7},{7,5},{8,10},{10,8},{12,... | collective-permute-start | bytes 786440 | tf_op jit(solution)/shard_map/ppermute | solution.py:680
  76.5 0.6 collective-permute-start.10
  77.2 1.2 %collective-permute-start.9 = (bf16[128,2048]{1,0:T(8,128)(2,1)S(1)}, bf16[128,2048]{1,0:T(8,128)(2,1)S(1)}, u32[]{:S(2)}, u32[]{:S(2)}) collective-permute-start(bf16[128,2048]{1,0:T(8,128)(2,1)S(1)} %join.6), channel_id=1, source_target_pairs={{0,1},{1,0},{8,9},{9,8},{16,17},{17,16},{24,25},{25,24},{2,3},{3,2... | collective-permute-start | bytes 1572872 | tf_op jit(solution)/shard_map/ppermute | solution.py:614
  78.5 0.1 add_and_choose.12
  78.7 1.6 %collective-permute-start.28 = (bf16[128,1024]{1,0:T(8,128)(2,1)S(1)}, bf16[128,1024]{1,0:T(8,128)(2,1)S(1)}, u32[]{:S(2)}, u32[]{:S(2)}) collective-permute-start(bf16[128,1024]{1,0:T(8,128)(2,1)S(1)} %get-tuple-element.60.refs_2_), channel_id=1, source_target_pairs={{0,2},{2,0},{4,6},{6,4},{1,3},{3,1},{5,7},{7,5},{8,10},{10,8},{12,... | collective-permute-start | bytes 786440 | tf_op jit(solution)/shard_map/ppermute | solution.py:680
  80.3 1.5 %back_product.19.refs_2_.refs_3_.refs_0_ = bf16[128,1024]{1,0:T(8,128)(2,1)S(1)} custom-call(bf16[256,2048]{1,0:T(8,128)(2,1)S(1)} %take_rows.3.refs_0_, bf16[5120,2048]{1,0:T(8,128)(2,1)S(1)} %get-tuple-element.38.refs_1_.refs_4_, bf16[128,1024]{1,0:T(8,128)(2,1)S(1)} %get-tuple-element.60.refs_2_), custom_call_target="tpu_custom_call" | custom-call | flops 1000 | bytes 3 | tf_op jit(solution)/shard_map/back_product/pallas_call | solution.py:109
  81.8 1.2 %collective-permute-done.26.refs_1_.refs_4_ = bf16[128,1024]{1,0:T(8,128)(2,1)S(1)} collective-permute-done((bf16[128,1024]{1,0:T(8,128)(2,1)S(1)}, bf16[128,1024]{1,0:T(8,128)(2,1)S(1)}, u32[]{:S(2)}, u32[]{:S(2)}) %collective-permute-start.26) | collective-permute-done | bytes 262176 | tf_op jit(solution)/shard_map/ppermute | solution.py:680
  83.0 0.1 add_and_choose.13
  83.2 2.6 %collective-permute-start.27 = (bf16[128,1024]{1,0:T(8,128)(2,1)S(1)}, bf16[128,1024]{1,0:T(8,128)(2,1)S(1)}, u32[]{:S(2)}, u32[]{:S(2)}) collective-permute-start(bf16[128,1024]{1,0:T(8,128)(2,1)S(1)} %get-tuple-element.61), channel_id=1, source_target_pairs={{0,2},{2,0},{4,6},{6,4},{1,3},{3,1},{5,7},{7,5},{8,10},{10,8},{12,... | collective-permute-start | bytes 786440 | tf_op jit(solution)/shard_map/ppermute | solution.py:680
  85.8 3.6 %collective-permute-done.10.refs_3_.refs_6_ = bf16[128,2048]{1,0:T(8,128)(2,1)S(1)} collective-permute-done((bf16[128,2048]{1,0:T(8,128)(2,1)S(1)}, bf16[128,2048]{1,0:T(8,128)(2,1)S(1)}, u32[]{:S(2)}, u32[]{:S(2)}) %collective-permute-start.10) | collective-permute-done | bytes 524320 | tf_op jit(solution)/shard_map/ppermute | solution.py:614
  89.3 0.4 collective-permute-done.9.refs_2_.refs_5_
  89.7 1.5 %collective-permute-start.11 = (bf16[128,2048]{1,0:T(8,128)(2,1)S(1)}, bf16[128,2048]{1,0:T(8,128)(2,1)S(1)}, u32[]{:S(2)}, u32[]{:S(2)}) collective-permute-start(bf16[128,2048]{1,0:T(8,128)(2,1)S(1)} %join.8), channel_id=1, source_target_pairs={{0,17},{1,16},{8,25},{9,24},{16,1},{17,0},{24,9},{25,8},{2,19},{3,... | collective-permute-start | bytes 1572872 | tf_op jit(solution)/shard_map/ppermute | solution.py:614
  91.4 1.1 finish.5.refs_2_.refs_7_
  92.5 0.8 collective-permute-done.27.refs_1_.refs_6_
  93.6 2.3 %collective-permute-start.34 = (bf16[128,1024]{1,0:T(8,128)(2,1)S(1)}, bf16[128,1024]{1,0:T(8,128)(2,1)S(1)}, u32[]{:S(2)}, u32[]{:S(2)}) collective-permute-start(bf16[128,1024]{1,0:T(8,128)(2,1)S(1)} %add_term.25.refs_5_), channel_id=1, source_target_pairs={{0,2},{2,0},{4,6},{6,4},{1,3},{3,1},{5,7},{7,5},{8,10},{10,8},{12,... | collective-permute-start | bytes 786440 | tf_op jit(solution)/shard_map/ppermute | solution.py:680
  96.0 3.8 %collective-permute-start.32 = (bf16[128,1024]{1,0:T(8,128)(2,1)S(1)}, bf16[128,1024]{1,0:T(8,128)(2,1)S(1)}, u32[]{:S(2)}, u32[]{:S(2)}) collective-permute-start(bf16[128,1024]{1,0:T(8,128)(2,1)S(1)} %add_term.23.refs_8_.refs_5_), channel_id=1, source_target_pairs={{0,2},{2,0},{4,6},{6,4},{1,3},{3,1},{5,7},{7,5},{8,10},{10,8},{12,... | collective-permute-start | bytes 786440 | tf_op jit(solution)/shard_map/ppermute | solution.py:680
  99.8 1.1 finish.6.refs_2_.refs_7_
  101.0 2.8 %collective-permute-start.31 = (bf16[128,1024]{1,0:T(8,128)(2,1)S(1)}, bf16[128,1024]{1,0:T(8,128)(2,1)S(1)}, u32[]{:S(2)}, u32[]{:S(2)}) collective-permute-start(bf16[128,1024]{1,0:T(8,128)(2,1)S(1)} %add_term.24.refs_8_.refs_5_), channel_id=1, source_target_pairs={{0,2},{2,0},{4,6},{6,4},{1,3},{3,1},{5,7},{7,5},{8,10},{10,8},{12,... | collective-permute-start | bytes 786440 | tf_op jit(solution)/shard_map/ppermute | solution.py:680
  103.8 1.1 finish.7.refs_7_
  105.0 0.6 copy-done.3
  105.6 2.1 %place_rows.1.refs_8_ = bf16[512,2048]{1,0:T(8,128)(2,1)} custom-call(s32[1,512]{1,0:T(1,128)S(1)} %bitcast.7, bf16[512,512]{1,0:T(8,128)(2,1)S(1)} %get-tuple-element.44.refs_1_, bf16[512,2048]{1,0:T(8,128)(2,1)S(1)} %copy-done.3, bf16[256,2048]{1,0:T(8,128)(2,1)S(1)} %get-tuple-element.49.refs_0_.refs_3_, ...), custom_call_target="tpu_custom_call" | custom-call | flops 6400000000 | bytes 21333332 | tf_op jit(solution)/shard_map/place_rows/pallas_call | solution.py:109
  107.7 0.9 collective-permute-done.32.refs_6_
  108.6 1.1 finish.8.refs_7_
  109.8 3.8 %collective-permute-done.31.refs_6_ = bf16[128,1024]{1,0:T(8,128)(2,1)S(1)} collective-permute-done((bf16[128,1024]{1,0:T(8,128)(2,1)S(1)}, bf16[128,1024]{1,0:T(8,128)(2,1)S(1)}, u32[]{:S(2)}, u32[]{:S(2)}) %collective-permute-start.31) | collective-permute-done | bytes 262176 | tf_op jit(solution)/shard_map/ppermute | solution.py:680
  113.6 1.1 finish.9
  (68 shorter events, 1.9 us)
Async XLA Ops:
  3.0 12.6 %collective-permute-start = (bf16[64,2048]{1,0:T(8,128)(2,1)S(1)}, bf16[64,2048]{1,0:T(8,128)(2,1)S(1)}, u32[]{:S(2)}, u32[]{:S(2)}) collective-permute-start(bf16[64,2048]{1,0:T(8,128)(2,1)S(1)} %get-tuple-element.37.refs_5_), channel_id=1, source_target_pairs={{0,1},{1,0},{8,9},{9,8},{16,17},{17,16},{24,25},{25,24},{2,3},{3,2... | collective-permute-start | bytes 786440 | tf_op jit(solution)/shard_map/ppermute | solution.py:614
  6.0 9.6 %collective-permute-start.1 = (bf16[64,2048]{1,0:T(8,128)(2,1)S(1)}, bf16[64,2048]{1,0:T(8,128)(2,1)S(1)}, u32[]{:S(2)}, u32[]{:S(2)}) collective-permute-start(bf16[64,2048]{1,0:T(8,128)(2,1)S(1)} %get-tuple-element.42), channel_id=1, source_target_pairs={{0,16},{1,17},{8,24},{9,25},{16,0},{17,1},{24,8},{25,9},{2,18},{3,... | collective-permute-start | bytes 786440 | tf_op jit(solution)/shard_map/ppermute | solution.py:614
  7.5 11.7 %collective-permute-start.2 = (bf16[64,2048]{1,0:T(8,128)(2,1)S(1)}, bf16[64,2048]{1,0:T(8,128)(2,1)S(1)}, u32[]{:S(2)}, u32[]{:S(2)}) collective-permute-start(bf16[64,2048]{1,0:T(8,128)(2,1)S(1)} %get-tuple-element.43), channel_id=1, source_target_pairs={{0,17},{1,16},{8,25},{9,24},{16,1},{17,0},{24,9},{25,8},{2,19},{3,... | collective-permute-start | bytes 786440 | tf_op jit(solution)/shard_map/ppermute | solution.py:614
  19.2 2.0 %collective-permute-start.3 = (bf16[128,2048]{1,0:T(8,128)(2,1)S(1)}, bf16[128,2048]{1,0:T(8,128)(2,1)S(1)}, u32[]{:S(2)}, u32[]{:S(2)}) collective-permute-start(bf16[128,2048]{1,0:T(8,128)(2,1)S(1)} %relay.1), channel_id=1, source_target_pairs={{0,8},{1,9},{8,0},{9,1},{16,24},{17,25},{24,16},{25,17},{2,10},{3,... | collective-permute-start | bytes 1572872 | tf_op jit(solution)/shard_map/ppermute | solution.py:614
  23.0 8.4 %collective-permute-start.4 = (bf16[128,1024]{1,0:T(8,128)(2,1)S(1)}, bf16[128,1024]{1,0:T(8,128)(2,1)S(1)}, u32[]{:S(2)}, u32[]{:S(2)}) collective-permute-start(bf16[128,1024]{1,0:T(8,128)(2,1)S(1)} %back_product.10.refs_2_.refs_0_), channel_id=1, source_target_pairs={{0,2},{2,0},{4,6},{6,4},{1,3},{3,1},{5,7},{7,5},{8,10},{10,8},{12,... | collective-permute-start | bytes 786440 | tf_op jit(solution)/shard_map/ppermute | solution.py:680
  27.1 12.6 %collective-permute-start.12 = (bf16[128,2048]{1,0:T(8,128)(2,1)S(1)}, bf16[128,2048]{1,0:T(8,128)(2,1)S(1)}, u32[]{:S(2)}, u32[]{:S(2)}) collective-permute-start(bf16[128,2048]{1,0:T(8,128)(2,1)S(1)} %get-tuple-element.55), channel_id=1, source_target_pairs={{0,8},{1,9},{8,0},{9,1},{16,24},{17,25},{24,16},{25,17},{2,10},{3,... | collective-permute-start | bytes 1572872 | tf_op jit(solution)/shard_map/ppermute | solution.py:614
  31.5 11.4 %collective-permute-start.6 = (bf16[128,1024]{1,0:T(8,128)(2,1)S(1)}, bf16[128,1024]{1,0:T(8,128)(2,1)S(1)}, u32[]{:S(2)}, u32[]{:S(2)}) collective-permute-start(bf16[128,1024]{1,0:T(8,128)(2,1)S(1)} %back_product.12.refs_2_.refs_0_), channel_id=1, source_target_pairs={{0,2},{2,0},{4,6},{6,4},{1,3},{3,1},{5,7},{7,5},{8,10},{10,8},{12,... | collective-permute-start | bytes 786440 | tf_op jit(solution)/shard_map/ppermute | solution.py:680
  33.3 9.7 %collective-permute-start.5 = (bf16[128,1024]{1,0:T(8,128)(2,1)S(1)}, bf16[128,1024]{1,0:T(8,128)(2,1)S(1)}, u32[]{:S(2)}, u32[]{:S(2)}) collective-permute-start(bf16[128,1024]{1,0:T(8,128)(2,1)S(1)} %add_term.13.refs_6_.refs_1_), channel_id=1, source_target_pairs={{0,8},{2,4},{4,2},{6,14},{8,0},{10,12},{12,10},{14,6},{16,24},{18,... | collective-permute-start | bytes 786440 | tf_op jit(solution)/shard_map/ppermute | solution.py:725
  34.8 13.1 %collective-permute-start.16 = (bf16[128,1024]{1,0:T(8,128)(2,1)S(1)}, bf16[128,1024]{1,0:T(8,128)(2,1)S(1)}, u32[]{:S(2)}, u32[]{:S(2)}) collective-permute-start(bf16[128,1024]{1,0:T(8,128)(2,1)S(1)} %back_product.11.refs_2_.refs_0_), channel_id=1, source_target_pairs={{0,2},{2,0},{4,6},{6,4},{1,3},{3,1},{5,7},{7,5},{8,10},{10,8},{12,... | collective-permute-start | bytes 786440 | tf_op jit(solution)/shard_map/ppermute | solution.py:680
  39.8 8.8 %collective-permute-start.14 = (bf16[64,2048]{1,0:T(8,128)(2,1)S(1)}, bf16[64,2048]{1,0:T(8,128)(2,1)S(1)}, u32[]{:S(2)}, u32[]{:S(2)}) collective-permute-start(bf16[64,2048]{1,0:T(8,128)(2,1)S(1)} %join.10), channel_id=1, source_target_pairs={{0,16},{1,17},{8,24},{9,25},{16,0},{17,1},{24,8},{25,9},{2,18},{3,... | collective-permute-start | bytes 786440 | tf_op jit(solution)/shard_map/ppermute | solution.py:614
  41.3 7.3 %collective-permute-start.13 = (bf16[64,2048]{1,0:T(8,128)(2,1)S(1)}, bf16[64,2048]{1,0:T(8,128)(2,1)S(1)}, u32[]{:S(2)}, u32[]{:S(2)}) collective-permute-start(bf16[64,2048]{1,0:T(8,128)(2,1)S(1)} %join.9), channel_id=1, source_target_pairs={{0,1},{1,0},{8,9},{9,8},{16,17},{17,16},{24,25},{25,24},{2,3},{3,2... | collective-permute-start | bytes 786440 | tf_op jit(solution)/shard_map/ppermute | solution.py:614
  43.1 7.3 %collective-permute-start.7 = (bf16[128,1024]{1,0:T(8,128)(2,1)S(1)}, bf16[128,1024]{1,0:T(8,128)(2,1)S(1)}, u32[]{:S(2)}, u32[]{:S(2)}) collective-permute-start(bf16[128,1024]{1,0:T(8,128)(2,1)S(1)} %get-tuple-element.48), channel_id=1, source_target_pairs={{0,2},{2,0},{4,6},{6,4},{1,3},{3,1},{5,7},{7,5},{8,10},{10,8},{12,... | collective-permute-start | bytes 786440 | tf_op jit(solution)/shard_map/ppermute | solution.py:680
  47.9 0.7 copy-start.4
  48.0 3.9 %collective-permute-start.17 = (bf16[128,1024]{1,0:T(8,128)(2,1)S(1)}, bf16[128,1024]{1,0:T(8,128)(2,1)S(1)}, u32[]{:S(2)}, u32[]{:S(2)}) collective-permute-start(bf16[128,1024]{1,0:T(8,128)(2,1)S(1)} %add_term.16.refs_1_), channel_id=1, source_target_pairs={{0,8},{2,4},{4,2},{6,14},{8,0},{10,12},{12,10},{14,6},{16,24},{18,... | collective-permute-start | bytes 786440 | tf_op jit(solution)/shard_map/ppermute | solution.py:725
  48.6 9.2 %collective-permute-start.15 = (bf16[64,2048]{1,0:T(8,128)(2,1)S(1)}, bf16[64,2048]{1,0:T(8,128)(2,1)S(1)}, u32[]{:S(2)}, u32[]{:S(2)}) collective-permute-start(bf16[64,2048]{1,0:T(8,128)(2,1)S(1)} %join.11), channel_id=1, source_target_pairs={{0,17},{1,16},{8,25},{9,24},{16,1},{17,0},{24,9},{25,8},{2,19},{3,... | collective-permute-start | bytes 786440 | tf_op jit(solution)/shard_map/ppermute | solution.py:614
  51.3 25.2 %collective-permute-start.8 = (bf16[256,2048]{1,0:T(8,128)(2,1)S(1)}, bf16[256,2048]{1,0:T(8,128)(2,1)S(1)}, u32[]{:S(2)}, u32[]{:S(2)}) collective-permute-start(bf16[256,2048]{1,0:T(8,128)(2,1)S(1)} %get-tuple-element.50), channel_id=1, source_target_pairs={{0,8},{1,9},{8,0},{9,1},{16,24},{17,25},{24,16},{25,17},{2,10},{3,... | collective-permute-start | bytes 3145736 | tf_op jit(solution)/shard_map/ppermute | solution.py:614
  51.4 8.6 %collective-permute-start.18 = (bf16[128,1024]{1,0:T(8,128)(2,1)S(1)}, bf16[128,1024]{1,0:T(8,128)(2,1)S(1)}, u32[]{:S(2)}, u32[]{:S(2)}) collective-permute-start(bf16[128,1024]{1,0:T(8,128)(2,1)S(1)} %add_term.14.refs_4_.refs_1_), channel_id=1, source_target_pairs={{0,8},{2,4},{4,2},{6,14},{8,0},{10,12},{12,10},{14,6},{16,24},{18,... | collective-permute-start | bytes 786440 | tf_op jit(solution)/shard_map/ppermute | solution.py:725
  52.0 13.2 %collective-permute-start.21 = (bf16[128,1024]{1,0:T(8,128)(2,1)S(1)}, bf16[128,1024]{1,0:T(8,128)(2,1)S(1)}, u32[]{:S(2)}, u32[]{:S(2)}) collective-permute-start(bf16[128,1024]{1,0:T(8,128)(2,1)S(1)} %get-tuple-element.56.refs_11_.refs_2_), channel_id=1, source_target_pairs={{0,2},{2,0},{4,6},{6,4},{1,3},{3,1},{5,7},{7,5},{8,10},{10,8},{12,... | collective-permute-start | bytes 786440 | tf_op jit(solution)/shard_map/ppermute | solution.py:680
  56.6 8.8 %collective-permute-start.20 = (bf16[128,1024]{1,0:T(8,128)(2,1)S(1)}, bf16[128,1024]{1,0:T(8,128)(2,1)S(1)}, u32[]{:S(2)}, u32[]{:S(2)}) collective-permute-start(bf16[128,1024]{1,0:T(8,128)(2,1)S(1)} %add_term.15.refs_2_.refs_4_.refs_1_), channel_id=1, source_target_pairs={{0,8},{2,4},{4,2},{6,14},{8,0},{10,12},{12,10},{14,6},{16,24},{18,... | collective-permute-start | bytes 786440 | tf_op jit(solution)/shard_map/ppermute | solution.py:725
  60.1 10.7 %collective-permute-start.19 = (bf16[128,1024]{1,0:T(8,128)(2,1)S(1)}, bf16[128,1024]{1,0:T(8,128)(2,1)S(1)}, u32[]{:S(2)}, u32[]{:S(2)}) collective-permute-start(bf16[128,1024]{1,0:T(8,128)(2,1)S(1)} %get-tuple-element.57.refs_2_), channel_id=1, source_target_pairs={{0,2},{2,0},{4,6},{6,4},{1,3},{3,1},{5,7},{7,5},{8,10},{10,8},{12,... | collective-permute-start | bytes 786440 | tf_op jit(solution)/shard_map/ppermute | solution.py:680
  65.3 5.7 %collective-permute-start.23 = (bf16[128,1024]{1,0:T(8,128)(2,1)S(1)}, bf16[128,1024]{1,0:T(8,128)(2,1)S(1)}, u32[]{:S(2)}, u32[]{:S(2)}) collective-permute-start(bf16[128,1024]{1,0:T(8,128)(2,1)S(1)} %add_term.17.refs_4_.refs_1_), channel_id=1, source_target_pairs={{0,8},{2,4},{4,2},{6,14},{8,0},{10,12},{12,10},{14,6},{16,24},{18,... | collective-permute-start | bytes 786440 | tf_op jit(solution)/shard_map/ppermute | solution.py:725
  65.5 12.9 %collective-permute-start.24 = (bf16[128,1024]{1,0:T(8,128)(2,1)S(1)}, bf16[128,1024]{1,0:T(8,128)(2,1)S(1)}, u32[]{:S(2)}, u32[]{:S(2)}) collective-permute-start(bf16[128,1024]{1,0:T(8,128)(2,1)S(1)} %get-tuple-element.58.refs_2_), channel_id=1, source_target_pairs={{0,2},{2,0},{4,6},{6,4},{1,3},{3,1},{5,7},{7,5},{8,10},{10,8},{12,... | collective-permute-start | bytes 786440 | tf_op jit(solution)/shard_map/ppermute | solution.py:680
  70.9 7.6 %collective-permute-start.22 = (bf16[128,1024]{1,0:T(8,128)(2,1)S(1)}, bf16[128,1024]{1,0:T(8,128)(2,1)S(1)}, u32[]{:S(2)}, u32[]{:S(2)}) collective-permute-start(bf16[128,1024]{1,0:T(8,128)(2,1)S(1)} %add_term.18.refs_4_.refs_1_), channel_id=1, source_target_pairs={{0,8},{2,4},{4,2},{6,14},{8,0},{10,12},{12,10},{14,6},{16,24},{18,... | collective-permute-start | bytes 786440 | tf_op jit(solution)/shard_map/ppermute | solution.py:725
  72.6 10.3 %collective-permute-start.26 = (bf16[128,1024]{1,0:T(8,128)(2,1)S(1)}, bf16[128,1024]{1,0:T(8,128)(2,1)S(1)}, u32[]{:S(2)}, u32[]{:S(2)}) collective-permute-start(bf16[128,1024]{1,0:T(8,128)(2,1)S(1)} %get-tuple-element.59.refs_2_), channel_id=1, source_target_pairs={{0,2},{2,0},{4,6},{6,4},{1,3},{3,1},{5,7},{7,5},{8,10},{10,8},{12,... | collective-permute-start | bytes 786440 | tf_op jit(solution)/shard_map/ppermute | solution.py:680
  76.5 12.8 %collective-permute-start.10 = (bf16[128,2048]{1,0:T(8,128)(2,1)S(1)}, bf16[128,2048]{1,0:T(8,128)(2,1)S(1)}, u32[]{:S(2)}, u32[]{:S(2)}) collective-permute-start(bf16[128,2048]{1,0:T(8,128)(2,1)S(1)} %join.7), channel_id=1, source_target_pairs={{0,16},{1,17},{8,24},{9,25},{16,0},{17,1},{24,8},{25,9},{2,18},{3,... | collective-permute-start | bytes 1572872 | tf_op jit(solution)/shard_map/ppermute | solution.py:614
  77.2 12.5 %collective-permute-start.9 = (bf16[128,2048]{1,0:T(8,128)(2,1)S(1)}, bf16[128,2048]{1,0:T(8,128)(2,1)S(1)}, u32[]{:S(2)}, u32[]{:S(2)}) collective-permute-start(bf16[128,2048]{1,0:T(8,128)(2,1)S(1)} %join.6), channel_id=1, source_target_pairs={{0,1},{1,0},{8,9},{9,8},{16,17},{17,16},{24,25},{25,24},{2,3},{3,2... | collective-permute-start | bytes 1572872 | tf_op jit(solution)/shard_map/ppermute | solution.py:614
  78.4 4.6 %collective-permute-start.25 = (bf16[128,1024]{1,0:T(8,128)(2,1)S(1)}, bf16[128,1024]{1,0:T(8,128)(2,1)S(1)}, u32[]{:S(2)}, u32[]{:S(2)}) collective-permute-start(bf16[128,1024]{1,0:T(8,128)(2,1)S(1)} %add_term.19.refs_4_.refs_1_), channel_id=1, source_target_pairs={{0,8},{2,4},{4,2},{6,14},{8,0},{10,12},{12,10},{14,6},{16,24},{18,... | collective-permute-start | bytes 786440 | tf_op jit(solution)/shard_map/ppermute | solution.py:725
  78.7 12.6 %collective-permute-start.28 = (bf16[128,1024]{1,0:T(8,128)(2,1)S(1)}, bf16[128,1024]{1,0:T(8,128)(2,1)S(1)}, u32[]{:S(2)}, u32[]{:S(2)}) collective-permute-start(bf16[128,1024]{1,0:T(8,128)(2,1)S(1)} %get-tuple-element.60.refs_2_), channel_id=1, source_target_pairs={{0,2},{2,0},{4,6},{6,4},{1,3},{3,1},{5,7},{7,5},{8,10},{10,8},{12,... | collective-permute-start | bytes 786440 | tf_op jit(solution)/shard_map/ppermute | solution.py:680
  83.2 8.2 %copy-start = (bf16[256,3072]{1,0:T(8,128)(2,1)S(1)}, bf16[256,3072]{1,0:T(8,128)(2,1)}, u32[]{:S(2)}) copy-start(bf16[256,3072]{1,0:T(8,128)(2,1)} %get-tuple-element.63.refs_2_) | copy-start | bytes 4718596
  83.2 10.2 %collective-permute-start.27 = (bf16[128,1024]{1,0:T(8,128)(2,1)S(1)}, bf16[128,1024]{1,0:T(8,128)(2,1)S(1)}, u32[]{:S(2)}, u32[]{:S(2)}) collective-permute-start(bf16[128,1024]{1,0:T(8,128)(2,1)S(1)} %get-tuple-element.61), channel_id=1, source_target_pairs={{0,2},{2,0},{4,6},{6,4},{1,3},{3,1},{5,7},{7,5},{8,10},{10,8},{12,... | collective-permute-start | bytes 786440 | tf_op jit(solution)/shard_map/ppermute | solution.py:680
  85.8 7.8 %collective-permute-start.33 = (bf16[128,1024]{1,0:T(8,128)(2,1)S(1)}, bf16[128,1024]{1,0:T(8,128)(2,1)S(1)}, u32[]{:S(2)}, u32[]{:S(2)}) collective-permute-start(bf16[128,1024]{1,0:T(8,128)(2,1)S(1)} %add_term.20.refs_4_.refs_0_), channel_id=1, source_target_pairs={{0,8},{2,4},{4,2},{6,14},{8,0},{10,12},{12,10},{14,6},{16,24},{18,... | collective-permute-start | bytes 786440 | tf_op jit(solution)/shard_map/ppermute | solution.py:725
  89.7 15.2 %collective-permute-start.11 = (bf16[128,2048]{1,0:T(8,128)(2,1)S(1)}, bf16[128,2048]{1,0:T(8,128)(2,1)S(1)}, u32[]{:S(2)}, u32[]{:S(2)}) collective-permute-start(bf16[128,2048]{1,0:T(8,128)(2,1)S(1)} %join.8), channel_id=1, source_target_pairs={{0,17},{1,16},{8,25},{9,24},{16,1},{17,0},{24,9},{25,8},{2,19},{3,... | collective-permute-start | bytes 1572872 | tf_op jit(solution)/shard_map/ppermute | solution.py:614
  91.3 4.6 %collective-permute-start.30 = (bf16[128,1024]{1,0:T(8,128)(2,1)S(1)}, bf16[128,1024]{1,0:T(8,128)(2,1)S(1)}, u32[]{:S(2)}, u32[]{:S(2)}) collective-permute-start(bf16[128,1024]{1,0:T(8,128)(2,1)S(1)} %add_term.21.refs_7_.refs_0_.refs_2_), channel_id=1, source_target_pairs={{0,8},{2,4},{4,2},{6,14},{8,0},{10,12},{12,10},{14,6},{16,24},{18,... | collective-permute-start | bytes 786440 | tf_op jit(solution)/shard_map/ppermute | solution.py:725
  93.4 7.5 %collective-permute-start.29 = (bf16[128,1024]{1,0:T(8,128)(2,1)S(1)}, bf16[128,1024]{1,0:T(8,128)(2,1)S(1)}, u32[]{:S(2)}, u32[]{:S(2)}) collective-permute-start(bf16[128,1024]{1,0:T(8,128)(2,1)S(1)} %add_term.22.refs_2_.refs_0_), channel_id=1, source_target_pairs={{0,8},{2,4},{4,2},{6,14},{8,0},{10,12},{12,10},{14,6},{16,24},{18,... | collective-permute-start | bytes 786440 | tf_op jit(solution)/shard_map/ppermute | solution.py:725
  93.6 10.2 %collective-permute-start.34 = (bf16[128,1024]{1,0:T(8,128)(2,1)S(1)}, bf16[128,1024]{1,0:T(8,128)(2,1)S(1)}, u32[]{:S(2)}, u32[]{:S(2)}) collective-permute-start(bf16[128,1024]{1,0:T(8,128)(2,1)S(1)} %add_term.25.refs_5_), channel_id=1, source_target_pairs={{0,2},{2,0},{4,6},{6,4},{1,3},{3,1},{5,7},{7,5},{8,10},{10,8},{12,... | collective-permute-start | bytes 786440 | tf_op jit(solution)/shard_map/ppermute | solution.py:680
  96.0 12.7 %collective-permute-start.32 = (bf16[128,1024]{1,0:T(8,128)(2,1)S(1)}, bf16[128,1024]{1,0:T(8,128)(2,1)S(1)}, u32[]{:S(2)}, u32[]{:S(2)}) collective-permute-start(bf16[128,1024]{1,0:T(8,128)(2,1)S(1)} %add_term.23.refs_8_.refs_5_), channel_id=1, source_target_pairs={{0,2},{2,0},{4,6},{6,4},{1,3},{3,1},{5,7},{7,5},{8,10},{10,8},{12,... | collective-permute-start | bytes 786440 | tf_op jit(solution)/shard_map/ppermute | solution.py:680
  101.0 12.6 %collective-permute-start.31 = (bf16[128,1024]{1,0:T(8,128)(2,1)S(1)}, bf16[128,1024]{1,0:T(8,128)(2,1)S(1)}, u32[]{:S(2)}, u32[]{:S(2)}) collective-permute-start(bf16[128,1024]{1,0:T(8,128)(2,1)S(1)} %add_term.24.refs_8_.refs_5_), channel_id=1, source_target_pairs={{0,2},{2,0},{4,6},{6,4},{1,3},{3,1},{5,7},{7,5},{8,10},{10,8},{12,... | collective-permute-start | bytes 786440 | tf_op jit(solution)/shard_map/ppermute | solution.py:680
  103.8 1.2 %copy-start.2 = (s32[512]{0:T(512)S(1)}, s32[512]{0:T(512)}, u32[]{:S(2)}) copy-start(s32[512]{0:T(512)} %param.11) | copy-start | bytes 6148
  103.8 1.8 %copy-start.3 = (bf16[512,2048]{1,0:T(8,128)(2,1)S(1)}, bf16[512,2048]{1,0:T(8,128)(2,1)}, u32[]{:S(2)}) copy-start(bf16[512,2048]{1,0:T(8,128)(2,1)} %refs_2_.1) | copy-start | bytes 6291460
  105.6 3.1 %copy-start.1 = (bf16[256,2048]{1,0:T(8,128)(2,1)S(1)}, bf16[256,2048]{1,0:T(8,128)(2,1)}, u32[]{:S(2)}) copy-start(bf16[256,2048]{1,0:T(8,128)(2,1)} %get-tuple-element.68.refs_2_) | copy-start | bytes 3145732

commit v3 on v2

--- a/solution.py
+++ b/solution.py
@@ -18,6 +18,8 @@
 NODE = 800_000_000
 TAKE = 3_200_000_000
 PLACE = 6_400_000_000
+FINISH = 2_000_000_000
+PRODUCT = 400_000_000
 
 
 def gelu_value(values):
@@ -180,22 +182,30 @@
     return outs, held
 
 
-def split_rows(hot, rows, deps=()):
-    height = hot.shape[0] // 2
-
-    def kernel(hot_ref, rows_ref, stay_ref, swap_ref):
-        dot_columns(hot_ref[:height], rows_ref, stay_ref)
-        dot_columns(hot_ref[height:], rows_ref, swap_ref)
-
-    return call(
+def split_rows(hot, rows, parts, deps=()):
+    half, width = hot.shape[0] // 2, rows.shape[1]
+    height = half // parts
+
+    def kernel(hot_ref, rows_ref, stay_ref, *swap_refs):
+        for start in range(0, width, 512):
+            span = slice(start, start + 512)
+            packed = jnp.dot(hot_ref[...], rows_ref[:, span], preferred_element_type=F32)
+            packed = packed.astype(BF)
+            stay_ref[:, span] = packed[:half]
+            for i, swap_ref in enumerate(swap_refs):
+                first = half + i * height
+                swap_ref[:, span] = packed[first : first + height]
+
+    stay, *swaps = call(
         kernel,
         "split_rows",
-        [pltpu.VMEM((height, rows.shape[1]), BF)] * 2,
+        [pltpu.VMEM((half, width), BF)] + [pltpu.VMEM((height, width), BF)] * parts,
         [VMEM, VMEM],
-        [VMEM] * 2,
+        [VMEM] * (1 + parts),
         (hot, rows),
         deps,
     )
+    return stay, swaps
 
 
 def join(stay, got, index, height, deps=()):
@@ -203,7 +213,7 @@
 
     def kernel(stay_ref, got_ref, out_ref):
         out_ref[:height] = stay_ref[span]
-        out_ref[height:] = got_ref[span]
+        out_ref[height:] = got_ref[...]
 
     return call(
         kernel,
@@ -235,118 +245,30 @@
     )
 
 
-def gelu_product(pre_ref, w_ref, slope_ref, total_ref, first, waits):
-    block = 512
-    for i, wait in enumerate(waits):
-        span = slice(i * block, (i + 1) * block)
-        values = pre_ref[:, span].astype(F32)
-        share = 0.5 * (1.0 + lax.erf(values * 0.7071067811865476))
-        slope = share + values * jnp.exp(-0.5 * values * values) * 0.3989422804014327
-        slope_ref[:, span] = slope.astype(BF)
-        wait()
-        term = jnp.dot(
-            (values * share).astype(BF),
-            w_ref[first + i * block : first + (i + 1) * block],
-            preferred_element_type=F32,
-        )
-        if first + i == 0:
-            total_ref[...] = term
-        else:
-            total_ref[...] += term
-
-
-def prepare(me, row_slots, ctx_slots, early, shift, groups, pair, pre_act, w_out, cut, deps=()):
+def prepare(me, row_slots, ctx_slots, early, shift, groups, pair, pre_act, w_out, deps=()):
     n, depth = pre_act.shape
     width = w_out.shape[1]
     tokens = ctx_slots.shape[1]
-    late = (1 << shift) - early
-    half = n * early >> shift
+    capacity = 1 << shift
+    late = capacity - early
+    half = n * early // capacity
+    wires = groups * capacity
     spans = [slice(start, start + 512) for start in range(0, depth, 512)]
 
     def kernel(me_ref, row_hbm, ctx_hbm, pre_hbm, w_hbm, *refs):
-        early_ref, late_ref, w_ref, product_ref, slope_hbm = refs[:5]
-        row_ref, ctx_ref, pre_ref, slope_ref, sems = refs[5:]
+        early_ref, all_ref, back_ref, late_ref, merged_ref, place_ref = refs[:6]
+        w_ref, product_ref, slope_hbm = refs[6:9]
+        row_ref, ctx_ref, pre_ref, slope_ref, sems = refs[9:]
         small = [
             pltpu.make_async_copy(row_hbm, row_ref, sems.at[len(spans)]),
             pltpu.make_async_copy(ctx_hbm, ctx_ref, sems.at[len(spans) + 1]),
         ]
-        values_copy = pltpu.make_async_copy(
-            pre_hbm.at[:, 0:cut], pre_ref, sems.at[len(spans) + 2]
-        )
-        slope_copy = pltpu.make_async_copy(slope_ref, slope_hbm, sems.at[len(spans) + 3])
+        values_copy = pltpu.make_async_copy(pre_hbm, pre_ref, sems.at[len(spans) + 2])
         copies = [
             pltpu.make_async_copy(w_hbm.at[span], w_ref.at[span], sems.at[i])
             for i, span in enumerate(spans)
         ]
         for copy in [*small, values_copy, *copies]:
-            copy.start()
-        for copy in small:
-            copy.wait()
-        row = row_ref[...]
-        offset = (row >> shift) ^ me_ref[0]
-        rank, is_early, place = arrival(row, shift, early)
-        wire = came_from(offset, pair, groups) * early + rank
-        order = iota((half, n), 0) == place
-        source = jnp.sum(jnp.where(order, wire, 0), axis=1, keepdims=True)
-        early_ref[...] = as_hot(iota((half, groups * early), 1) == source)
-        ctx = ctx_ref[...]
-        offset = (ctx >> shift) ^ me_ref[0]
-        rank = rank_in_block(ctx, shift)
-        target = came_from(offset, pair, groups) * late + rank - early
-        target = jnp.where((ctx >= 0) & (rank >= early), target, -1)
-        late_ref[...] = as_hot(iota((groups * late, tokens), 0) == target)
-        values_copy.wait()
-        used = cut // 512
-        waits = [copy.wait for copy in copies[:used]]
-        gelu_product(pre_ref, w_ref, slope_ref, product_ref, 0, waits)
-        slope_copy.start()
-        for copy in copies[used:]:
-            copy.wait()
-        slope_copy.wait()
-
-    shapes = [(half, groups * early), (groups * late, tokens), (depth, width)]
-    return call(
-        kernel,
-        "prepare",
-        [pltpu.VMEM(shape, BF) for shape in shapes]
-        + [pltpu.VMEM((n, width), F32), pltpu.HBM((n, cut), BF)],
-        [SMEM] + [ANY] * 4,
-        [VMEM] * 4 + [ANY],
-        (me, row_slots, ctx_slots, pre_act, w_out),
-        deps,
-        limit=10,
-        pins={i: pltpu.HBM for i in range(1, 5)},
-        flops=4 * n * depth * width,
-        scratch_shapes=[
-            pltpu.VMEM((1, n), I32),
-            pltpu.VMEM((1, tokens), I32),
-            pltpu.VMEM((n, cut), BF),
-            pltpu.VMEM((n, cut), BF),
-            pltpu.SemaphoreType.DMA((len(spans) + 4,)),
-        ],
-    )
-
-
-def prepare_more(
-    me, row_slots, ctx_slots, early, shift, groups, pair, pre_act, w_here, product, cut, deps=()
-):
-    n, depth = pre_act.shape
-    width = w_here.shape[1]
-    tokens = ctx_slots.shape[1]
-    capacity = 1 << shift
-    late = capacity - early
-    wires = groups * capacity
-
-    def kernel(me_ref, row_hbm, ctx_hbm, pre_hbm, w_ref, part_ref, *refs):
-        all_ref, back_ref, merged_ref, place_ref, product_ref, slope_hbm = refs[:6]
-        row_ref, ctx_ref, pre_ref, slope_ref, sems = refs[6:]
-        small = [
-            pltpu.make_async_copy(row_hbm, row_ref, sems.at[0]),
-            pltpu.make_async_copy(ctx_hbm, ctx_ref, sems.at[1]),
-        ]
-        values_copy = pltpu.make_async_copy(pre_hbm.at[:, cut:depth], pre_ref, sems.at[2])
-        slope_copy = pltpu.make_async_copy(slope_ref, slope_hbm, sems.at[3])
-        for copy in [*small, values_copy]:
             copy.start()
         for copy in small:
             copy.wait()
@@ -360,39 +282,71 @@
         )
         order = iota((n, n), 0) == place
         source = jnp.sum(jnp.where(order, wire, 0), axis=1, keepdims=True)
+        early_ref[...] = as_hot(iota((half, groups * early), 1) == source[:half])
         all_ref[...] = as_hot(iota((n, wires), 1) == source)
         back_ref[...] = as_hot(iota((n, n), 1) == as_column(place))
         target = (came_from(offset, pair, groups) << shift) + (row & (capacity - 1))
         merged_ref[...] = as_hot(iota((wires, n), 0) == target)
         ctx = ctx_ref[...]
         offset = (ctx >> shift) ^ me_ref[0]
+        rank = rank_in_block(ctx, shift)
+        target = came_from(offset, pair, groups) * late + rank - early
+        target = jnp.where((ctx >= 0) & (rank >= early), target, -1)
+        late_ref[...] = as_hot(iota((groups * late, tokens), 0) == target)
         source = (goes_to(offset, pair) << shift) + (ctx & (capacity - 1))
         source = as_column(jnp.where(ctx >= 0, source, -1))
         place_ref[...] = as_hot(iota((tokens, wires), 1) == source)
         values_copy.wait()
-        product_ref[...] = part_ref[...]
-        waits = [lambda: None] * ((depth - cut) // 512)
-        gelu_product(pre_ref, w_ref, slope_ref, product_ref, cut, waits)
-        slope_copy.start()
-        slope_copy.wait()
-
-    shapes = [(n, wires), (n, n), (wires, n), (tokens, wires)]
-    return call(
-        kernel,
-        "prepare_more",
+        slope_copies = []
+        for i, (copy, span) in enumerate(zip(copies, spans)):
+            values = pre_ref[:, span].astype(F32)
+            share = 0.5 * (1.0 + lax.erf(values * 0.7071067811865476))
+            slope = share + values * jnp.exp(-0.5 * values * values) * 0.3989422804014327
+            slope_ref[:, span] = slope.astype(BF)
+            slope_copies.append(
+                pltpu.make_async_copy(
+                    slope_ref.at[:, span], slope_hbm.at[:, span], sems.at[len(spans) + 3 + i]
+                )
+            )
+            slope_copies[-1].start()
+            copy.wait()
+            term = jnp.dot(
+                (values * share).astype(BF), w_ref[span], preferred_element_type=F32
+            )
+            if i == 0:
+                product_ref[...] = term
+            else:
+                product_ref[...] += term
+        for copy in slope_copies:
+            copy.wait()
+
+    shapes = [
+        (half, groups * early),
+        (n, wires),
+        (n, n),
+        (groups * late, tokens),
+        (wires, n),
+        (tokens, wires),
+        (depth, width),
+    ]
+    return call(
+        kernel,
+        "prepare",
         [pltpu.VMEM(shape, BF) for shape in shapes]
-        + [pltpu.VMEM((n, width), F32), pltpu.HBM((n, depth - cut), BF)],
-        [SMEM] + [ANY] * 3 + [VMEM] * 2,
-        [VMEM] * 5 + [ANY],
-        (me, row_slots, ctx_slots, pre_act, w_here, product),
-        deps,
-        pins={1: pltpu.HBM, 2: pltpu.HBM, 3: pltpu.HBM, 4: pltpu.VMEM},
+        + [pltpu.VMEM((n, width), F32), pltpu.HBM((n, depth), BF)],
+        [SMEM] + [ANY] * 4,
+        [VMEM] * 8 + [ANY],
+        (me, row_slots, ctx_slots, pre_act, w_out),
+        deps,
+        limit=10,
+        pins={i: pltpu.HBM for i in range(1, 5)},
+        flops=4 * n * depth * width,
         scratch_shapes=[
             pltpu.VMEM((1, n), I32),
             pltpu.VMEM((1, tokens), I32),
-            pltpu.VMEM((n, depth - cut), BF),
-            pltpu.VMEM((n, depth - cut), BF),
-            pltpu.SemaphoreType.DMA((4,)),
+            pltpu.VMEM((n, depth), BF),
+            pltpu.VMEM((n, depth), BF),
+            pltpu.SemaphoreType.DMA((2 * len(spans) + 3,)),
         ],
     )
 
@@ -453,6 +407,7 @@
         (rows, w_rows),
         deps,
         pins={1: pltpu.VMEM},
+        flops=PRODUCT,
     )
 
 
@@ -545,8 +500,8 @@
     )
 
 
-def finish(inner, hot, sums, slope, start_at, depth, so_far, first, width, deps=()):
-    n = hot.shape[0]
+def finish(inner, hot, sums, slope, so_far, first, width, deps=()):
+    n, depth = slope.shape
     flat = [array for pair in sums for array in pair]
 
     def kernel(inner_ref, hot_ref, slope_ref, *refs):
@@ -562,7 +517,7 @@
                 rows_ref[start : start + height] = block[:, i * width : (i + 1) * width]
                 start += height
         total = jnp.dot(hot_ref[...], rows_ref[...], preferred_element_type=F32)
-        slopes = slope_ref[:, first - start_at : first - start_at + width]
+        slopes = slope_ref[:, first : first + width]
         done_ref[...] = (total * slopes.astype(F32)).astype(BF)
         copy = pltpu.make_async_copy(done_ref, out_ref.at[:, first : first + width], sem)
         copy.start()
@@ -585,6 +540,7 @@
         args,
         deps,
         pins=pins,
+        flops=FINISH,
         scratch_shapes=[
             pltpu.VMEM((n, width), BF),
             pltpu.VMEM((n, width), BF),
@@ -640,22 +596,24 @@
         me, inner, ctx_slots, cotangent, 0, early, shift, groups, pair
     )
     first_in = exchange_pairs(first_out)
-    cut = 3 * size
-    hot_early, hot_late, w_here, forward, slope_low = prepare(
-        me, row_slots, ctx_slots, early, shift, groups, pair, pre_act, w_out, cut, (first_out[1],)
+    (
+        hot_early, hot_all, hot_back, hot_late, hot_merged, hot_place,
+        w_here, forward, slope,
+    ) = prepare(
+        me, row_slots, ctx_slots, early, shift, groups, pair, pre_act, w_out, (first_out[1],)
     )
 
     def exchange_in_turn(hot, sent, height, deps):
-        stay, swap = split_rows(hot, sent, deps)
-        got = exchange(pair, swap)
-        came = [(stay, slice(0, height)), (got, slice(0, height))]
+        stay, swaps = split_rows(hot, sent, half, deps)
+        got = [exchange(pair, swap) for swap in swaps]
+        came = [(stay, slice(0, height)), whole(got[0])]
         offsets = [(i // pair) * 2 * pair + i % pair for i in range(1, half)]
         blocks = {}
         for straight in (True, False):
             after = tuple(blocks.values())
             for i, offset in enumerate(offsets, 1):
                 if (offset & (offset - 1) == 0) == straight:
-                    blocks[i] = exchange(offset, join(stay, got, i, height, after))
+                    blocks[i] = exchange(offset, join(stay, got[i], i, height, after))
         return came + [whole(blocks[i]) for i in range(1, half)]
 
     def product(j, deps=()):
@@ -681,10 +639,7 @@
 
     def finish_block(k, so_far, *deps):
         sums = [(totals[i], from_pair[i + 3]) for i in (k, k + per_part)]
-        slope, start_at = (slope_low, 0) if k * size < cut else (slope_high, cut)
-        return finish(
-            inner, hot_back, sums, slope, start_at, depth, so_far, k * size, size, deps
-        )
+        return finish(inner, hot_back, sums, slope, so_far, k * size, size, deps)
 
     to_pair(0, terms[0])
     to_pair(1, terms[1])
@@ -692,24 +647,8 @@
     for j in range(chunks):
         after = []
         ahead = j + 2
-        if j == 1:
-            hot_all, hot_back, hot_merged, hot_place, forward, slope_high = prepare_more(
-                me,
-                row_slots,
-                ctx_slots,
-                early,
-                shift,
-                groups,
-                pair,
-                pre_act,
-                w_here,
-                forward,
-                cut,
-                (halves[j - 1] if j else terms[2],),
-            )
-            after.append(hot_all)
         if ahead < chunks:
-            previous = (send[j + 1],) if j >= 3 else (terms[j + 1],)
+            previous = (send[j + 1],) if j >= 2 else (terms[j + 1],)
             if ahead == per_part:
                 grads = take_rows(hot_all, first_in + second_in, previous)
             terms[ahead] = product(ahead, previous)
@@ -727,18 +666,17 @@
             value, _ = lax.optimization_barrier((terms[2], halves[0]))
             to_pair(2, value)
         elif ahead < chunks:
-            for k in {1: (), 2: (1, 2)}.get(j, (j,)):
-                totals[k - 1], send[k + 2] = add_and_choose(
-                    inner, halves[k - 1], from_far[k - 1], terms[k + 2], (halves[j],)
-                )
-                to_pair(k + 2, send[k + 2])
+            totals[j - 1], send[ahead] = add_and_choose(
+                inner, halves[j - 1], from_far[j - 1], terms[ahead], (halves[j],)
+            )
+            to_pair(ahead, send[ahead])
         else:
             totals[j - 1] = add_term(halves[j - 1], from_far[j - 1], (halves[j],))
             to_pair(ahead, totals[j - 1])
     grad_pre = finish_block(1, grad_pre, totals[chunks - 2])
     totals[chunks - 1] = add_term(halves[chunks - 1], from_far[chunks - 1], (grad_pre,))
     to_pair(chunks + 2, totals[chunks - 1])
-    embeds = place_rows(ctx_slots, hot_place, arrived, text_rows, (totals[chunks - 1],))
+    embeds = place_rows(ctx_slots, hot_place, arrived, text_rows, (halves[chunks - 2],))
     for k in range(2, per_part):
         grad_pre = finish_block(k, grad_pre, *([embeds] if k == 3 else []))
     return embeds, grad_pre

time: 115 us -> 112 us (0.974)
  waiting for transfers between devices: 20.1 us -> 16.8 us
  starting transfers between devices: 49.8 us -> 51.9 us
  Pallas kernels: 42.5 us -> 41 us
    ppermute x12 -> x18, waiting for transfers between devices: 10.6 us -> 6.8 us  [exchange(): return lax.ppermute(piece, GROUP_AXES, [(i, i ^ k) for i in range(groups)])]
    ppermute x13, starting transfers between devices: 35.8 us -> 37.3 us  [to_pair(): from_pair[j] = lax.ppermute(value, 'tp', outer_pairs)]
    pallas_call x51 -> x50, Pallas kernels: 42.5 us -> 41 us  [call(): pl.pallas_call(body, out_shape=out_shape, in_specs=list(in_specs) + [ANY]...]
    ppermute x12 -> x18, starting transfers between devices: 13 us -> 13.4 us  [exchange(): return lax.ppermute(piece, GROUP_AXES, [(i, i ^ k) for i in range(groups)])]
  transfers between devices with their start and end apart: 35 -> 41, of which waited for: 10 -> 13; matrix products, arithmetic and copies ran while one was open for 0% -> 0% of each run, Pallas kernels for 32% -> 32%
where the time goes in v3:
time: 112 us
  starting transfers between devices  51.9 us (46%)
  Pallas kernels  41 us (37%)
  waiting for transfers between devices  16.8 us (15%)
  between operations  1.42 us (1%)
    pallas_call x50, Pallas kernels, call(): pl.pallas_call(body, out_shape=out_shape, in_specs=list(in_specs) + [ANY]...  41 us
    ppermute x13, starting transfers between devices, to_pair(): from_pair[j] = lax.ppermute(value, 'tp', outer_pairs)  37.3 us
    ppermute x18, starting transfers between devices, exchange(): return lax.ppermute(piece, GROUP_AXES, [(i, i ^ k) for i in range(groups)])  13.4 us
    ppermute x13, waiting for transfers between devices, to_pair(): from_pair[j] = lax.ppermute(value, 'tp', outer_pairs)  9.96 us
    ppermute x18, waiting for transfers between devices, exchange(): return lax.ppermute(piece, GROUP_AXES, [(i, i ^ k) for i in range(groups)])  6.8 us
  transfers between devices with their start and end apart: 41, of which 13 were waited for; matrix products, arithmetic and copies ran while one was open for 0% of the time, Pallas kernels for 32%

profile of v3, /device:TPU:0, one launch (start us, length us, event | category | flops | bytes accessed | tf_op | source)
XLA Modules:
  0.0 111.7 jit_solution(17256094740404471298)
XLA Ops:
  0.6 2.3 %pack_context.1 = (bf16[64,2048]{1,0:T(8,128)(2,1)S(1)}, bf16[64,2048]{1,0:T(8,128)(2,1)S(1)}, bf16[64,2048]{1,0:T(8,128)(2,1)S(1)}, bf16[64,2048]{1,0:T(8,128)(2,1)S(1)}, bf16[512,2048]{1,0:T(8,128)(2,1)S(1)}) custom-call(s32[1]{0:T(128)} %bitcast.1.refs_0_, s32[1]{0:T(128)} %bitcast.3.refs_1_.refs_0_, s32[1,512]{1,0:T(1,128)} %bitcast.4, ...), custom_call_target="tpu_custom_call" | custom-call | flops 1000 | bytes 3 | tf_op jit(solution)/shard_map/pack_context/pallas_call | solution.py:111
  3.0 3.0 %collective-permute-start.1 = (bf16[64,2048]{1,0:T(8,128)(2,1)S(1)}, bf16[64,2048]{1,0:T(8,128)(2,1)S(1)}, u32[]{:S(2)}, u32[]{:S(2)}) collective-permute-start(bf16[64,2048]{1,0:T(8,128)(2,1)S(1)} %get-tuple-element.47), channel_id=1, source_target_pairs={{0,16},{1,17},{8,24},{9,25},{16,0},{17,1},{24,8},{25,9},{2,18},{3,... | collective-permute-start | bytes 786440 | tf_op jit(solution)/shard_map/ppermute | solution.py:570
  6.0 1.5 %collective-permute-start.2 = (bf16[64,2048]{1,0:T(8,128)(2,1)S(1)}, bf16[64,2048]{1,0:T(8,128)(2,1)S(1)}, u32[]{:S(2)}, u32[]{:S(2)}) collective-permute-start(bf16[64,2048]{1,0:T(8,128)(2,1)S(1)} %get-tuple-element.48), channel_id=1, source_target_pairs={{0,17},{1,16},{8,25},{9,24},{16,1},{17,0},{24,9},{25,8},{2,19},{3,... | collective-permute-start | bytes 786440 | tf_op jit(solution)/shard_map/ppermute | solution.py:570
  7.5 11.0 %prepare.1 = (bf16[128,256]{1,0:T(8,128)(2,1)S(1)}, bf16[256,512]{1,0:T(8,128)(2,1)S(1)}, bf16[256,256]{1,0:T(8,128)(2,1)S(1)}, bf16[256,512]{1,0:T(8,128)(2,1)S...) custom-call(s32[1]{0:T(128)} %bitcast.1.refs_0_, ...), custom_call_target="tpu_custom_call" | custom-call | flops 10737418240 | bytes 35791392 | tf_op jit(solution)/shard_map/prepare/pallas_call | solution.py:111
  18.5 0.7 collective-permute-done.2.refs_3_.refs_4_
  19.2 1.4 %collective-permute-done.refs_1_.refs_2_ = bf16[64,2048]{1,0:T(8,128)(2,1)S(1)} collective-permute-done((bf16[64,2048]{1,0:T(8,128)(2,1)S(1)}, bf16[64,2048]{1,0:T(8,128)(2,1)S(1)}, u32[]{:S(2)}, u32[]{:S(2)}) %collective-permute-start) | collective-permute-done | bytes 262176 | tf_op jit(solution)/shard_map/ppermute | solution.py:570
  20.7 1.9 %collective-permute-done.3.refs_5_ = bf16[128,2048]{1,0:T(8,128)(2,1)S(1)} collective-permute-done((bf16[128,2048]{1,0:T(8,128)(2,1)S(1)}, bf16[128,2048]{1,0:T(8,128)(2,1)S(1)}, u32[]{:S(2)}, u32[]{:S(2)}) %collective-permute-start.3) | collective-permute-done | bytes 524320 | tf_op jit(solution)/shard_map/ppermute | solution.py:570
  22.6 0.3 take_rows.2.refs_0_
  22.9 1.5 %back_product.10.refs_2_.refs_0_ = bf16[128,1024]{1,0:T(8,128)(2,1)S(1)} custom-call(bf16[128,2048]{1,0:T(8,128)(2,1)S(1)} %take_rows.2.refs_0_, bf16[5120,2048]{1,0:T(8,128)(2,1)S(1)} %get-tuple-element.49.refs_1_), custom_call_target="tpu_custom_call" | custom-call | flops 400000000 | bytes 1333333 | tf_op jit(solution)/shard_map/back_product/pallas_call | solution.py:111
  24.4 1.6 %collective-permute-start.4 = (bf16[128,1024]{1,0:T(8,128)(2,1)S(1)}, bf16[128,1024]{1,0:T(8,128)(2,1)S(1)}, u32[]{:S(2)}, u32[]{:S(2)}) collective-permute-start(bf16[128,1024]{1,0:T(8,128)(2,1)S(1)} %back_product.10.refs_2_.refs_0_), channel_id=1, source_target_pairs={{0,2},{2,0},{4,6},{6,4},{1,3},{3,1},{5,7},{7,5},{8,10},{10,8},{12,... | collective-permute-start | bytes 786440 | tf_op jit(solution)/shard_map/ppermute | solution.py:638
  26.1 1.5 %back_product.11.refs_2_.refs_0_ = bf16[128,1024]{1,0:T(8,128)(2,1)S(1)} custom-call(bf16[128,2048]{1,0:T(8,128)(2,1)S(1)} %take_rows.2.refs_0_, bf16[5120,2048]{1,0:T(8,128)(2,1)S(1)} %get-tuple-element.49.refs_1_, bf16[128,1024]{1,0:T(8,128)(2,1)S(1)} %back_product.10.refs_2_.refs_0_), custom_call_target="tpu_custom_call" | custom-call | flops 400000000 | bytes 1333333 | tf_op jit(solution)/shard_map/back_product/pallas_call | solution.py:111
  27.6 0.9 split_rows.3
  28.6 0.5 collective-permute-start.16
  29.1 0.4 collective-permute-start.6
  29.5 1.5 %back_product.12.refs_2_.refs_0_ = bf16[128,1024]{1,0:T(8,128)(2,1)S(1)} custom-call(bf16[128,2048]{1,0:T(8,128)(2,1)S(1)} %take_rows.2.refs_0_, bf16[5120,2048]{1,0:T(8,128)(2,1)S(1)} %get-tuple-element.49.refs_1_, bf16[128,1024]{1,0:T(8,128)(2,1)S(1)} %back_product.11.refs_2_.refs_0_), custom_call_target="tpu_custom_call" | custom-call | flops 400000000 | bytes 1333333 | tf_op jit(solution)/shard_map/back_product/pallas_call | solution.py:111
  31.1 1.6 %collective-permute-start.19 = (bf16[64,2048]{1,0:T(8,128)(2,1)S(1)}, bf16[64,2048]{1,0:T(8,128)(2,1)S(1)}, u32[]{:S(2)}, u32[]{:S(2)}) collective-permute-start(bf16[64,2048]{1,0:T(8,128)(2,1)S(1)} %join.10), channel_id=1, source_target_pairs={{0,16},{1,17},{8,24},{9,25},{16,0},{17,1},{24,8},{25,9},{2,18},{3,... | collective-permute-start | bytes 786440 | tf_op jit(solution)/shard_map/ppermute | solution.py:570
  32.7 0.6 collective-permute-start.17
  33.2 0.4 collective-permute-done.4.refs_1_
  33.8 0.5 collective-permute-start.20
  34.3 1.5 %back_product.13.refs_2_.refs_3_.refs_0_ = bf16[128,1024]{1,0:T(8,128)(2,1)S(1)} custom-call(bf16[128,2048]{1,0:T(8,128)(2,1)S(1)} %take_rows.2.refs_0_, bf16[5120,2048]{1,0:T(8,128)(2,1)S(1)} %get-tuple-element.49.refs_1_, bf16[128,1024]{1,0:T(8,128)(2,1)S(1)} %back_product.12.refs_2_.refs_0_), custom_call_target="tpu_custom_call" | custom-call | flops 400000000 | bytes 1333333 | tf_op jit(solution)/shard_map/back_product/pallas_call | solution.py:111
  35.8 2.7 %collective-permute-done.6.refs_1_ = bf16[128,1024]{1,0:T(8,128)(2,1)S(1)} collective-permute-done((bf16[128,1024]{1,0:T(8,128)(2,1)S(1)}, bf16[128,1024]{1,0:T(8,128)(2,1)S(1)}, u32[]{:S(2)}, u32[]{:S(2)}) %collective-permute-start.6) | collective-permute-done | bytes 262176 | tf_op jit(solution)/shard_map/ppermute | solution.py:638
  38.5 1.6 %collective-permute-start.23 = (bf16[128,1024]{1,0:T(8,128)(2,1)S(1)}, bf16[128,1024]{1,0:T(8,128)(2,1)S(1)}, u32[]{:S(2)}, u32[]{:S(2)}) collective-permute-start(bf16[128,1024]{1,0:T(8,128)(2,1)S(1)} %back_product.12.refs_2_.refs_0_), channel_id=1, source_target_pairs={{0,2},{2,0},{4,6},{6,4},{1,3},{3,1},{5,7},{7,5},{8,10},{10,8},{12,... | collective-permute-start | bytes 786440 | tf_op jit(solution)/shard_map/ppermute | solution.py:638
  40.2 0.5 collective-permute-start.15
  40.7 1.5 %collective-permute-start.21 = (bf16[64,2048]{1,0:T(8,128)(2,1)S(1)}, bf16[64,2048]{1,0:T(8,128)(2,1)S(1)}, u32[]{:S(2)}, u32[]{:S(2)}) collective-permute-start(bf16[64,2048]{1,0:T(8,128)(2,1)S(1)} %join.11), channel_id=1, source_target_pairs={{0,17},{1,16},{8,25},{9,24},{16,1},{17,0},{24,9},{25,8},{2,19},{3,... | collective-permute-start | bytes 786440 | tf_op jit(solution)/shard_map/ppermute | solution.py:570
  42.3 2.7 %collective-permute-start.7 = (bf16[128,1024]{1,0:T(8,128)(2,1)S(1)}, bf16[128,1024]{1,0:T(8,128)(2,1)S(1)}, u32[]{:S(2)}, u32[]{:S(2)}) collective-permute-start(bf16[128,1024]{1,0:T(8,128)(2,1)S(1)} %get-tuple-element.50.refs_2_), channel_id=1, source_target_pairs={{0,2},{2,0},{4,6},{6,4},{1,3},{3,1},{5,7},{7,5},{8,10},{10,8},{12,... | collective-permute-start | bytes 786440 | tf_op jit(solution)/shard_map/ppermute | solution.py:638
  45.1 1.5 %back_product.14.refs_2_.refs_3_.refs_0_ = bf16[128,1024]{1,0:T(8,128)(2,1)S(1)} custom-call(bf16[128,2048]{1,0:T(8,128)(2,1)S(1)} %take_rows.2.refs_0_, bf16[5120,2048]{1,0:T(8,128)(2,1)S(1)} %get-tuple-element.49.refs_1_, bf16[128,1024]{1,0:T(8,128)(2,1)S(1)} %get-tuple-element.50.refs_2_), custom_call_target="tpu_custom_call" | custom-call | flops 400000000 | bytes 1333333 | tf_op jit(solution)/shard_map/back_product/pallas_call | solution.py:111
  46.9 3.7 %collective-permute-start.24 = (bf16[128,1024]{1,0:T(8,128)(2,1)S(1)}, bf16[128,1024]{1,0:T(8,128)(2,1)S(1)}, u32[]{:S(2)}, u32[]{:S(2)}) collective-permute-start(bf16[128,1024]{1,0:T(8,128)(2,1)S(1)} %get-tuple-element.65.refs_11_.refs_2_), channel_id=1, source_target_pairs={{0,2},{2,0},{4,6},{6,4},{1,3},{3,1},{5,7},{7,5},{8,10},{10,8},{12,... | collective-permute-start | bytes 786440 | tf_op jit(solution)/shard_map/ppermute | solution.py:638
  50.6 0.7 take_rows.3.refs_0_
  51.3 0.8 collective-permute-done.7.refs_1_.refs_4_
  52.3 1.5 %back_product.15.refs_3_.refs_0_ = bf16[128,1024]{1,0:T(8,128)(2,1)S(1)} custom-call(bf16[256,2048]{1,0:T(8,128)(2,1)S(1)} %take_rows.3.refs_0_, bf16[5120,2048]{1,0:T(8,128)(2,1)S(1)} %get-tuple-element.49.refs_1_, bf16[128,1024]{1,0:T(8,128)(2,1)S(1)} %get-tuple-element.65.refs_11_.refs_2_), custom_call_target="tpu_custom_call" | custom-call | flops 400000000 | bytes 1333333 | tf_op jit(solution)/shard_map/back_product/pallas_call | solution.py:111
  53.9 3.3 %collective-permute-start.28 = (bf16[128,1024]{1,0:T(8,128)(2,1)S(1)}, bf16[128,1024]{1,0:T(8,128)(2,1)S(1)}, u32[]{:S(2)}, u32[]{:S(2)}) collective-permute-start(bf16[128,1024]{1,0:T(8,128)(2,1)S(1)} %get-tuple-element.66.refs_2_), channel_id=1, source_target_pairs={{0,2},{2,0},{4,6},{6,4},{1,3},{3,1},{5,7},{7,5},{8,10},{10,8},{12,... | collective-permute-start | bytes 786440 | tf_op jit(solution)/shard_map/ppermute | solution.py:638
  57.2 1.5 %back_product.16.refs_2_.refs_3_.refs_0_ = bf16[128,1024]{1,0:T(8,128)(2,1)S(1)} custom-call(bf16[256,2048]{1,0:T(8,128)(2,1)S(1)} %take_rows.3.refs_0_, bf16[5120,2048]{1,0:T(8,128)(2,1)S(1)} %get-tuple-element.49.refs_1_, bf16[128,1024]{1,0:T(8,128)(2,1)S(1)} %get-tuple-element.66.refs_2_), custom_call_target="tpu_custom_call" | custom-call | flops 400000000 | bytes 1333333 | tf_op jit(solution)/shard_map/back_product/pallas_call | solution.py:111
  59.0 3.5 %collective-permute-start.30 = (bf16[128,1024]{1,0:T(8,128)(2,1)S(1)}, bf16[128,1024]{1,0:T(8,128)(2,1)S(1)}, u32[]{:S(2)}, u32[]{:S(2)}) collective-permute-start(bf16[128,1024]{1,0:T(8,128)(2,1)S(1)} %get-tuple-element.67.refs_2_), channel_id=1, source_target_pairs={{0,2},{2,0},{4,6},{6,4},{1,3},{3,1},{5,7},{7,5},{8,10},{10,8},{12,... | collective-permute-start | bytes 786440 | tf_op jit(solution)/shard_map/ppermute | solution.py:638
  62.5 1.5 %back_product.17.refs_2_.refs_3_.refs_0_ = bf16[128,1024]{1,0:T(8,128)(2,1)S(1)} custom-call(bf16[256,2048]{1,0:T(8,128)(2,1)S(1)} %take_rows.3.refs_0_, bf16[5120,2048]{1,0:T(8,128)(2,1)S(1)} %get-tuple-element.49.refs_1_, bf16[128,1024]{1,0:T(8,128)(2,1)S(1)} %get-tuple-element.67.refs_2_), custom_call_target="tpu_custom_call" | custom-call | flops 400000000 | bytes 1333333 | tf_op jit(solution)/shard_map/back_product/pallas_call | solution.py:111
  64.2 0.5 copy-done.3
  64.9 0.7 split_rows.2
  65.7 0.5 collective-permute-start.11
  66.3 2.9 %collective-permute-start.32 = (bf16[128,1024]{1,0:T(8,128)(2,1)S(1)}, bf16[128,1024]{1,0:T(8,128)(2,1)S(1)}, u32[]{:S(2)}, u32[]{:S(2)}) collective-permute-start(bf16[128,1024]{1,0:T(8,128)(2,1)S(1)} %get-tuple-element.68.refs_2_), channel_id=1, source_target_pairs={{0,2},{2,0},{4,6},{6,4},{1,3},{3,1},{5,7},{7,5},{8,10},{10,8},{12,... | collective-permute-start | bytes 786440 | tf_op jit(solution)/shard_map/ppermute | solution.py:638
  69.1 1.5 %back_product.18.refs_2_.refs_3_.refs_0_ = bf16[128,1024]{1,0:T(8,128)(2,1)S(1)} custom-call(bf16[256,2048]{1,0:T(8,128)(2,1)S(1)} %take_rows.3.refs_0_, bf16[5120,2048]{1,0:T(8,128)(2,1)S(1)} %get-tuple-element.49.refs_1_, bf16[128,1024]{1,0:T(8,128)(2,1)S(1)} %get-tuple-element.68.refs_2_), custom_call_target="tpu_custom_call" | custom-call | flops 400000000 | bytes 1333333 | tf_op jit(solution)/shard_map/back_product/pallas_call | solution.py:111
  70.7 0.1 add_and_choose.12
  70.8 2.5 %collective-permute-start.31 = (bf16[128,1024]{1,0:T(8,128)(2,1)S(1)}, bf16[128,1024]{1,0:T(8,128)(2,1)S(1)}, u32[]{:S(2)}, u32[]{:S(2)}) collective-permute-start(bf16[128,1024]{1,0:T(8,128)(2,1)S(1)} %get-tuple-element.69.refs_2_), channel_id=1, source_target_pairs={{0,2},{2,0},{4,6},{6,4},{1,3},{3,1},{5,7},{7,5},{8,10},{10,8},{12,... | collective-permute-start | bytes 786440 | tf_op jit(solution)/shard_map/ppermute | solution.py:638
  73.3 1.5 %back_product.19.refs_2_.refs_3_.refs_0_ = bf16[128,1024]{1,0:T(8,128)(2,1)S(1)} custom-call(bf16[256,2048]{1,0:T(8,128)(2,1)S(1)} %take_rows.3.refs_0_, bf16[5120,2048]{1,0:T(8,128)(2,1)S(1)} %get-tuple-element.49.refs_1_, bf16[128,1024]{1,0:T(8,128)(2,1)S(1)} %get-tuple-element.69.refs_2_), custom_call_target="tpu_custom_call" | custom-call | flops 400000000 | bytes 1333333 | tf_op jit(solution)/shard_map/back_product/pallas_call | solution.py:111
  74.9 1.3 %collective-permute-done.32.refs_1_.refs_4_ = bf16[128,1024]{1,0:T(8,128)(2,1)S(1)} collective-permute-done((bf16[128,1024]{1,0:T(8,128)(2,1)S(1)}, bf16[128,1024]{1,0:T(8,128)(2,1)S(1)}, u32[]{:S(2)}, u32[]{:S(2)}) %collective-permute-start.32) | collective-permute-done | bytes 262176 | tf_op jit(solution)/shard_map/ppermute | solution.py:638
  76.4 1.7 %collective-permute-start.12 = (bf16[128,2048]{1,0:T(8,128)(2,1)S(1)}, bf16[128,2048]{1,0:T(8,128)(2,1)S(1)}, u32[]{:S(2)}, u32[]{:S(2)}) collective-permute-start(bf16[128,2048]{1,0:T(8,128)(2,1)S(1)} %join.7), channel_id=1, source_target_pairs={{0,16},{1,17},{8,24},{9,25},{16,0},{17,1},{24,8},{25,9},{2,18},{3,... | collective-permute-start | bytes 1572872 | tf_op jit(solution)/shard_map/ppermute | solution.py:570
  78.2 0.4 collective-permute-start.10
  78.6 2.6 %collective-permute-done.31.refs_1_.refs_6_ = bf16[128,1024]{1,0:T(8,128)(2,1)S(1)} collective-permute-done((bf16[128,1024]{1,0:T(8,128)(2,1)S(1)}, bf16[128,1024]{1,0:T(8,128)(2,1)S(1)}, u32[]{:S(2)}, u32[]{:S(2)}) %collective-permute-start.31) | collective-permute-done | bytes 262176 | tf_op jit(solution)/shard_map/ppermute | solution.py:638
  81.2 0.3 add_term.20.refs_8_.refs_7_.refs_0_.refs_2_
  81.5 0.6 collective-permute-start.36
  82.2 6.9 %collective-permute-start.34 = (bf16[128,1024]{1,0:T(8,128)(2,1)S(1)}, bf16[128,1024]{1,0:T(8,128)(2,1)S(1)}, u32[]{:S(2)}, u32[]{:S(2)}) collective-permute-start(bf16[128,1024]{1,0:T(8,128)(2,1)S(1)} %get-tuple-element.73), channel_id=1, source_target_pairs={{0,2},{2,0},{4,6},{6,4},{1,3},{3,1},{5,7},{7,5},{8,10},{10,8},{12,... | collective-permute-start | bytes 786440 | tf_op jit(solution)/shard_map/ppermute | solution.py:638
  89.2 1.1 %finish.5.refs_2_.refs_7_ = bf16[256,5120]{1,0:T(8,128)(2,1)} custom-call(s32[1]{0:T(128)} %bitcast.3.refs_1_.refs_0_, bf16[256,256]{1,0:T(8,128)(2,1)S(1)} %get-tuple-element.70.refs_1_, bf16[256,5120]{1,0:T(8,128)(2,1)S(1)} %copy-done, bf16[128,1024]{1,0:T(8,128)(2,1)S(1)} %get-tuple-element.74.refs_3_, ...), custom_call_target="tpu_custom_call" | custom-call | flops 2000000000 | bytes 6666666 | tf_op jit(solution)/shard_map/finish/pallas_call | solution.py:111
  90.4 0.4 collective-permute-done.12.refs_3_.refs_6_
  90.8 0.6 collective-permute-start.40
  91.4 0.9 collective-permute-done.10.refs_2_.refs_5_
  92.3 0.8 collective-permute-start.14
  93.1 1.5 %collective-permute-done.34.refs_1_.refs_6_ = bf16[128,1024]{1,0:T(8,128)(2,1)S(1)} collective-permute-done((bf16[128,1024]{1,0:T(8,128)(2,1)S(1)}, bf16[128,1024]{1,0:T(8,128)(2,1)S(1)}, u32[]{:S(2)}, u32[]{:S(2)}) %collective-permute-start.34) | collective-permute-done | bytes 262176 | tf_op jit(solution)/shard_map/ppermute | solution.py:638
  94.9 3.6 %collective-permute-start.38 = (bf16[128,1024]{1,0:T(8,128)(2,1)S(1)}, bf16[128,1024]{1,0:T(8,128)(2,1)S(1)}, u32[]{:S(2)}, u32[]{:S(2)}) collective-permute-start(bf16[128,1024]{1,0:T(8,128)(2,1)S(1)} %add_term.23.refs_8_.refs_5_), channel_id=1, source_target_pairs={{0,2},{2,0},{4,6},{6,4},{1,3},{3,1},{5,7},{7,5},{8,10},{10,8},{12,... | collective-permute-start | bytes 786440 | tf_op jit(solution)/shard_map/ppermute | solution.py:638
  98.5 1.1 %finish.6.refs_2_.refs_7_ = bf16[256,5120]{1,0:T(8,128)(2,1)} custom-call(s32[1]{0:T(128)} %bitcast.3.refs_1_.refs_0_, bf16[256,256]{1,0:T(8,128)(2,1)S(1)} %get-tuple-element.70.refs_1_, bf16[256,5120]{1,0:T(8,128)(2,1)S(1)} %copy-done, bf16[128,1024]{1,0:T(8,128)(2,1)S(1)} %get-tuple-element.76.refs_3_, ...), custom_call_target="tpu_custom_call", output_to_operand_aliasing={{}: (7, {})} | custom-call | flops 2000000000 | bytes 6666666 | tf_op jit(solution)/shard_map/finish/pallas_call | solution.py:111
  99.7 4.1 %collective-permute-start.37 = (bf16[128,1024]{1,0:T(8,128)(2,1)S(1)}, bf16[128,1024]{1,0:T(8,128)(2,1)S(1)}, u32[]{:S(2)}, u32[]{:S(2)}) collective-permute-start(bf16[128,1024]{1,0:T(8,128)(2,1)S(1)} %add_term.24.refs_5_), channel_id=1, source_target_pairs={{0,2},{2,0},{4,6},{6,4},{1,3},{3,1},{5,7},{7,5},{8,10},{10,8},{12,... | collective-permute-start | bytes 786440 | tf_op jit(solution)/shard_map/ppermute | solution.py:638
  103.8 1.1 %finish.7.refs_7_ = bf16[256,5120]{1,0:T(8,128)(2,1)} custom-call(s32[1]{0:T(128)} %bitcast.3.refs_1_.refs_0_, bf16[256,256]{1,0:T(8,128)(2,1)S(1)} %get-tuple-element.70.refs_1_, bf16[256,5120]{1,0:T(8,128)(2,1)S(1)} %copy-done, bf16[128,1024]{1,0:T(8,128)(2,1)S(1)} %get-tuple-element.79.refs_3_, ...), custom_call_target="tpu_custom_call", output_to_operand_aliasing={{}: (7, {})} | custom-call | flops 2000000000 | bytes 6666666 | tf_op jit(solution)/shard_map/finish/pallas_call | solution.py:111
  104.9 1.6 %collective-permute-done.14.refs_7_ = bf16[128,2048]{1,0:T(8,128)(2,1)S(1)} collective-permute-done((bf16[128,2048]{1,0:T(8,128)(2,1)S(1)}, bf16[128,2048]{1,0:T(8,128)(2,1)S(1)}, u32[]{:S(2)}, u32[]{:S(2)}) %collective-permute-start.14) | collective-permute-done | bytes 524320 | tf_op jit(solution)/shard_map/ppermute | solution.py:570
  106.5 2.1 %place_rows.1.refs_8_ = bf16[512,2048]{1,0:T(8,128)(2,1)} custom-call(s32[1,512]{1,0:T(1,128)S(1)} %bitcast.6, bf16[512,512]{1,0:T(8,128)(2,1)S(1)} %get-tuple-element.42.refs_1_, bf16[512,2048]{1,0:T(8,128)(2,1)S(1)} %copy-done.2, bf16[256,2048]{1,0:T(8,128)(2,1)S(1)} %get-tuple-element.51.refs_0_.refs_3_, ...), custom_call_target="tpu_custom_call" | custom-call | flops 6400000000 | bytes 21333332 | tf_op jit(solution)/shard_map/place_rows/pallas_call | solution.py:111
  108.6 1.1 %finish.8.refs_7_ = bf16[256,5120]{1,0:T(8,128)(2,1)} custom-call(s32[1]{0:T(128)} %bitcast.3.refs_1_.refs_0_, bf16[256,256]{1,0:T(8,128)(2,1)S(1)} %get-tuple-element.70.refs_1_, bf16[256,5120]{1,0:T(8,128)(2,1)S(1)} %copy-done, bf16[128,1024]{1,0:T(8,128)(2,1)S(1)} %get-tuple-element.78.refs_3_, ...), custom_call_target="tpu_custom_call", output_to_operand_aliasing={{}: (7, {})} | custom-call | flops 2000000000 | bytes 6666666 | tf_op jit(solution)/shard_map/finish/pallas_call | solution.py:111
  109.8 0.6 collective-permute-done.37.refs_6_
  110.4 1.1 %finish.9 = bf16[256,5120]{1,0:T(8,128)(2,1)} custom-call(s32[1]{0:T(128)} %bitcast.3.refs_1_.refs_0_, bf16[256,256]{1,0:T(8,128)(2,1)S(1)} %get-tuple-element.70.refs_1_, bf16[256,5120]{1,0:T(8,128)(2,1)S(1)} %copy-done, bf16[128,1024]{1,0:T(8,128)(2,1)S(1)} %get-tuple-element.72.refs_3_, ...), custom_call_target="tpu_custom_call", output_to_operand_aliasing={{}: (7, {})} | custom-call | flops 2000000000 | bytes 6666666 | tf_op jit(solution)/shard_map/finish/pallas_call | solution.py:111
  (77 shorter events, 2.8 us)
Async XLA Ops:
  3.0 15.5 %collective-permute-start.1 = (bf16[64,2048]{1,0:T(8,128)(2,1)S(1)}, bf16[64,2048]{1,0:T(8,128)(2,1)S(1)}, u32[]{:S(2)}, u32[]{:S(2)}) collective-permute-start(bf16[64,2048]{1,0:T(8,128)(2,1)S(1)} %get-tuple-element.47), channel_id=1, source_target_pairs={{0,16},{1,17},{8,24},{9,25},{16,0},{17,1},{24,8},{25,9},{2,18},{3,... | collective-permute-start | bytes 786440 | tf_op jit(solution)/shard_map/ppermute | solution.py:570
  6.0 13.2 %collective-permute-start.2 = (bf16[64,2048]{1,0:T(8,128)(2,1)S(1)}, bf16[64,2048]{1,0:T(8,128)(2,1)S(1)}, u32[]{:S(2)}, u32[]{:S(2)}) collective-permute-start(bf16[64,2048]{1,0:T(8,128)(2,1)S(1)} %get-tuple-element.48), channel_id=1, source_target_pairs={{0,17},{1,16},{8,25},{9,24},{16,1},{17,0},{24,9},{25,8},{2,19},{3,... | collective-permute-start | bytes 786440 | tf_op jit(solution)/shard_map/ppermute | solution.py:570
  7.5 13.1 %collective-permute-start = (bf16[64,2048]{1,0:T(8,128)(2,1)S(1)}, bf16[64,2048]{1,0:T(8,128)(2,1)S(1)}, u32[]{:S(2)}, u32[]{:S(2)}) collective-permute-start(bf16[64,2048]{1,0:T(8,128)(2,1)S(1)} %get-tuple-element.41.refs_5_), channel_id=1, source_target_pairs={{0,1},{1,0},{8,9},{9,8},{16,17},{17,16},{24,25},{25,24},{2,3},{3,2... | collective-permute-start | bytes 786440 | tf_op jit(solution)/shard_map/ppermute | solution.py:570
  20.6 2.0 %collective-permute-start.3 = (bf16[128,2048]{1,0:T(8,128)(2,1)S(1)}, bf16[128,2048]{1,0:T(8,128)(2,1)S(1)}, u32[]{:S(2)}, u32[]{:S(2)}) collective-permute-start(bf16[128,2048]{1,0:T(8,128)(2,1)S(1)} %relay.1), channel_id=1, source_target_pairs={{0,8},{1,9},{8,0},{9,1},{16,24},{17,25},{24,16},{25,17},{2,10},{3,... | collective-permute-start | bytes 1572872 | tf_op jit(solution)/shard_map/ppermute | solution.py:570
  24.4 9.2 %collective-permute-start.4 = (bf16[128,1024]{1,0:T(8,128)(2,1)S(1)}, bf16[128,1024]{1,0:T(8,128)(2,1)S(1)}, u32[]{:S(2)}, u32[]{:S(2)}) collective-permute-start(bf16[128,1024]{1,0:T(8,128)(2,1)S(1)} %back_product.10.refs_2_.refs_0_), channel_id=1, source_target_pairs={{0,2},{2,0},{4,6},{6,4},{1,3},{3,1},{5,7},{7,5},{8,10},{10,8},{12,... | collective-permute-start | bytes 786440 | tf_op jit(solution)/shard_map/ppermute | solution.py:638
  28.5 2.5 %collective-permute-start.18 = (bf16[32,2048]{1,0:T(8,128)(2,1)S(1)}, bf16[32,2048]{1,0:T(8,128)(2,1)S(1)}, u32[]{:S(2)}, u32[]{:S(2)}) collective-permute-start(bf16[32,2048]{1,0:T(8,128)(2,1)S(1)} %get-tuple-element.62), channel_id=1, source_target_pairs={{0,8},{1,9},{8,0},{9,1},{16,24},{17,25},{24,16},{25,17},{2,10},{3,... | collective-permute-start | bytes 393224 | tf_op jit(solution)/shard_map/ppermute | solution.py:570
  28.6 4.1 %collective-permute-start.16 = (bf16[32,2048]{1,0:T(8,128)(2,1)S(1)}, bf16[32,2048]{1,0:T(8,128)(2,1)S(1)}, u32[]{:S(2)}, u32[]{:S(2)}) collective-permute-start(bf16[32,2048]{1,0:T(8,128)(2,1)S(1)} %get-tuple-element.61), channel_id=1, source_target_pairs={{0,8},{1,9},{8,0},{9,1},{16,24},{17,25},{24,16},{25,17},{2,10},{3,... | collective-permute-start | bytes 393224 | tf_op jit(solution)/shard_map/ppermute | solution.py:570
  29.1 9.4 %collective-permute-start.6 = (bf16[128,1024]{1,0:T(8,128)(2,1)S(1)}, bf16[128,1024]{1,0:T(8,128)(2,1)S(1)}, u32[]{:S(2)}, u32[]{:S(2)}) collective-permute-start(bf16[128,1024]{1,0:T(8,128)(2,1)S(1)} %back_product.11.refs_2_.refs_0_), channel_id=1, source_target_pairs={{0,2},{2,0},{4,6},{6,4},{1,3},{3,1},{5,7},{7,5},{8,10},{10,8},{12,... | collective-permute-start | bytes 786440 | tf_op jit(solution)/shard_map/ppermute | solution.py:638
  31.1 9.1 %collective-permute-start.19 = (bf16[64,2048]{1,0:T(8,128)(2,1)S(1)}, bf16[64,2048]{1,0:T(8,128)(2,1)S(1)}, u32[]{:S(2)}, u32[]{:S(2)}) collective-permute-start(bf16[64,2048]{1,0:T(8,128)(2,1)S(1)} %join.10), channel_id=1, source_target_pairs={{0,16},{1,17},{8,24},{9,25},{16,0},{17,1},{24,8},{25,9},{2,18},{3,... | collective-permute-start | bytes 786440 | tf_op jit(solution)/shard_map/ppermute | solution.py:570
  32.7 8.0 %collective-permute-start.17 = (bf16[64,2048]{1,0:T(8,128)(2,1)S(1)}, bf16[64,2048]{1,0:T(8,128)(2,1)S(1)}, u32[]{:S(2)}, u32[]{:S(2)}) collective-permute-start(bf16[64,2048]{1,0:T(8,128)(2,1)S(1)} %join.9), channel_id=1, source_target_pairs={{0,1},{1,0},{8,9},{9,8},{16,17},{17,16},{24,25},{25,24},{2,3},{3,2... | collective-permute-start | bytes 786440 | tf_op jit(solution)/shard_map/ppermute | solution.py:570
  33.7 8.5 %collective-permute-start.5 = (bf16[128,1024]{1,0:T(8,128)(2,1)S(1)}, bf16[128,1024]{1,0:T(8,128)(2,1)S(1)}, u32[]{:S(2)}, u32[]{:S(2)}) collective-permute-start(bf16[128,1024]{1,0:T(8,128)(2,1)S(1)} %add_term.13.refs_1_), channel_id=1, source_target_pairs={{0,8},{2,4},{4,2},{6,14},{8,0},{10,12},{12,10},{14,6},{16,24},{18,... | collective-permute-start | bytes 786440 | tf_op jit(solution)/shard_map/ppermute | solution.py:664
  33.8 6.3 %collective-permute-start.20 = (bf16[32,2048]{1,0:T(8,128)(2,1)S(1)}, bf16[32,2048]{1,0:T(8,128)(2,1)S(1)}, u32[]{:S(2)}, u32[]{:S(2)}) collective-permute-start(bf16[32,2048]{1,0:T(8,128)(2,1)S(1)} %get-tuple-element.63), channel_id=1, source_target_pairs={{0,8},{1,9},{8,0},{9,1},{16,24},{17,25},{24,16},{25,17},{2,10},{3,... | collective-permute-start | bytes 393224 | tf_op jit(solution)/shard_map/ppermute | solution.py:570
  38.5 8.1 %collective-permute-start.23 = (bf16[128,1024]{1,0:T(8,128)(2,1)S(1)}, bf16[128,1024]{1,0:T(8,128)(2,1)S(1)}, u32[]{:S(2)}, u32[]{:S(2)}) collective-permute-start(bf16[128,1024]{1,0:T(8,128)(2,1)S(1)} %back_product.12.refs_2_.refs_0_), channel_id=1, source_target_pairs={{0,2},{2,0},{4,6},{6,4},{1,3},{3,1},{5,7},{7,5},{8,10},{10,8},{12,... | collective-permute-start | bytes 786440 | tf_op jit(solution)/shard_map/ppermute | solution.py:638
  40.1 6.6 %collective-permute-start.22 = (bf16[128,1024]{1,0:T(8,128)(2,1)S(1)}, bf16[128,1024]{1,0:T(8,128)(2,1)S(1)}, u32[]{:S(2)}, u32[]{:S(2)}) collective-permute-start(bf16[128,1024]{1,0:T(8,128)(2,1)S(1)} %add_term.14.refs_4_.refs_1_), channel_id=1, source_target_pairs={{0,8},{2,4},{4,2},{6,14},{8,0},{10,12},{12,10},{14,6},{16,24},{18,... | collective-permute-start | bytes 786440 | tf_op jit(solution)/shard_map/ppermute | solution.py:664
  40.2 10.4 %collective-permute-start.15 = (bf16[32,2048]{1,0:T(8,128)(2,1)S(1)}, bf16[32,2048]{1,0:T(8,128)(2,1)S(1)}, u32[]{:S(2)}, u32[]{:S(2)}) collective-permute-start(bf16[32,2048]{1,0:T(8,128)(2,1)S(1)} %get-tuple-element.60), channel_id=1, source_target_pairs={{0,8},{1,9},{8,0},{9,1},{16,24},{17,25},{24,16},{25,17},{2,10},{3,... | collective-permute-start | bytes 393224 | tf_op jit(solution)/shard_map/ppermute | solution.py:570
  40.7 9.8 %collective-permute-start.21 = (bf16[64,2048]{1,0:T(8,128)(2,1)S(1)}, bf16[64,2048]{1,0:T(8,128)(2,1)S(1)}, u32[]{:S(2)}, u32[]{:S(2)}) collective-permute-start(bf16[64,2048]{1,0:T(8,128)(2,1)S(1)} %join.11), channel_id=1, source_target_pairs={{0,17},{1,16},{8,25},{9,24},{16,1},{17,0},{24,9},{25,8},{2,19},{3,... | collective-permute-start | bytes 786440 | tf_op jit(solution)/shard_map/ppermute | solution.py:570
  42.3 9.8 %collective-permute-start.7 = (bf16[128,1024]{1,0:T(8,128)(2,1)S(1)}, bf16[128,1024]{1,0:T(8,128)(2,1)S(1)}, u32[]{:S(2)}, u32[]{:S(2)}) collective-permute-start(bf16[128,1024]{1,0:T(8,128)(2,1)S(1)} %get-tuple-element.50.refs_2_), channel_id=1, source_target_pairs={{0,2},{2,0},{4,6},{6,4},{1,3},{3,1},{5,7},{7,5},{8,10},{10,8},{12,... | collective-permute-start | bytes 786440 | tf_op jit(solution)/shard_map/ppermute | solution.py:638
  46.6 7.2 %collective-permute-start.25 = (bf16[128,1024]{1,0:T(8,128)(2,1)S(1)}, bf16[128,1024]{1,0:T(8,128)(2,1)S(1)}, u32[]{:S(2)}, u32[]{:S(2)}) collective-permute-start(bf16[128,1024]{1,0:T(8,128)(2,1)S(1)} %add_term.16.refs_4_.refs_1_), channel_id=1, source_target_pairs={{0,8},{2,4},{4,2},{6,14},{8,0},{10,12},{12,10},{14,6},{16,24},{18,... | collective-permute-start | bytes 786440 | tf_op jit(solution)/shard_map/ppermute | solution.py:664
  46.9 11.8 %collective-permute-start.24 = (bf16[128,1024]{1,0:T(8,128)(2,1)S(1)}, bf16[128,1024]{1,0:T(8,128)(2,1)S(1)}, u32[]{:S(2)}, u32[]{:S(2)}) collective-permute-start(bf16[128,1024]{1,0:T(8,128)(2,1)S(1)} %get-tuple-element.65.refs_11_.refs_2_), channel_id=1, source_target_pairs={{0,2},{2,0},{4,6},{6,4},{1,3},{3,1},{5,7},{7,5},{8,10},{10,8},{12,... | collective-permute-start | bytes 786440 | tf_op jit(solution)/shard_map/ppermute | solution.py:638
  52.2 6.6 %collective-permute-start.27 = (bf16[128,1024]{1,0:T(8,128)(2,1)S(1)}, bf16[128,1024]{1,0:T(8,128)(2,1)S(1)}, u32[]{:S(2)}, u32[]{:S(2)}) collective-permute-start(bf16[128,1024]{1,0:T(8,128)(2,1)S(1)} %add_term.15.refs_2_.refs_4_.refs_1_), channel_id=1, source_target_pairs={{0,8},{2,4},{4,2},{6,14},{8,0},{10,12},{12,10},{14,6},{16,24},{18,... | collective-permute-start | bytes 786440 | tf_op jit(solution)/shard_map/ppermute | solution.py:664
  53.9 10.1 %collective-permute-start.28 = (bf16[128,1024]{1,0:T(8,128)(2,1)S(1)}, bf16[128,1024]{1,0:T(8,128)(2,1)S(1)}, u32[]{:S(2)}, u32[]{:S(2)}) collective-permute-start(bf16[128,1024]{1,0:T(8,128)(2,1)S(1)} %get-tuple-element.66.refs_2_), channel_id=1, source_target_pairs={{0,2},{2,0},{4,6},{6,4},{1,3},{3,1},{5,7},{7,5},{8,10},{10,8},{12,... | collective-permute-start | bytes 786440 | tf_op jit(solution)/shard_map/ppermute | solution.py:638
  58.8 7.4 %collective-permute-start.26 = (bf16[128,1024]{1,0:T(8,128)(2,1)S(1)}, bf16[128,1024]{1,0:T(8,128)(2,1)S(1)}, u32[]{:S(2)}, u32[]{:S(2)}) collective-permute-start(bf16[128,1024]{1,0:T(8,128)(2,1)S(1)} %add_term.17.refs_4_.refs_1_), channel_id=1, source_target_pairs={{0,8},{2,4},{4,2},{6,14},{8,0},{10,12},{12,10},{14,6},{16,24},{18,... | collective-permute-start | bytes 786440 | tf_op jit(solution)/shard_map/ppermute | solution.py:664
  59.0 11.6 %collective-permute-start.30 = (bf16[128,1024]{1,0:T(8,128)(2,1)S(1)}, bf16[128,1024]{1,0:T(8,128)(2,1)S(1)}, u32[]{:S(2)}, u32[]{:S(2)}) collective-permute-start(bf16[128,1024]{1,0:T(8,128)(2,1)S(1)} %get-tuple-element.67.refs_2_), channel_id=1, source_target_pairs={{0,2},{2,0},{4,6},{6,4},{1,3},{3,1},{5,7},{7,5},{8,10},{10,8},{12,... | collective-permute-start | bytes 786440 | tf_op jit(solution)/shard_map/ppermute | solution.py:638
  64.0 0.7 copy-start.3
  64.1 6.6 %collective-permute-start.29 = (bf16[128,1024]{1,0:T(8,128)(2,1)S(1)}, bf16[128,1024]{1,0:T(8,128)(2,1)S(1)}, u32[]{:S(2)}, u32[]{:S(2)}) collective-permute-start(bf16[128,1024]{1,0:T(8,128)(2,1)S(1)} %add_term.18.refs_4_.refs_1_), channel_id=1, source_target_pairs={{0,8},{2,4},{4,2},{6,14},{8,0},{10,12},{12,10},{14,6},{16,24},{18,... | collective-permute-start | bytes 786440 | tf_op jit(solution)/shard_map/ppermute | solution.py:664
  65.6 12.6 %collective-permute-start.9 = (bf16[64,2048]{1,0:T(8,128)(2,1)S(1)}, bf16[64,2048]{1,0:T(8,128)(2,1)S(1)}, u32[]{:S(2)}, u32[]{:S(2)}) collective-permute-start(bf16[64,2048]{1,0:T(8,128)(2,1)S(1)} %get-tuple-element.53), channel_id=1, source_target_pairs={{0,8},{1,9},{8,0},{9,1},{16,24},{17,25},{24,16},{25,17},{2,10},{3,... | collective-permute-start | bytes 786440 | tf_op jit(solution)/shard_map/ppermute | solution.py:570
  65.7 10.7 %collective-permute-start.11 = (bf16[64,2048]{1,0:T(8,128)(2,1)S(1)}, bf16[64,2048]{1,0:T(8,128)(2,1)S(1)}, u32[]{:S(2)}, u32[]{:S(2)}) collective-permute-start(bf16[64,2048]{1,0:T(8,128)(2,1)S(1)} %get-tuple-element.54), channel_id=1, source_target_pairs={{0,8},{1,9},{8,0},{9,1},{16,24},{17,25},{24,16},{25,17},{2,10},{3,... | collective-permute-start | bytes 786440 | tf_op jit(solution)/shard_map/ppermute | solution.py:570
  66.3 10.0 %collective-permute-start.32 = (bf16[128,1024]{1,0:T(8,128)(2,1)S(1)}, bf16[128,1024]{1,0:T(8,128)(2,1)S(1)}, u32[]{:S(2)}, u32[]{:S(2)}) collective-permute-start(bf16[128,1024]{1,0:T(8,128)(2,1)S(1)} %get-tuple-element.68.refs_2_), channel_id=1, source_target_pairs={{0,2},{2,0},{4,6},{6,4},{1,3},{3,1},{5,7},{7,5},{8,10},{10,8},{12,... | collective-permute-start | bytes 786440 | tf_op jit(solution)/shard_map/ppermute | solution.py:638
  70.8 10.4 %collective-permute-start.31 = (bf16[128,1024]{1,0:T(8,128)(2,1)S(1)}, bf16[128,1024]{1,0:T(8,128)(2,1)S(1)}, u32[]{:S(2)}, u32[]{:S(2)}) collective-permute-start(bf16[128,1024]{1,0:T(8,128)(2,1)S(1)} %get-tuple-element.69.refs_2_), channel_id=1, source_target_pairs={{0,2},{2,0},{4,6},{6,4},{1,3},{3,1},{5,7},{7,5},{8,10},{10,8},{12,... | collective-permute-start | bytes 786440 | tf_op jit(solution)/shard_map/ppermute | solution.py:638
  74.8 6.7 %collective-permute-start.33 = (bf16[128,1024]{1,0:T(8,128)(2,1)S(1)}, bf16[128,1024]{1,0:T(8,128)(2,1)S(1)}, u32[]{:S(2)}, u32[]{:S(2)}) collective-permute-start(bf16[128,1024]{1,0:T(8,128)(2,1)S(1)} %add_term.19.refs_4_.refs_1_), channel_id=1, source_target_pairs={{0,8},{2,4},{4,2},{6,14},{8,0},{10,12},{12,10},{14,6},{16,24},{18,... | collective-permute-start | bytes 786440 | tf_op jit(solution)/shard_map/ppermute | solution.py:664
  76.3 5.9 %collective-permute-start.39 = (bf16[128,1024]{1,0:T(8,128)(2,1)S(1)}, bf16[128,1024]{1,0:T(8,128)(2,1)S(1)}, u32[]{:S(2)}, u32[]{:S(2)}) collective-permute-start(bf16[128,1024]{1,0:T(8,128)(2,1)S(1)} %add_term.21.refs_4_.refs_0_), channel_id=1, source_target_pairs={{0,8},{2,4},{4,2},{6,14},{8,0},{10,12},{12,10},{14,6},{16,24},{18,... | collective-permute-start | bytes 786440 | tf_op jit(solution)/shard_map/ppermute | solution.py:664
  76.4 14.4 %collective-permute-start.12 = (bf16[128,2048]{1,0:T(8,128)(2,1)S(1)}, bf16[128,2048]{1,0:T(8,128)(2,1)S(1)}, u32[]{:S(2)}, u32[]{:S(2)}) collective-permute-start(bf16[128,2048]{1,0:T(8,128)(2,1)S(1)} %join.7), channel_id=1, source_target_pairs={{0,16},{1,17},{8,24},{9,25},{16,0},{17,1},{24,8},{25,9},{2,18},{3,... | collective-permute-start | bytes 1572872 | tf_op jit(solution)/shard_map/ppermute | solution.py:570
  78.2 14.1 %collective-permute-start.10 = (bf16[128,2048]{1,0:T(8,128)(2,1)S(1)}, bf16[128,2048]{1,0:T(8,128)(2,1)S(1)}, u32[]{:S(2)}, u32[]{:S(2)}) collective-permute-start(bf16[128,2048]{1,0:T(8,128)(2,1)S(1)} %join.6), channel_id=1, source_target_pairs={{0,1},{1,0},{8,9},{9,8},{16,17},{17,16},{24,25},{25,24},{2,3},{3,2... | collective-permute-start | bytes 1572872 | tf_op jit(solution)/shard_map/ppermute | solution.py:570
  81.2 9.1 %collective-permute-start.13 = (bf16[64,2048]{1,0:T(8,128)(2,1)S(1)}, bf16[64,2048]{1,0:T(8,128)(2,1)S(1)}, u32[]{:S(2)}, u32[]{:S(2)}) collective-permute-start(bf16[64,2048]{1,0:T(8,128)(2,1)S(1)} %get-tuple-element.55), channel_id=1, source_target_pairs={{0,8},{1,9},{8,0},{9,1},{16,24},{17,25},{24,16},{25,17},{2,10},{3,... | collective-permute-start | bytes 786440 | tf_op jit(solution)/shard_map/ppermute | solution.py:570
  81.5 7.6 %copy-start = (bf16[256,5120]{1,0:T(8,128)(2,1)S(1)}, bf16[256,5120]{1,0:T(8,128)(2,1)}, u32[]{:S(2)}) copy-start(bf16[256,5120]{1,0:T(8,128)(2,1)} %get-tuple-element.71.refs_2_) | copy-start | bytes 7864324
  81.5 13.3 %collective-permute-start.36 = (bf16[128,1024]{1,0:T(8,128)(2,1)S(1)}, bf16[128,1024]{1,0:T(8,128)(2,1)S(1)}, u32[]{:S(2)}, u32[]{:S(2)}) collective-permute-start(bf16[128,1024]{1,0:T(8,128)(2,1)S(1)} %add_term.20.refs_8_.refs_7_.refs_0_.refs_2_), channel_id=1, source_target_pairs={{0,8},{2,4},{4,2},{6,14},{8,0},{10,12},{12,10},{14,6},{16,24},{18,... | collective-permute-start | bytes 786440 | tf_op jit(solution)/shard_map/ppermute | solution.py:664
  82.2 12.4 %collective-permute-start.34 = (bf16[128,1024]{1,0:T(8,128)(2,1)S(1)}, bf16[128,1024]{1,0:T(8,128)(2,1)S(1)}, u32[]{:S(2)}, u32[]{:S(2)}) collective-permute-start(bf16[128,1024]{1,0:T(8,128)(2,1)S(1)} %get-tuple-element.73), channel_id=1, source_target_pairs={{0,2},{2,0},{4,6},{6,4},{1,3},{3,1},{5,7},{7,5},{8,10},{10,8},{12,... | collective-permute-start | bytes 786440 | tf_op jit(solution)/shard_map/ppermute | solution.py:638
  90.3 14.6 %collective-permute-start.8 = (bf16[64,2048]{1,0:T(8,128)(2,1)S(1)}, bf16[64,2048]{1,0:T(8,128)(2,1)S(1)}, u32[]{:S(2)}, u32[]{:S(2)}) collective-permute-start(bf16[64,2048]{1,0:T(8,128)(2,1)S(1)} %get-tuple-element.52), channel_id=1, source_target_pairs={{0,8},{1,9},{8,0},{9,1},{16,24},{17,25},{24,16},{25,17},{2,10},{3,... | collective-permute-start | bytes 786440 | tf_op jit(solution)/shard_map/ppermute | solution.py:570
  90.8 13.0 %collective-permute-start.40 = (bf16[128,1024]{1,0:T(8,128)(2,1)S(1)}, bf16[128,1024]{1,0:T(8,128)(2,1)S(1)}, u32[]{:S(2)}, u32[]{:S(2)}) collective-permute-start(bf16[128,1024]{1,0:T(8,128)(2,1)S(1)} %add_term.25.refs_5_), channel_id=1, source_target_pairs={{0,2},{2,0},{4,6},{6,4},{1,3},{3,1},{5,7},{7,5},{8,10},{10,8},{12,... | collective-permute-start | bytes 786440 | tf_op jit(solution)/shard_map/ppermute | solution.py:638
  92.3 14.2 %collective-permute-start.14 = (bf16[128,2048]{1,0:T(8,128)(2,1)S(1)}, bf16[128,2048]{1,0:T(8,128)(2,1)S(1)}, u32[]{:S(2)}, u32[]{:S(2)}) collective-permute-start(bf16[128,2048]{1,0:T(8,128)(2,1)S(1)} %join.8), channel_id=1, source_target_pairs={{0,17},{1,16},{8,25},{9,24},{16,1},{17,0},{24,9},{25,8},{2,19},{3,... | collective-permute-start | bytes 1572872 | tf_op jit(solution)/shard_map/ppermute | solution.py:570
  94.7 4.9 %collective-permute-start.35 = (bf16[128,1024]{1,0:T(8,128)(2,1)S(1)}, bf16[128,1024]{1,0:T(8,128)(2,1)S(1)}, u32[]{:S(2)}, u32[]{:S(2)}) collective-permute-start(bf16[128,1024]{1,0:T(8,128)(2,1)S(1)} %add_term.22.refs_2_.refs_0_), channel_id=1, source_target_pairs={{0,8},{2,4},{4,2},{6,14},{8,0},{10,12},{12,10},{14,6},{16,24},{18,... | collective-permute-start | bytes 786440 | tf_op jit(solution)/shard_map/ppermute | solution.py:664
  94.9 13.8 %collective-permute-start.38 = (bf16[128,1024]{1,0:T(8,128)(2,1)S(1)}, bf16[128,1024]{1,0:T(8,128)(2,1)S(1)}, u32[]{:S(2)}, u32[]{:S(2)}) collective-permute-start(bf16[128,1024]{1,0:T(8,128)(2,1)S(1)} %add_term.23.refs_8_.refs_5_), channel_id=1, source_target_pairs={{0,2},{2,0},{4,6},{6,4},{1,3},{3,1},{5,7},{7,5},{8,10},{10,8},{12,... | collective-permute-start | bytes 786440 | tf_op jit(solution)/shard_map/ppermute | solution.py:638
  99.7 10.7 %collective-permute-start.37 = (bf16[128,1024]{1,0:T(8,128)(2,1)S(1)}, bf16[128,1024]{1,0:T(8,128)(2,1)S(1)}, u32[]{:S(2)}, u32[]{:S(2)}) collective-permute-start(bf16[128,1024]{1,0:T(8,128)(2,1)S(1)} %add_term.24.refs_5_), channel_id=1, source_target_pairs={{0,2},{2,0},{4,6},{6,4},{1,3},{3,1},{5,7},{7,5},{8,10},{10,8},{12,... | collective-permute-start | bytes 786440 | tf_op jit(solution)/shard_map/ppermute | solution.py:638
  103.8 2.7 %copy-start.1 = (s32[512]{0:T(512)S(1)}, s32[512]{0:T(512)}, u32[]{:S(2)}) copy-start(s32[512]{0:T(512)} %param.11) | copy-start | bytes 6148
  103.8 2.7 %copy-start.2 = (bf16[512,2048]{1,0:T(8,128)(2,1)S(1)}, bf16[512,2048]{1,0:T(8,128)(2,1)}, u32[]{:S(2)}) copy-start(bf16[512,2048]{1,0:T(8,128)(2,1)} %refs_2_.1) | copy-start | bytes 6291460

commit v4 on v3

--- a/solution.py
+++ b/solution.py
@@ -18,7 +18,7 @@
 NODE = 800_000_000
 TAKE = 3_200_000_000
 PLACE = 6_400_000_000
-FINISH = 2_000_000_000
+FINISH = 1_000_000_000
 PRODUCT = 400_000_000
 
 
@@ -671,7 +671,8 @@
             )
             to_pair(ahead, send[ahead])
         else:
-            totals[j - 1] = add_term(halves[j - 1], from_far[j - 1], (halves[j],))
+            weight = {chunks - 2: 4, chunks - 1: 2}.get(j, 1)
+            totals[j - 1] = add_term(halves[j - 1], from_far[j - 1], (halves[j],), weight)
             to_pair(ahead, totals[j - 1])
     grad_pre = finish_block(1, grad_pre, totals[chunks - 2])
     totals[chunks - 1] = add_term(halves[chunks - 1], from_far[chunks - 1], (grad_pre,))

time: 112 us -> 108 us (0.964)
  waiting for transfers between devices: 16.8 us -> 12.5 us
    ppermute x13, waiting for transfers between devices: 9.96 us -> 5.36 us  [to_pair(): from_pair[j] = lax.ppermute(value, 'tp', outer_pairs)]
  transfers between devices with their start and end apart: 41 -> 41, of which waited for: 13 -> 10; matrix products, arithmetic and copies ran while one was open for 0% -> 0% of each run, Pallas kernels for 32% -> 33%
where the time goes in v4:
time: 108 us
  starting transfers between devices  52.7 us (49%)
  Pallas kernels  40.8 us (38%)
  waiting for transfers between devices  12.5 us (12%)
  between operations  1.43 us (1%)
    pallas_call x50, Pallas kernels, call(): pl.pallas_call(body, out_shape=out_shape, in_specs=list(in_specs) + [ANY]...  40.8 us
    ppermute x13, starting transfers between devices, to_pair(): from_pair[j] = lax.ppermute(value, 'tp', outer_pairs)  37.8 us
    ppermute x18, starting transfers between devices, exchange(): return lax.ppermute(piece, GROUP_AXES, [(i, i ^ k) for i in range(groups)])  14.2 us
    ppermute x18, waiting for transfers between devices, exchange(): return lax.ppermute(piece, GROUP_AXES, [(i, i ^ k) for i in range(groups)])  7.09 us
    ppermute x13, waiting for transfers between devices, to_pair(): from_pair[j] = lax.ppermute(value, 'tp', outer_pairs)  5.36 us
  transfers between devices with their start and end apart: 41, of which 10 were waited for; matrix products, arithmetic and copies ran while one was open for 0% of the time, Pallas kernels for 33%

profile of v4, /device:TPU:0, one launch (start us, length us, event | category | flops | bytes accessed | tf_op | source)
XLA Modules:
  0.0 108.0 jit_solution(10397844141535256668)
XLA Ops:
  0.6 2.3 %pack_context.1 = (bf16[64,2048]{1,0:T(8,128)(2,1)S(1)}, bf16[64,2048]{1,0:T(8,128)(2,1)S(1)}, bf16[64,2048]{1,0:T(8,128)(2,1)S(1)}, bf16[64,2048]{1,0:T(8,128)(2,1)S(1)}, bf16[512,2048]{1,0:T(8,128)(2,1)S(1)}) custom-call(s32[1]{0:T(128)} %bitcast.1.refs_0_, s32[1]{0:T(128)} %bitcast.3.refs_1_.refs_0_, s32[1,512]{1,0:T(1,128)} %bitcast.4, ...), custom_call_target="tpu_custom_call" | custom-call | flops 1000 | bytes 3 | tf_op jit(solution)/shard_map/pack_context/pallas_call | solution.py:111
  3.0 3.0 %collective-permute-start.1 = (bf16[64,2048]{1,0:T(8,128)(2,1)S(1)}, bf16[64,2048]{1,0:T(8,128)(2,1)S(1)}, u32[]{:S(2)}, u32[]{:S(2)}) collective-permute-start(bf16[64,2048]{1,0:T(8,128)(2,1)S(1)} %get-tuple-element.47), channel_id=1, source_target_pairs={{0,16},{1,17},{8,24},{9,25},{16,0},{17,1},{24,8},{25,9},{2,18},{3,... | collective-permute-start | bytes 786440 | tf_op jit(solution)/shard_map/ppermute | solution.py:570
  6.0 1.5 %collective-permute-start.2 = (bf16[64,2048]{1,0:T(8,128)(2,1)S(1)}, bf16[64,2048]{1,0:T(8,128)(2,1)S(1)}, u32[]{:S(2)}, u32[]{:S(2)}) collective-permute-start(bf16[64,2048]{1,0:T(8,128)(2,1)S(1)} %get-tuple-element.48), channel_id=1, source_target_pairs={{0,17},{1,16},{8,25},{9,24},{16,1},{17,0},{24,9},{25,8},{2,19},{3,... | collective-permute-start | bytes 786440 | tf_op jit(solution)/shard_map/ppermute | solution.py:570
  7.5 11.0 %prepare.1 = (bf16[128,256]{1,0:T(8,128)(2,1)S(1)}, bf16[256,512]{1,0:T(8,128)(2,1)S(1)}, bf16[256,256]{1,0:T(8,128)(2,1)S(1)}, bf16[256,512]{1,0:T(8,128)(2,1)S...) custom-call(s32[1]{0:T(128)} %bitcast.1.refs_0_, ...), custom_call_target="tpu_custom_call" | custom-call | flops 10737418240 | bytes 35791392 | tf_op jit(solution)/shard_map/prepare/pallas_call | solution.py:111
  18.5 0.7 collective-permute-done.2.refs_3_.refs_4_
  19.2 1.4 %collective-permute-done.refs_1_.refs_2_ = bf16[64,2048]{1,0:T(8,128)(2,1)S(1)} collective-permute-done((bf16[64,2048]{1,0:T(8,128)(2,1)S(1)}, bf16[64,2048]{1,0:T(8,128)(2,1)S(1)}, u32[]{:S(2)}, u32[]{:S(2)}) %collective-permute-start) | collective-permute-done | bytes 262176 | tf_op jit(solution)/shard_map/ppermute | solution.py:570
  20.7 1.9 %collective-permute-done.3.refs_5_ = bf16[128,2048]{1,0:T(8,128)(2,1)S(1)} collective-permute-done((bf16[128,2048]{1,0:T(8,128)(2,1)S(1)}, bf16[128,2048]{1,0:T(8,128)(2,1)S(1)}, u32[]{:S(2)}, u32[]{:S(2)}) %collective-permute-start.3) | collective-permute-done | bytes 524320 | tf_op jit(solution)/shard_map/ppermute | solution.py:570
  22.6 0.3 take_rows.2.refs_0_
  22.9 1.5 %back_product.10.refs_2_.refs_0_ = bf16[128,1024]{1,0:T(8,128)(2,1)S(1)} custom-call(bf16[128,2048]{1,0:T(8,128)(2,1)S(1)} %take_rows.2.refs_0_, bf16[5120,2048]{1,0:T(8,128)(2,1)S(1)} %get-tuple-element.49.refs_1_), custom_call_target="tpu_custom_call" | custom-call | flops 400000000 | bytes 1333333 | tf_op jit(solution)/shard_map/back_product/pallas_call | solution.py:111
  24.4 1.6 %collective-permute-start.4 = (bf16[128,1024]{1,0:T(8,128)(2,1)S(1)}, bf16[128,1024]{1,0:T(8,128)(2,1)S(1)}, u32[]{:S(2)}, u32[]{:S(2)}) collective-permute-start(bf16[128,1024]{1,0:T(8,128)(2,1)S(1)} %back_product.10.refs_2_.refs_0_), channel_id=1, source_target_pairs={{0,2},{2,0},{4,6},{6,4},{1,3},{3,1},{5,7},{7,5},{8,10},{10,8},{12,... | collective-permute-start | bytes 786440 | tf_op jit(solution)/shard_map/ppermute | solution.py:638
  26.1 1.5 %back_product.11.refs_2_.refs_0_ = bf16[128,1024]{1,0:T(8,128)(2,1)S(1)} custom-call(bf16[128,2048]{1,0:T(8,128)(2,1)S(1)} %take_rows.2.refs_0_, bf16[5120,2048]{1,0:T(8,128)(2,1)S(1)} %get-tuple-element.49.refs_1_, bf16[128,1024]{1,0:T(8,128)(2,1)S(1)} %back_product.10.refs_2_.refs_0_), custom_call_target="tpu_custom_call" | custom-call | flops 400000000 | bytes 1333333 | tf_op jit(solution)/shard_map/back_product/pallas_call | solution.py:111
  27.6 0.9 split_rows.3
  28.6 0.5 collective-permute-start.16
  29.1 0.4 collective-permute-start.6
  29.5 1.5 %back_product.12.refs_2_.refs_0_ = bf16[128,1024]{1,0:T(8,128)(2,1)S(1)} custom-call(bf16[128,2048]{1,0:T(8,128)(2,1)S(1)} %take_rows.2.refs_0_, bf16[5120,2048]{1,0:T(8,128)(2,1)S(1)} %get-tuple-element.49.refs_1_, bf16[128,1024]{1,0:T(8,128)(2,1)S(1)} %back_product.11.refs_2_.refs_0_), custom_call_target="tpu_custom_call" | custom-call | flops 400000000 | bytes 1333333 | tf_op jit(solution)/shard_map/back_product/pallas_call | solution.py:111
  31.1 1.6 %collective-permute-start.19 = (bf16[64,2048]{1,0:T(8,128)(2,1)S(1)}, bf16[64,2048]{1,0:T(8,128)(2,1)S(1)}, u32[]{:S(2)}, u32[]{:S(2)}) collective-permute-start(bf16[64,2048]{1,0:T(8,128)(2,1)S(1)} %join.10), channel_id=1, source_target_pairs={{0,16},{1,17},{8,24},{9,25},{16,0},{17,1},{24,8},{25,9},{2,18},{3,... | collective-permute-start | bytes 786440 | tf_op jit(solution)/shard_map/ppermute | solution.py:570
  32.7 0.6 collective-permute-start.17
  33.2 0.4 collective-permute-done.4.refs_1_
  33.8 0.5 collective-permute-start.20
  34.3 1.5 %back_product.13.refs_2_.refs_3_.refs_0_ = bf16[128,1024]{1,0:T(8,128)(2,1)S(1)} custom-call(bf16[128,2048]{1,0:T(8,128)(2,1)S(1)} %take_rows.2.refs_0_, bf16[5120,2048]{1,0:T(8,128)(2,1)S(1)} %get-tuple-element.49.refs_1_, bf16[128,1024]{1,0:T(8,128)(2,1)S(1)} %back_product.12.refs_2_.refs_0_), custom_call_target="tpu_custom_call" | custom-call | flops 400000000 | bytes 1333333 | tf_op jit(solution)/shard_map/back_product/pallas_call | solution.py:111
  35.8 2.7 %collective-permute-done.6.refs_1_ = bf16[128,1024]{1,0:T(8,128)(2,1)S(1)} collective-permute-done((bf16[128,1024]{1,0:T(8,128)(2,1)S(1)}, bf16[128,1024]{1,0:T(8,128)(2,1)S(1)}, u32[]{:S(2)}, u32[]{:S(2)}) %collective-permute-start.6) | collective-permute-done | bytes 262176 | tf_op jit(solution)/shard_map/ppermute | solution.py:638
  38.5 1.6 %collective-permute-start.23 = (bf16[128,1024]{1,0:T(8,128)(2,1)S(1)}, bf16[128,1024]{1,0:T(8,128)(2,1)S(1)}, u32[]{:S(2)}, u32[]{:S(2)}) collective-permute-start(bf16[128,1024]{1,0:T(8,128)(2,1)S(1)} %back_product.12.refs_2_.refs_0_), channel_id=1, source_target_pairs={{0,2},{2,0},{4,6},{6,4},{1,3},{3,1},{5,7},{7,5},{8,10},{10,8},{12,... | collective-permute-start | bytes 786440 | tf_op jit(solution)/shard_map/ppermute | solution.py:638
  40.2 0.5 collective-permute-start.15
  40.7 1.5 %collective-permute-start.21 = (bf16[64,2048]{1,0:T(8,128)(2,1)S(1)}, bf16[64,2048]{1,0:T(8,128)(2,1)S(1)}, u32[]{:S(2)}, u32[]{:S(2)}) collective-permute-start(bf16[64,2048]{1,0:T(8,128)(2,1)S(1)} %join.11), channel_id=1, source_target_pairs={{0,17},{1,16},{8,25},{9,24},{16,1},{17,0},{24,9},{25,8},{2,19},{3,... | collective-permute-start | bytes 786440 | tf_op jit(solution)/shard_map/ppermute | solution.py:570
  42.3 2.7 %collective-permute-start.7 = (bf16[128,1024]{1,0:T(8,128)(2,1)S(1)}, bf16[128,1024]{1,0:T(8,128)(2,1)S(1)}, u32[]{:S(2)}, u32[]{:S(2)}) collective-permute-start(bf16[128,1024]{1,0:T(8,128)(2,1)S(1)} %get-tuple-element.50.refs_2_), channel_id=1, source_target_pairs={{0,2},{2,0},{4,6},{6,4},{1,3},{3,1},{5,7},{7,5},{8,10},{10,8},{12,... | collective-permute-start | bytes 786440 | tf_op jit(solution)/shard_map/ppermute | solution.py:638
  45.1 1.5 %back_product.14.refs_2_.refs_3_.refs_0_ = bf16[128,1024]{1,0:T(8,128)(2,1)S(1)} custom-call(bf16[128,2048]{1,0:T(8,128)(2,1)S(1)} %take_rows.2.refs_0_, bf16[5120,2048]{1,0:T(8,128)(2,1)S(1)} %get-tuple-element.49.refs_1_, bf16[128,1024]{1,0:T(8,128)(2,1)S(1)} %get-tuple-element.50.refs_2_), custom_call_target="tpu_custom_call" | custom-call | flops 400000000 | bytes 1333333 | tf_op jit(solution)/shard_map/back_product/pallas_call | solution.py:111
  46.7 0.1 add_and_choose.8
  46.9 3.7 %collective-permute-start.24 = (bf16[128,1024]{1,0:T(8,128)(2,1)S(1)}, bf16[128,1024]{1,0:T(8,128)(2,1)S(1)}, u32[]{:S(2)}, u32[]{:S(2)}) collective-permute-start(bf16[128,1024]{1,0:T(8,128)(2,1)S(1)} %get-tuple-element.65.refs_11_.refs_2_), channel_id=1, source_target_pairs={{0,2},{2,0},{4,6},{6,4},{1,3},{3,1},{5,7},{7,5},{8,10},{10,8},{12,... | collective-permute-start | bytes 786440 | tf_op jit(solution)/shard_map/ppermute | solution.py:638
  50.6 0.7 take_rows.3.refs_0_
  51.3 0.8 collective-permute-done.7.refs_1_.refs_4_
  52.3 1.5 %back_product.15.refs_3_.refs_0_ = bf16[128,1024]{1,0:T(8,128)(2,1)S(1)} custom-call(bf16[256,2048]{1,0:T(8,128)(2,1)S(1)} %take_rows.3.refs_0_, bf16[5120,2048]{1,0:T(8,128)(2,1)S(1)} %get-tuple-element.49.refs_1_, bf16[128,1024]{1,0:T(8,128)(2,1)S(1)} %get-tuple-element.65.refs_11_.refs_2_), custom_call_target="tpu_custom_call" | custom-call | flops 400000000 | bytes 1333333 | tf_op jit(solution)/shard_map/back_product/pallas_call | solution.py:111
  53.9 3.3 %collective-permute-start.28 = (bf16[128,1024]{1,0:T(8,128)(2,1)S(1)}, bf16[128,1024]{1,0:T(8,128)(2,1)S(1)}, u32[]{:S(2)}, u32[]{:S(2)}) collective-permute-start(bf16[128,1024]{1,0:T(8,128)(2,1)S(1)} %get-tuple-element.66.refs_2_), channel_id=1, source_target_pairs={{0,2},{2,0},{4,6},{6,4},{1,3},{3,1},{5,7},{7,5},{8,10},{10,8},{12,... | collective-permute-start | bytes 786440 | tf_op jit(solution)/shard_map/ppermute | solution.py:638
  57.2 1.5 %back_product.16.refs_2_.refs_3_.refs_0_ = bf16[128,1024]{1,0:T(8,128)(2,1)S(1)} custom-call(bf16[256,2048]{1,0:T(8,128)(2,1)S(1)} %take_rows.3.refs_0_, bf16[5120,2048]{1,0:T(8,128)(2,1)S(1)} %get-tuple-element.49.refs_1_, bf16[128,1024]{1,0:T(8,128)(2,1)S(1)} %get-tuple-element.66.refs_2_), custom_call_target="tpu_custom_call" | custom-call | flops 400000000 | bytes 1333333 | tf_op jit(solution)/shard_map/back_product/pallas_call | solution.py:111
  59.0 3.5 %collective-permute-start.30 = (bf16[128,1024]{1,0:T(8,128)(2,1)S(1)}, bf16[128,1024]{1,0:T(8,128)(2,1)S(1)}, u32[]{:S(2)}, u32[]{:S(2)}) collective-permute-start(bf16[128,1024]{1,0:T(8,128)(2,1)S(1)} %get-tuple-element.67.refs_2_), channel_id=1, source_target_pairs={{0,2},{2,0},{4,6},{6,4},{1,3},{3,1},{5,7},{7,5},{8,10},{10,8},{12,... | collective-permute-start | bytes 786440 | tf_op jit(solution)/shard_map/ppermute | solution.py:638
  62.5 0.1 round_merged.1.refs_1_
  62.6 0.7 split_rows.2
  63.4 0.5 collective-permute-start.11
  63.9 1.5 %back_product.17.refs_2_.refs_3_.refs_0_ = bf16[128,1024]{1,0:T(8,128)(2,1)S(1)} custom-call(bf16[256,2048]{1,0:T(8,128)(2,1)S(1)} %take_rows.3.refs_0_, bf16[5120,2048]{1,0:T(8,128)(2,1)S(1)} %get-tuple-element.49.refs_1_, bf16[128,1024]{1,0:T(8,128)(2,1)S(1)} %get-tuple-element.67.refs_2_), custom_call_target="tpu_custom_call" | custom-call | flops 400000000 | bytes 1333333 | tf_op jit(solution)/shard_map/back_product/pallas_call | solution.py:111
  65.5 0.1 collective-permute-start.29
  65.7 0.1 add_and_choose.11
  65.8 1.9 %collective-permute-start.32 = (bf16[128,1024]{1,0:T(8,128)(2,1)S(1)}, bf16[128,1024]{1,0:T(8,128)(2,1)S(1)}, u32[]{:S(2)}, u32[]{:S(2)}) collective-permute-start(bf16[128,1024]{1,0:T(8,128)(2,1)S(1)} %get-tuple-element.68.refs_2_), channel_id=1, source_target_pairs={{0,2},{2,0},{4,6},{6,4},{1,3},{3,1},{5,7},{7,5},{8,10},{10,8},{12,... | collective-permute-start | bytes 786440 | tf_op jit(solution)/shard_map/ppermute | solution.py:638
  67.7 1.5 %back_product.18.refs_2_.refs_3_.refs_0_ = bf16[128,1024]{1,0:T(8,128)(2,1)S(1)} custom-call(bf16[256,2048]{1,0:T(8,128)(2,1)S(1)} %take_rows.3.refs_0_, bf16[5120,2048]{1,0:T(8,128)(2,1)S(1)} %get-tuple-element.49.refs_1_, bf16[128,1024]{1,0:T(8,128)(2,1)S(1)} %get-tuple-element.68.refs_2_), custom_call_target="tpu_custom_call" | custom-call | flops 400000000 | bytes 1333333 | tf_op jit(solution)/shard_map/back_product/pallas_call | solution.py:111
  69.4 1.7 %collective-permute-start.12 = (bf16[128,2048]{1,0:T(8,128)(2,1)S(1)}, bf16[128,2048]{1,0:T(8,128)(2,1)S(1)}, u32[]{:S(2)}, u32[]{:S(2)}) collective-permute-start(bf16[128,2048]{1,0:T(8,128)(2,1)S(1)} %join.7), channel_id=1, source_target_pairs={{0,16},{1,17},{8,24},{9,25},{16,0},{17,1},{24,8},{25,9},{2,18},{3,... | collective-permute-start | bytes 1572872 | tf_op jit(solution)/shard_map/ppermute | solution.py:570
  71.2 0.4 collective-permute-start.10
  71.6 0.1 add_and_choose.12
  71.7 3.9 %collective-permute-start.31 = (bf16[128,1024]{1,0:T(8,128)(2,1)S(1)}, bf16[128,1024]{1,0:T(8,128)(2,1)S(1)}, u32[]{:S(2)}, u32[]{:S(2)}) collective-permute-start(bf16[128,1024]{1,0:T(8,128)(2,1)S(1)} %get-tuple-element.69.refs_2_), channel_id=1, source_target_pairs={{0,2},{2,0},{4,6},{6,4},{1,3},{3,1},{5,7},{7,5},{8,10},{10,8},{12,... | collective-permute-start | bytes 786440 | tf_op jit(solution)/shard_map/ppermute | solution.py:638
  75.6 1.5 %back_product.19.refs_2_.refs_3_.refs_0_ = bf16[128,1024]{1,0:T(8,128)(2,1)S(1)} custom-call(bf16[256,2048]{1,0:T(8,128)(2,1)S(1)} %take_rows.3.refs_0_, bf16[5120,2048]{1,0:T(8,128)(2,1)S(1)} %get-tuple-element.49.refs_1_, bf16[128,1024]{1,0:T(8,128)(2,1)S(1)} %get-tuple-element.69.refs_2_), custom_call_target="tpu_custom_call" | custom-call | flops 400000000 | bytes 1333333 | tf_op jit(solution)/shard_map/back_product/pallas_call | solution.py:111
  77.5 2.5 %collective-permute-start.34 = (bf16[128,1024]{1,0:T(8,128)(2,1)S(1)}, bf16[128,1024]{1,0:T(8,128)(2,1)S(1)}, u32[]{:S(2)}, u32[]{:S(2)}) collective-permute-start(bf16[128,1024]{1,0:T(8,128)(2,1)S(1)} %get-tuple-element.73), channel_id=1, source_target_pairs={{0,2},{2,0},{4,6},{6,4},{1,3},{3,1},{5,7},{7,5},{8,10},{10,8},{12,... | collective-permute-start | bytes 786440 | tf_op jit(solution)/shard_map/ppermute | solution.py:638
  79.9 0.4 collective-permute-done.31.refs_1_.refs_6_
  80.5 1.1 %finish.5.refs_2_.refs_7_ = bf16[256,5120]{1,0:T(8,128)(2,1)} custom-call(s32[1]{0:T(128)} %bitcast.3.refs_1_.refs_0_, bf16[256,256]{1,0:T(8,128)(2,1)S(1)} %get-tuple-element.70.refs_1_, bf16[256,5120]{1,0:T(8,128)(2,1)S(1)} %copy-done, bf16[128,1024]{1,0:T(8,128)(2,1)S(1)} %get-tuple-element.74.refs_3_, ...), custom_call_target="tpu_custom_call" | custom-call | flops 1000000000 | bytes 3333333 | tf_op jit(solution)/shard_map/finish/pallas_call | solution.py:111
  81.6 0.6 collective-permute-start.8
  82.2 1.6 %collective-permute-done.12.refs_3_.refs_6_ = bf16[128,2048]{1,0:T(8,128)(2,1)S(1)} collective-permute-done((bf16[128,2048]{1,0:T(8,128)(2,1)S(1)}, bf16[128,2048]{1,0:T(8,128)(2,1)S(1)}, u32[]{:S(2)}, u32[]{:S(2)}) %collective-permute-start.12) | collective-permute-done | bytes 524320 | tf_op jit(solution)/shard_map/ppermute | solution.py:570
  83.8 1.5 %collective-permute-done.10.refs_2_.refs_5_ = bf16[128,2048]{1,0:T(8,128)(2,1)S(1)} collective-permute-done((bf16[128,2048]{1,0:T(8,128)(2,1)S(1)}, bf16[128,2048]{1,0:T(8,128)(2,1)S(1)}, u32[]{:S(2)}, u32[]{:S(2)}) %collective-permute-start.10) | collective-permute-done | bytes 524320 | tf_op jit(solution)/shard_map/ppermute | solution.py:570
  85.3 1.1 %collective-permute-start.14 = (bf16[128,2048]{1,0:T(8,128)(2,1)S(1)}, bf16[128,2048]{1,0:T(8,128)(2,1)S(1)}, u32[]{:S(2)}, u32[]{:S(2)}) collective-permute-start(bf16[128,2048]{1,0:T(8,128)(2,1)S(1)} %join.8), channel_id=1, source_target_pairs={{0,17},{1,16},{8,25},{9,24},{16,1},{17,0},{24,9},{25,8},{2,19},{3,... | collective-permute-start | bytes 1572872 | tf_op jit(solution)/shard_map/ppermute | solution.py:570
  86.7 3.3 %collective-permute-start.40 = (bf16[128,1024]{1,0:T(8,128)(2,1)S(1)}, bf16[128,1024]{1,0:T(8,128)(2,1)S(1)}, u32[]{:S(2)}, u32[]{:S(2)}) collective-permute-start(bf16[128,1024]{1,0:T(8,128)(2,1)S(1)} %add_term.25.refs_5_), channel_id=1, source_target_pairs={{0,2},{2,0},{4,6},{6,4},{1,3},{3,1},{5,7},{7,5},{8,10},{10,8},{12,... | collective-permute-start | bytes 786440 | tf_op jit(solution)/shard_map/ppermute | solution.py:638
  90.1 5.5 %collective-permute-start.38 = (bf16[128,1024]{1,0:T(8,128)(2,1)S(1)}, bf16[128,1024]{1,0:T(8,128)(2,1)S(1)}, u32[]{:S(2)}, u32[]{:S(2)}) collective-permute-start(bf16[128,1024]{1,0:T(8,128)(2,1)S(1)} %add_term.23.refs_8_.refs_5_), channel_id=1, source_target_pairs={{0,2},{2,0},{4,6},{6,4},{1,3},{3,1},{5,7},{7,5},{8,10},{10,8},{12,... | collective-permute-start | bytes 786440 | tf_op jit(solution)/shard_map/ppermute | solution.py:638
  95.6 1.1 %finish.6.refs_2_.refs_7_ = bf16[256,5120]{1,0:T(8,128)(2,1)} custom-call(s32[1]{0:T(128)} %bitcast.3.refs_1_.refs_0_, bf16[256,256]{1,0:T(8,128)(2,1)S(1)} %get-tuple-element.70.refs_1_, bf16[256,5120]{1,0:T(8,128)(2,1)S(1)} %copy-done, bf16[128,1024]{1,0:T(8,128)(2,1)S(1)} %get-tuple-element.76.refs_3_, ...), custom_call_target="tpu_custom_call", output_to_operand_aliasing={{}: (7, {})} | custom-call | flops 1000000000 | bytes 3333333 | tf_op jit(solution)/shard_map/finish/pallas_call | solution.py:111
  96.9 3.7 %collective-permute-start.37 = (bf16[128,1024]{1,0:T(8,128)(2,1)S(1)}, bf16[128,1024]{1,0:T(8,128)(2,1)S(1)}, u32[]{:S(2)}, u32[]{:S(2)}) collective-permute-start(bf16[128,1024]{1,0:T(8,128)(2,1)S(1)} %add_term.24.refs_5_), channel_id=1, source_target_pairs={{0,2},{2,0},{4,6},{6,4},{1,3},{3,1},{5,7},{7,5},{8,10},{10,8},{12,... | collective-permute-start | bytes 786440 | tf_op jit(solution)/shard_map/ppermute | solution.py:638
  100.6 1.1 %finish.7.refs_7_ = bf16[256,5120]{1,0:T(8,128)(2,1)} custom-call(s32[1]{0:T(128)} %bitcast.3.refs_1_.refs_0_, bf16[256,256]{1,0:T(8,128)(2,1)S(1)} %get-tuple-element.70.refs_1_, bf16[256,5120]{1,0:T(8,128)(2,1)S(1)} %copy-done, bf16[128,1024]{1,0:T(8,128)(2,1)S(1)} %get-tuple-element.79.refs_3_, ...), custom_call_target="tpu_custom_call", output_to_operand_aliasing={{}: (7, {})} | custom-call | flops 1000000000 | bytes 3333333 | tf_op jit(solution)/shard_map/finish/pallas_call | solution.py:111
  101.8 0.6 copy-done.2
  102.4 2.1 %place_rows.1.refs_8_ = bf16[512,2048]{1,0:T(8,128)(2,1)} custom-call(s32[1,512]{1,0:T(1,128)S(1)} %bitcast.6, bf16[512,512]{1,0:T(8,128)(2,1)S(1)} %get-tuple-element.42.refs_1_, bf16[512,2048]{1,0:T(8,128)(2,1)S(1)} %copy-done.2, bf16[256,2048]{1,0:T(8,128)(2,1)S(1)} %get-tuple-element.51.refs_0_.refs_3_, ...), custom_call_target="tpu_custom_call" | custom-call | flops 6400000000 | bytes 21333332 | tf_op jit(solution)/shard_map/place_rows/pallas_call | solution.py:111
  104.5 1.1 %finish.8.refs_7_ = bf16[256,5120]{1,0:T(8,128)(2,1)} custom-call(s32[1]{0:T(128)} %bitcast.3.refs_1_.refs_0_, bf16[256,256]{1,0:T(8,128)(2,1)S(1)} %get-tuple-element.70.refs_1_, bf16[256,5120]{1,0:T(8,128)(2,1)S(1)} %copy-done, bf16[128,1024]{1,0:T(8,128)(2,1)S(1)} %get-tuple-element.78.refs_3_, ...), custom_call_target="tpu_custom_call", output_to_operand_aliasing={{}: (7, {})} | custom-call | flops 1000000000 | bytes 3333333 | tf_op jit(solution)/shard_map/finish/pallas_call | solution.py:111
  105.7 1.0 collective-permute-done.37.refs_6_
  106.7 1.1 %finish.9 = bf16[256,5120]{1,0:T(8,128)(2,1)} custom-call(s32[1]{0:T(128)} %bitcast.3.refs_1_.refs_0_, bf16[256,256]{1,0:T(8,128)(2,1)S(1)} %get-tuple-element.70.refs_1_, bf16[256,5120]{1,0:T(8,128)(2,1)S(1)} %copy-done, bf16[128,1024]{1,0:T(8,128)(2,1)S(1)} %get-tuple-element.72.refs_3_, ...), custom_call_target="tpu_custom_call", output_to_operand_aliasing={{}: (7, {})} | custom-call | flops 1000000000 | bytes 3333333 | tf_op jit(solution)/shard_map/finish/pallas_call | solution.py:111
  (77 shorter events, 2.4 us)
Async XLA Ops:
  3.0 15.5 %collective-permute-start.1 = (bf16[64,2048]{1,0:T(8,128)(2,1)S(1)}, bf16[64,2048]{1,0:T(8,128)(2,1)S(1)}, u32[]{:S(2)}, u32[]{:S(2)}) collective-permute-start(bf16[64,2048]{1,0:T(8,128)(2,1)S(1)} %get-tuple-element.47), channel_id=1, source_target_pairs={{0,16},{1,17},{8,24},{9,25},{16,0},{17,1},{24,8},{25,9},{2,18},{3,... | collective-permute-start | bytes 786440 | tf_op jit(solution)/shard_map/ppermute | solution.py:570
  6.0 13.2 %collective-permute-start.2 = (bf16[64,2048]{1,0:T(8,128)(2,1)S(1)}, bf16[64,2048]{1,0:T(8,128)(2,1)S(1)}, u32[]{:S(2)}, u32[]{:S(2)}) collective-permute-start(bf16[64,2048]{1,0:T(8,128)(2,1)S(1)} %get-tuple-element.48), channel_id=1, source_target_pairs={{0,17},{1,16},{8,25},{9,24},{16,1},{17,0},{24,9},{25,8},{2,19},{3,... | collective-permute-start | bytes 786440 | tf_op jit(solution)/shard_map/ppermute | solution.py:570
  7.5 13.1 %collective-permute-start = (bf16[64,2048]{1,0:T(8,128)(2,1)S(1)}, bf16[64,2048]{1,0:T(8,128)(2,1)S(1)}, u32[]{:S(2)}, u32[]{:S(2)}) collective-permute-start(bf16[64,2048]{1,0:T(8,128)(2,1)S(1)} %get-tuple-element.41.refs_5_), channel_id=1, source_target_pairs={{0,1},{1,0},{8,9},{9,8},{16,17},{17,16},{24,25},{25,24},{2,3},{3,2... | collective-permute-start | bytes 786440 | tf_op jit(solution)/shard_map/ppermute | solution.py:570
  20.6 2.0 %collective-permute-start.3 = (bf16[128,2048]{1,0:T(8,128)(2,1)S(1)}, bf16[128,2048]{1,0:T(8,128)(2,1)S(1)}, u32[]{:S(2)}, u32[]{:S(2)}) collective-permute-start(bf16[128,2048]{1,0:T(8,128)(2,1)S(1)} %relay.1), channel_id=1, source_target_pairs={{0,8},{1,9},{8,0},{9,1},{16,24},{17,25},{24,16},{25,17},{2,10},{3,... | collective-permute-start | bytes 1572872 | tf_op jit(solution)/shard_map/ppermute | solution.py:570
  24.4 9.2 %collective-permute-start.4 = (bf16[128,1024]{1,0:T(8,128)(2,1)S(1)}, bf16[128,1024]{1,0:T(8,128)(2,1)S(1)}, u32[]{:S(2)}, u32[]{:S(2)}) collective-permute-start(bf16[128,1024]{1,0:T(8,128)(2,1)S(1)} %back_product.10.refs_2_.refs_0_), channel_id=1, source_target_pairs={{0,2},{2,0},{4,6},{6,4},{1,3},{3,1},{5,7},{7,5},{8,10},{10,8},{12,... | collective-permute-start | bytes 786440 | tf_op jit(solution)/shard_map/ppermute | solution.py:638
  28.5 2.5 %collective-permute-start.18 = (bf16[32,2048]{1,0:T(8,128)(2,1)S(1)}, bf16[32,2048]{1,0:T(8,128)(2,1)S(1)}, u32[]{:S(2)}, u32[]{:S(2)}) collective-permute-start(bf16[32,2048]{1,0:T(8,128)(2,1)S(1)} %get-tuple-element.62), channel_id=1, source_target_pairs={{0,8},{1,9},{8,0},{9,1},{16,24},{17,25},{24,16},{25,17},{2,10},{3,... | collective-permute-start | bytes 393224 | tf_op jit(solution)/shard_map/ppermute | solution.py:570
  28.6 4.1 %collective-permute-start.16 = (bf16[32,2048]{1,0:T(8,128)(2,1)S(1)}, bf16[32,2048]{1,0:T(8,128)(2,1)S(1)}, u32[]{:S(2)}, u32[]{:S(2)}) collective-permute-start(bf16[32,2048]{1,0:T(8,128)(2,1)S(1)} %get-tuple-element.61), channel_id=1, source_target_pairs={{0,8},{1,9},{8,0},{9,1},{16,24},{17,25},{24,16},{25,17},{2,10},{3,... | collective-permute-start | bytes 393224 | tf_op jit(solution)/shard_map/ppermute | solution.py:570
  29.1 9.4 %collective-permute-start.6 = (bf16[128,1024]{1,0:T(8,128)(2,1)S(1)}, bf16[128,1024]{1,0:T(8,128)(2,1)S(1)}, u32[]{:S(2)}, u32[]{:S(2)}) collective-permute-start(bf16[128,1024]{1,0:T(8,128)(2,1)S(1)} %back_product.11.refs_2_.refs_0_), channel_id=1, source_target_pairs={{0,2},{2,0},{4,6},{6,4},{1,3},{3,1},{5,7},{7,5},{8,10},{10,8},{12,... | collective-permute-start | bytes 786440 | tf_op jit(solution)/shard_map/ppermute | solution.py:638
  31.1 9.1 %collective-permute-start.19 = (bf16[64,2048]{1,0:T(8,128)(2,1)S(1)}, bf16[64,2048]{1,0:T(8,128)(2,1)S(1)}, u32[]{:S(2)}, u32[]{:S(2)}) collective-permute-start(bf16[64,2048]{1,0:T(8,128)(2,1)S(1)} %join.10), channel_id=1, source_target_pairs={{0,16},{1,17},{8,24},{9,25},{16,0},{17,1},{24,8},{25,9},{2,18},{3,... | collective-permute-start | bytes 786440 | tf_op jit(solution)/shard_map/ppermute | solution.py:570
  32.7 8.0 %collective-permute-start.17 = (bf16[64,2048]{1,0:T(8,128)(2,1)S(1)}, bf16[64,2048]{1,0:T(8,128)(2,1)S(1)}, u32[]{:S(2)}, u32[]{:S(2)}) collective-permute-start(bf16[64,2048]{1,0:T(8,128)(2,1)S(1)} %join.9), channel_id=1, source_target_pairs={{0,1},{1,0},{8,9},{9,8},{16,17},{17,16},{24,25},{25,24},{2,3},{3,2... | collective-permute-start | bytes 786440 | tf_op jit(solution)/shard_map/ppermute | solution.py:570
  33.7 8.5 %collective-permute-start.5 = (bf16[128,1024]{1,0:T(8,128)(2,1)S(1)}, bf16[128,1024]{1,0:T(8,128)(2,1)S(1)}, u32[]{:S(2)}, u32[]{:S(2)}) collective-permute-start(bf16[128,1024]{1,0:T(8,128)(2,1)S(1)} %add_term.13.refs_1_), channel_id=1, source_target_pairs={{0,8},{2,4},{4,2},{6,14},{8,0},{10,12},{12,10},{14,6},{16,24},{18,... | collective-permute-start | bytes 786440 | tf_op jit(solution)/shard_map/ppermute | solution.py:664
  33.8 6.3 %collective-permute-start.20 = (bf16[32,2048]{1,0:T(8,128)(2,1)S(1)}, bf16[32,2048]{1,0:T(8,128)(2,1)S(1)}, u32[]{:S(2)}, u32[]{:S(2)}) collective-permute-start(bf16[32,2048]{1,0:T(8,128)(2,1)S(1)} %get-tuple-element.63), channel_id=1, source_target_pairs={{0,8},{1,9},{8,0},{9,1},{16,24},{17,25},{24,16},{25,17},{2,10},{3,... | collective-permute-start | bytes 393224 | tf_op jit(solution)/shard_map/ppermute | solution.py:570
  38.5 8.1 %collective-permute-start.23 = (bf16[128,1024]{1,0:T(8,128)(2,1)S(1)}, bf16[128,1024]{1,0:T(8,128)(2,1)S(1)}, u32[]{:S(2)}, u32[]{:S(2)}) collective-permute-start(bf16[128,1024]{1,0:T(8,128)(2,1)S(1)} %back_product.12.refs_2_.refs_0_), channel_id=1, source_target_pairs={{0,2},{2,0},{4,6},{6,4},{1,3},{3,1},{5,7},{7,5},{8,10},{10,8},{12,... | collective-permute-start | bytes 786440 | tf_op jit(solution)/shard_map/ppermute | solution.py:638
  40.1 6.6 %collective-permute-start.22 = (bf16[128,1024]{1,0:T(8,128)(2,1)S(1)}, bf16[128,1024]{1,0:T(8,128)(2,1)S(1)}, u32[]{:S(2)}, u32[]{:S(2)}) collective-permute-start(bf16[128,1024]{1,0:T(8,128)(2,1)S(1)} %add_term.14.refs_4_.refs_1_), channel_id=1, source_target_pairs={{0,8},{2,4},{4,2},{6,14},{8,0},{10,12},{12,10},{14,6},{16,24},{18,... | collective-permute-start | bytes 786440 | tf_op jit(solution)/shard_map/ppermute | solution.py:664
  40.2 10.4 %collective-permute-start.15 = (bf16[32,2048]{1,0:T(8,128)(2,1)S(1)}, bf16[32,2048]{1,0:T(8,128)(2,1)S(1)}, u32[]{:S(2)}, u32[]{:S(2)}) collective-permute-start(bf16[32,2048]{1,0:T(8,128)(2,1)S(1)} %get-tuple-element.60), channel_id=1, source_target_pairs={{0,8},{1,9},{8,0},{9,1},{16,24},{17,25},{24,16},{25,17},{2,10},{3,... | collective-permute-start | bytes 393224 | tf_op jit(solution)/shard_map/ppermute | solution.py:570
  40.7 9.8 %collective-permute-start.21 = (bf16[64,2048]{1,0:T(8,128)(2,1)S(1)}, bf16[64,2048]{1,0:T(8,128)(2,1)S(1)}, u32[]{:S(2)}, u32[]{:S(2)}) collective-permute-start(bf16[64,2048]{1,0:T(8,128)(2,1)S(1)} %join.11), channel_id=1, source_target_pairs={{0,17},{1,16},{8,25},{9,24},{16,1},{17,0},{24,9},{25,8},{2,19},{3,... | collective-permute-start | bytes 786440 | tf_op jit(solution)/shard_map/ppermute | solution.py:570
  42.3 9.8 %collective-permute-start.7 = (bf16[128,1024]{1,0:T(8,128)(2,1)S(1)}, bf16[128,1024]{1,0:T(8,128)(2,1)S(1)}, u32[]{:S(2)}, u32[]{:S(2)}) collective-permute-start(bf16[128,1024]{1,0:T(8,128)(2,1)S(1)} %get-tuple-element.50.refs_2_), channel_id=1, source_target_pairs={{0,2},{2,0},{4,6},{6,4},{1,3},{3,1},{5,7},{7,5},{8,10},{10,8},{12,... | collective-permute-start | bytes 786440 | tf_op jit(solution)/shard_map/ppermute | solution.py:638
  46.6 7.2 %collective-permute-start.25 = (bf16[128,1024]{1,0:T(8,128)(2,1)S(1)}, bf16[128,1024]{1,0:T(8,128)(2,1)S(1)}, u32[]{:S(2)}, u32[]{:S(2)}) collective-permute-start(bf16[128,1024]{1,0:T(8,128)(2,1)S(1)} %add_term.16.refs_4_.refs_1_), channel_id=1, source_target_pairs={{0,8},{2,4},{4,2},{6,14},{8,0},{10,12},{12,10},{14,6},{16,24},{18,... | collective-permute-start | bytes 786440 | tf_op jit(solution)/shard_map/ppermute | solution.py:664
  46.9 11.9 %collective-permute-start.24 = (bf16[128,1024]{1,0:T(8,128)(2,1)S(1)}, bf16[128,1024]{1,0:T(8,128)(2,1)S(1)}, u32[]{:S(2)}, u32[]{:S(2)}) collective-permute-start(bf16[128,1024]{1,0:T(8,128)(2,1)S(1)} %get-tuple-element.65.refs_11_.refs_2_), channel_id=1, source_target_pairs={{0,2},{2,0},{4,6},{6,4},{1,3},{3,1},{5,7},{7,5},{8,10},{10,8},{12,... | collective-permute-start | bytes 786440 | tf_op jit(solution)/shard_map/ppermute | solution.py:638
  52.2 6.7 %collective-permute-start.27 = (bf16[128,1024]{1,0:T(8,128)(2,1)S(1)}, bf16[128,1024]{1,0:T(8,128)(2,1)S(1)}, u32[]{:S(2)}, u32[]{:S(2)}) collective-permute-start(bf16[128,1024]{1,0:T(8,128)(2,1)S(1)} %add_term.15.refs_2_.refs_4_.refs_1_), channel_id=1, source_target_pairs={{0,8},{2,4},{4,2},{6,14},{8,0},{10,12},{12,10},{14,6},{16,24},{18,... | collective-permute-start | bytes 786440 | tf_op jit(solution)/shard_map/ppermute | solution.py:664
  53.9 11.5 %collective-permute-start.28 = (bf16[128,1024]{1,0:T(8,128)(2,1)S(1)}, bf16[128,1024]{1,0:T(8,128)(2,1)S(1)}, u32[]{:S(2)}, u32[]{:S(2)}) collective-permute-start(bf16[128,1024]{1,0:T(8,128)(2,1)S(1)} %get-tuple-element.66.refs_2_), channel_id=1, source_target_pairs={{0,2},{2,0},{4,6},{6,4},{1,3},{3,1},{5,7},{7,5},{8,10},{10,8},{12,... | collective-permute-start | bytes 786440 | tf_op jit(solution)/shard_map/ppermute | solution.py:638
  58.7 3.8 %copy-start.3 = (bf16[2048]{0:T(1024)(128)(2,1)S(1)}, bf16[2048]{0:T(1024)(128)(2,1)}, u32[]{:S(2)}) copy-start(bf16[2048]{0:T(1024)(128)(2,1)} %param.9) | copy-start | bytes 12292
  58.8 6.9 %collective-permute-start.26 = (bf16[128,1024]{1,0:T(8,128)(2,1)S(1)}, bf16[128,1024]{1,0:T(8,128)(2,1)S(1)}, u32[]{:S(2)}, u32[]{:S(2)}) collective-permute-start(bf16[128,1024]{1,0:T(8,128)(2,1)S(1)} %add_term.17.refs_4_.refs_1_), channel_id=1, source_target_pairs={{0,8},{2,4},{4,2},{6,14},{8,0},{10,12},{12,10},{14,6},{16,24},{18,... | collective-permute-start | bytes 786440 | tf_op jit(solution)/shard_map/ppermute | solution.py:664
  59.0 10.2 %collective-permute-start.30 = (bf16[128,1024]{1,0:T(8,128)(2,1)S(1)}, bf16[128,1024]{1,0:T(8,128)(2,1)S(1)}, u32[]{:S(2)}, u32[]{:S(2)}) collective-permute-start(bf16[128,1024]{1,0:T(8,128)(2,1)S(1)} %get-tuple-element.67.refs_2_), channel_id=1, source_target_pairs={{0,2},{2,0},{4,6},{6,4},{1,3},{3,1},{5,7},{7,5},{8,10},{10,8},{12,... | collective-permute-start | bytes 786440 | tf_op jit(solution)/shard_map/ppermute | solution.py:638
  63.4 7.8 %collective-permute-start.9 = (bf16[64,2048]{1,0:T(8,128)(2,1)S(1)}, bf16[64,2048]{1,0:T(8,128)(2,1)S(1)}, u32[]{:S(2)}, u32[]{:S(2)}) collective-permute-start(bf16[64,2048]{1,0:T(8,128)(2,1)S(1)} %get-tuple-element.53), channel_id=1, source_target_pairs={{0,8},{1,9},{8,0},{9,1},{16,24},{17,25},{24,16},{25,17},{2,10},{3,... | collective-permute-start | bytes 786440 | tf_op jit(solution)/shard_map/ppermute | solution.py:570
  63.4 5.9 %collective-permute-start.11 = (bf16[64,2048]{1,0:T(8,128)(2,1)S(1)}, bf16[64,2048]{1,0:T(8,128)(2,1)S(1)}, u32[]{:S(2)}, u32[]{:S(2)}) collective-permute-start(bf16[64,2048]{1,0:T(8,128)(2,1)S(1)} %get-tuple-element.54), channel_id=1, source_target_pairs={{0,8},{1,9},{8,0},{9,1},{16,24},{17,25},{24,16},{25,17},{2,10},{3,... | collective-permute-start | bytes 786440 | tf_op jit(solution)/shard_map/ppermute | solution.py:570
  65.5 6.1 %collective-permute-start.29 = (bf16[128,1024]{1,0:T(8,128)(2,1)S(1)}, bf16[128,1024]{1,0:T(8,128)(2,1)S(1)}, u32[]{:S(2)}, u32[]{:S(2)}) collective-permute-start(bf16[128,1024]{1,0:T(8,128)(2,1)S(1)} %add_term.18.refs_4_.refs_1_), channel_id=1, source_target_pairs={{0,8},{2,4},{4,2},{6,14},{8,0},{10,12},{12,10},{14,6},{16,24},{18,... | collective-permute-start | bytes 786440 | tf_op jit(solution)/shard_map/ppermute | solution.py:664
  65.8 11.4 %collective-permute-start.32 = (bf16[128,1024]{1,0:T(8,128)(2,1)S(1)}, bf16[128,1024]{1,0:T(8,128)(2,1)S(1)}, u32[]{:S(2)}, u32[]{:S(2)}) collective-permute-start(bf16[128,1024]{1,0:T(8,128)(2,1)S(1)} %get-tuple-element.68.refs_2_), channel_id=1, source_target_pairs={{0,2},{2,0},{4,6},{6,4},{1,3},{3,1},{5,7},{7,5},{8,10},{10,8},{12,... | collective-permute-start | bytes 786440 | tf_op jit(solution)/shard_map/ppermute | solution.py:638
  69.3 8.1 %collective-permute-start.33 = (bf16[128,1024]{1,0:T(8,128)(2,1)S(1)}, bf16[128,1024]{1,0:T(8,128)(2,1)S(1)}, u32[]{:S(2)}, u32[]{:S(2)}) collective-permute-start(bf16[128,1024]{1,0:T(8,128)(2,1)S(1)} %add_term.19.refs_4_.refs_1_), channel_id=1, source_target_pairs={{0,8},{2,4},{4,2},{6,14},{8,0},{10,12},{12,10},{14,6},{16,24},{18,... | collective-permute-start | bytes 786440 | tf_op jit(solution)/shard_map/ppermute | solution.py:664
  69.4 14.4 %collective-permute-start.12 = (bf16[128,2048]{1,0:T(8,128)(2,1)S(1)}, bf16[128,2048]{1,0:T(8,128)(2,1)S(1)}, u32[]{:S(2)}, u32[]{:S(2)}) collective-permute-start(bf16[128,2048]{1,0:T(8,128)(2,1)S(1)} %join.7), channel_id=1, source_target_pairs={{0,16},{1,17},{8,24},{9,25},{16,0},{17,1},{24,8},{25,9},{2,18},{3,... | collective-permute-start | bytes 1572872 | tf_op jit(solution)/shard_map/ppermute | solution.py:570
  71.2 14.1 %collective-permute-start.10 = (bf16[128,2048]{1,0:T(8,128)(2,1)S(1)}, bf16[128,2048]{1,0:T(8,128)(2,1)S(1)}, u32[]{:S(2)}, u32[]{:S(2)}) collective-permute-start(bf16[128,2048]{1,0:T(8,128)(2,1)S(1)} %join.6), channel_id=1, source_target_pairs={{0,1},{1,0},{8,9},{9,8},{16,17},{17,16},{24,25},{25,24},{2,3},{3,2... | collective-permute-start | bytes 1572872 | tf_op jit(solution)/shard_map/ppermute | solution.py:570
  71.7 8.7 %collective-permute-start.31 = (bf16[128,1024]{1,0:T(8,128)(2,1)S(1)}, bf16[128,1024]{1,0:T(8,128)(2,1)S(1)}, u32[]{:S(2)}, u32[]{:S(2)}) collective-permute-start(bf16[128,1024]{1,0:T(8,128)(2,1)S(1)} %get-tuple-element.69.refs_2_), channel_id=1, source_target_pairs={{0,2},{2,0},{4,6},{6,4},{1,3},{3,1},{5,7},{7,5},{8,10},{10,8},{12,... | collective-permute-start | bytes 786440 | tf_op jit(solution)/shard_map/ppermute | solution.py:638
  77.2 4.4 %collective-permute-start.13 = (bf16[64,2048]{1,0:T(8,128)(2,1)S(1)}, bf16[64,2048]{1,0:T(8,128)(2,1)S(1)}, u32[]{:S(2)}, u32[]{:S(2)}) collective-permute-start(bf16[64,2048]{1,0:T(8,128)(2,1)S(1)} %get-tuple-element.55), channel_id=1, source_target_pairs={{0,8},{1,9},{8,0},{9,1},{16,24},{17,25},{24,16},{25,17},{2,10},{3,... | collective-permute-start | bytes 786440 | tf_op jit(solution)/shard_map/ppermute | solution.py:570
  77.3 3.1 %copy-start = (bf16[256,5120]{1,0:T(8,128)(2,1)S(1)}, bf16[256,5120]{1,0:T(8,128)(2,1)}, u32[]{:S(2)}) copy-start(bf16[256,5120]{1,0:T(8,128)(2,1)} %get-tuple-element.71.refs_2_) | copy-start | bytes 7864324
  77.5 9.0 %collective-permute-start.34 = (bf16[128,1024]{1,0:T(8,128)(2,1)S(1)}, bf16[128,1024]{1,0:T(8,128)(2,1)S(1)}, u32[]{:S(2)}, u32[]{:S(2)}) collective-permute-start(bf16[128,1024]{1,0:T(8,128)(2,1)S(1)} %get-tuple-element.73), channel_id=1, source_target_pairs={{0,2},{2,0},{4,6},{6,4},{1,3},{3,1},{5,7},{7,5},{8,10},{10,8},{12,... | collective-permute-start | bytes 786440 | tf_op jit(solution)/shard_map/ppermute | solution.py:638
  80.4 6.2 %collective-permute-start.39 = (bf16[128,1024]{1,0:T(8,128)(2,1)S(1)}, bf16[128,1024]{1,0:T(8,128)(2,1)S(1)}, u32[]{:S(2)}, u32[]{:S(2)}) collective-permute-start(bf16[128,1024]{1,0:T(8,128)(2,1)S(1)} %add_term.21.refs_4_.refs_0_), channel_id=1, source_target_pairs={{0,8},{2,4},{4,2},{6,14},{8,0},{10,12},{12,10},{14,6},{16,24},{18,... | collective-permute-start | bytes 786440 | tf_op jit(solution)/shard_map/ppermute | solution.py:664
  81.6 20.1 %collective-permute-start.8 = (bf16[64,2048]{1,0:T(8,128)(2,1)S(1)}, bf16[64,2048]{1,0:T(8,128)(2,1)S(1)}, u32[]{:S(2)}, u32[]{:S(2)}) collective-permute-start(bf16[64,2048]{1,0:T(8,128)(2,1)S(1)} %get-tuple-element.52), channel_id=1, source_target_pairs={{0,8},{1,9},{8,0},{9,1},{16,24},{17,25},{24,16},{25,17},{2,10},{3,... | collective-permute-start | bytes 786440 | tf_op jit(solution)/shard_map/ppermute | solution.py:570
  83.8 6.2 %collective-permute-start.36 = (bf16[128,1024]{1,0:T(8,128)(2,1)S(1)}, bf16[128,1024]{1,0:T(8,128)(2,1)S(1)}, u32[]{:S(2)}, u32[]{:S(2)}) collective-permute-start(bf16[128,1024]{1,0:T(8,128)(2,1)S(1)} %add_term.20.refs_8_.refs_7_.refs_0_.refs_2_), channel_id=1, source_target_pairs={{0,8},{2,4},{4,2},{6,14},{8,0},{10,12},{12,10},{14,6},{16,24},{18,... | collective-permute-start | bytes 786440 | tf_op jit(solution)/shard_map/ppermute | solution.py:664
  85.3 16.4 %collective-permute-start.14 = (bf16[128,2048]{1,0:T(8,128)(2,1)S(1)}, bf16[128,2048]{1,0:T(8,128)(2,1)S(1)}, u32[]{:S(2)}, u32[]{:S(2)}) collective-permute-start(bf16[128,2048]{1,0:T(8,128)(2,1)S(1)} %join.8), channel_id=1, source_target_pairs={{0,17},{1,16},{8,25},{9,24},{16,1},{17,0},{24,9},{25,8},{2,19},{3,... | collective-permute-start | bytes 1572872 | tf_op jit(solution)/shard_map/ppermute | solution.py:570
  86.5 10.3 %collective-permute-start.35 = (bf16[128,1024]{1,0:T(8,128)(2,1)S(1)}, bf16[128,1024]{1,0:T(8,128)(2,1)S(1)}, u32[]{:S(2)}, u32[]{:S(2)}) collective-permute-start(bf16[128,1024]{1,0:T(8,128)(2,1)S(1)} %add_term.22.refs_2_.refs_0_), channel_id=1, source_target_pairs={{0,8},{2,4},{4,2},{6,14},{8,0},{10,12},{12,10},{14,6},{16,24},{18,... | collective-permute-start | bytes 786440 | tf_op jit(solution)/shard_map/ppermute | solution.py:664
  86.7 13.9 %collective-permute-start.40 = (bf16[128,1024]{1,0:T(8,128)(2,1)S(1)}, bf16[128,1024]{1,0:T(8,128)(2,1)S(1)}, u32[]{:S(2)}, u32[]{:S(2)}) collective-permute-start(bf16[128,1024]{1,0:T(8,128)(2,1)S(1)} %add_term.25.refs_5_), channel_id=1, source_target_pairs={{0,2},{2,0},{4,6},{6,4},{1,3},{3,1},{5,7},{7,5},{8,10},{10,8},{12,... | collective-permute-start | bytes 786440 | tf_op jit(solution)/shard_map/ppermute | solution.py:638
  90.1 14.4 %collective-permute-start.38 = (bf16[128,1024]{1,0:T(8,128)(2,1)S(1)}, bf16[128,1024]{1,0:T(8,128)(2,1)S(1)}, u32[]{:S(2)}, u32[]{:S(2)}) collective-permute-start(bf16[128,1024]{1,0:T(8,128)(2,1)S(1)} %add_term.23.refs_8_.refs_5_), channel_id=1, source_target_pairs={{0,2},{2,0},{4,6},{6,4},{1,3},{3,1},{5,7},{7,5},{8,10},{10,8},{12,... | collective-permute-start | bytes 786440 | tf_op jit(solution)/shard_map/ppermute | solution.py:638
  96.9 9.8 %collective-permute-start.37 = (bf16[128,1024]{1,0:T(8,128)(2,1)S(1)}, bf16[128,1024]{1,0:T(8,128)(2,1)S(1)}, u32[]{:S(2)}, u32[]{:S(2)}) collective-permute-start(bf16[128,1024]{1,0:T(8,128)(2,1)S(1)} %add_term.24.refs_5_), channel_id=1, source_target_pairs={{0,2},{2,0},{4,6},{6,4},{1,3},{3,1},{5,7},{7,5},{8,10},{10,8},{12,... | collective-permute-start | bytes 786440 | tf_op jit(solution)/shard_map/ppermute | solution.py:638
  100.6 1.2 %copy-start.1 = (s32[512]{0:T(512)S(1)}, s32[512]{0:T(512)}, u32[]{:S(2)}) copy-start(s32[512]{0:T(512)} %param.11) | copy-start | bytes 6148
  100.6 1.8 %copy-start.2 = (bf16[512,2048]{1,0:T(8,128)(2,1)S(1)}, bf16[512,2048]{1,0:T(8,128)(2,1)}, u32[]{:S(2)}) copy-start(bf16[512,2048]{1,0:T(8,128)(2,1)} %refs_2_.1) | copy-start | bytes 6291460
